TPU v7x, 256 devices: a whole 4x4x8 slice. The times are simulated.
256 devices in a mesh: seq: 64 (over z_hi, y, x), head: 4 (over z_lo, core).
Axes of the slice: x: 4, y: 4, z: 8 (z_hi: 4, z_lo: 2; z = z_hi * 2 + z_lo), core: 2. Of those that a mesh axis runs over, the one named last changes fastest.
Arguments:
- queries: bfloat16 [3, 16384, 2048], P(None, 'seq', 'head'), may hold values from -24 to 24
- key_vectors: bfloat16 [4, 16384, 2048], P(None, 'seq', 'head'), may hold values from -24 to 24
- values: bfloat16 [4, 16384, 2048], P(None, 'seq', 'head'), may hold values from -6 to 6
- learn_rates: float32 [3, 16384, 4], P(None, 'seq', 'head'), may hold values from 0.001 to 0.01
- norm_gain: float32 [2048], P('head'), may hold values from 0.1 to 1.9
- out_weight: bfloat16 [2048, 2048], P('head'), may hold values from -0.125 to 0.125
- incoming: float32 [64, 4, 3, 512, 512], P('seq', 'head'), may hold values from -0.25 to 0.25
Outputs:
- mixed_out: bfloat16 [3, 16384, 2048], P(None, 'seq', 'head')
- outgoing: float32 [64, 4, 3, 512, 512], P('seq', 'head')
All inputs are finite; a program needn't handle non-finite values.
Results may differ from a plain program's by a relative error of at most 0.013.
The roundings to bfloat16 on the way count: a program that leaves them out, or rounds other values in their place, can miss the bound.
Values may be sent and summed in bfloat16 or wider, within the bound.
No kernel may reach another device: no remote copies, remote signals or barrier semaphores. Data moves between devices by JAX's collectives and lax.ppermute only.
A program may use at most 64 MiB of HBM per device.

v0:
```python
import jax
import jax.numpy as jnp
from jax import lax
from jax.sharding import PartitionSpec as P


def shifted(x, axis, by):
    count = lax.axis_size(axis)
    return lax.ppermute(x, axis, [(i, (i + by) % count) for i in range(count)])


def fast_apply(rounded, query_rows):
    first_proj = jnp.dot(query_rows, rounded[0], preferred_element_type=jnp.float32)
    third_proj = jnp.dot(query_rows, rounded[1], preferred_element_type=jnp.float32)
    hidden = (first_proj * jax.nn.sigmoid(first_proj) * third_proj).astype(jnp.bfloat16)
    return jnp.dot(hidden, rounded[2], preferred_element_type=jnp.float32)


def fast_update(fast_state, rounded, key_rows, scaled_values):
    first_proj = jnp.dot(key_rows, rounded[0], preferred_element_type=jnp.float32)
    third_proj = jnp.dot(key_rows, rounded[1], preferred_element_type=jnp.float32)
    gate_sig = jax.nn.sigmoid(first_proj)
    hidden = (first_proj * gate_sig * third_proj).astype(jnp.bfloat16)
    grad_down = jnp.dot(hidden.T, scaled_values, preferred_element_type=jnp.float32)
    back_grad = jnp.dot(scaled_values, rounded[2].T, preferred_element_type=jnp.float32)
    grad_first = (back_grad * third_proj * gate_sig * (1.0 + first_proj * (1.0 - gate_sig))).astype(
        jnp.bfloat16
    )
    grad_third = (back_grad * first_proj * gate_sig).astype(jnp.bfloat16)
    grad_one = jnp.dot(key_rows.T, grad_first, preferred_element_type=jnp.float32)
    grad_three = jnp.dot(key_rows.T, grad_third, preferred_element_type=jnp.float32)
    stepped = fast_state + jnp.stack([grad_one, grad_three, grad_down])
    before_sq = jnp.mean(fast_state * fast_state, axis=1, keepdims=True)
    after_sq = jnp.mean(stepped * stepped, axis=1, keepdims=True)
    return stepped * jnp.sqrt((before_sq + 1e-06) / (after_sq + 1e-06))


def window_attend(query_rows, prior_keys, own_keys, prior_vals, own_vals):
    length = query_rows.shape[0]
    joined_keys = jnp.concatenate([prior_keys, own_keys], axis=0)
    joined_vals = jnp.concatenate([prior_vals, own_vals], axis=0)
    scores = jnp.dot(
        query_rows, joined_keys.T, preferred_element_type=jnp.float32
    ) * query_rows.shape[1] ** (-0.5)
    query_pos = jnp.arange(length)[:, None] + length
    key_pos = jnp.arange(2 * length)[None, :]
    allowed = (key_pos <= query_pos) & (key_pos > query_pos - length)
    scores = jnp.where(allowed, scores, -1e30)
    peak = jnp.max(scores, axis=1, keepdims=True)
    expo = jnp.exp(scores - peak)
    probs = (expo / jnp.sum(expo, axis=1, keepdims=True)).astype(jnp.bfloat16)
    return jnp.dot(probs, joined_vals, preferred_element_type=jnp.float32)


def mix_head(fast_out, attended, gain_row):
    normed = (
        fast_out
        * lax.rsqrt(jnp.mean(fast_out * fast_out, axis=1, keepdims=True) + 1e-06)
        * gain_row
    )
    return (attended + normed).astype(jnp.bfloat16)


def on_device(queries, key_vectors, values, learn_rates, norm_gain, out_weight, incoming):
    tick_count = queries.shape[0]
    fast_state = incoming[0, 0]
    outputs = []
    for tick_index in range(tick_count):
        query_rows = queries[tick_index]
        own_keys = key_vectors[tick_index + 1]
        own_vals = values[tick_index + 1]
        scaled_values = (learn_rates[tick_index] * own_vals.astype(jnp.float32)).astype(
            jnp.bfloat16
        )
        near_keys, near_vals = shifted((key_vectors[tick_index], values[tick_index]), "seq", 1)
        attended = window_attend(query_rows, near_keys, own_keys, near_vals, own_vals)
        rounded = fast_state.astype(jnp.bfloat16)
        fast_out = fast_apply(rounded, query_rows)
        updated = fast_update(fast_state, rounded, own_keys, scaled_values)
        if tick_index + 1 < tick_count:
            fast_state = shifted(updated, "seq", 1)
        else:
            fast_state = updated
        combined = mix_head(fast_out, attended, norm_gain)
        partial_value = jnp.dot(combined, out_weight, preferred_element_type=jnp.float32)
        outputs.append(
            lax.psum_scatter(
                partial_value.astype(jnp.bfloat16), "head", scatter_dimension=1, tiled=True
            )
        )
    return (jnp.stack(outputs), fast_state[None, None])


def solution(mesh):
    placed = (
        P(None, "seq", "head"),
        P(None, "seq", "head"),
        P(None, "seq", "head"),
        P(None, "seq", "head"),
        P("head"),
        P("head", None),
        P("seq", "head", None, None, None),
    )
    return jax.shard_map(
        on_device,
        mesh=mesh,
        in_specs=placed,
        out_specs=(P(None, "seq", "head"), P("seq", "head", None, None, None)),
        check_vma=False,
    )
```

profile of v0, /device:TPU:1, one launch (start us, length us, event | category | flops | bytes accessed | tf_op | source)
XLA Modules:
  0.0 452.1 jit_solution(7511799950043909370)
XLA Ops:
  7.3 2.2 bitcast_convert_fusion
  13.6 2.6 broadcast_multiply_fusion.1
  16.2 2.0 collective-permute-start.4
  22.3 2.0 fusion.55
  24.4 2.8 multiply_reduce_fusion.7
  27.1 111.5 %collective-permute-done = bf16[256,512]{1,0:T(8,128)(2,1)} collective-permute-done((bf16[256,512]{1,0:T(8,128)(2,1)}, bf16[256,512]{1,0:T(8,128)(2,1)}, u32[]{:S(2)}, u32[]{:S(2)}) %collective-permute-start) | collective-permute-done | bytes 262176 | tf_op jit(solution)/shard_map/ppermute | solution.py:9
  140.9 2.2 convert_element_type.128
  145.4 2.7 multiply_reduce_fusion.3
  148.2 4.5 broadcast_multiply_fusion
  152.7 3.4 convolution_convert_fusion.2
  156.3 202.3 %collective-permute-done.2 = bf16[256,512]{1,0:T(8,128)(2,1)S(1)} collective-permute-done((bf16[256,512]{1,0:T(8,128)(2,1)}, bf16[256,512]{1,0:T(8,128)(2,1)S(1)}, u32[]{:S(2)}, u32[]{:S(2)}) %collective-permute-start.2) | collective-permute-done | bytes 262176 | tf_op jit(solution)/shard_map/ppermute | solution.py:9
  360.9 2.2 convolution_bitcast_fusion.16
  363.1 2.8 multiply_reduce_fusion.6
  365.9 3.3 convolution_convert_fusion.1
  369.5 13.7 %collective-permute-done.5 = bf16[256,512]{1,0:T(8,128)(2,1)S(1)} collective-permute-done((bf16[256,512]{1,0:T(8,128)(2,1)}, bf16[256,512]{1,0:T(8,128)(2,1)S(1)}, u32[]{:S(2)}, u32[]{:S(2)}) %collective-permute-start.5) | collective-permute-done | bytes 262176 | tf_op jit(solution)/shard_map/ppermute | solution.py:9
  385.4 2.1 convert_element_type.141
  388.6 2.0 convolution_bitcast_fusion.12
  390.7 2.8 multiply_reduce_fusion.5
  393.4 2.3 fusion.61
  395.7 3.3 convolution_convert_fusion
  405.1 2.7 multiply_reduce_fusion.1
  407.9 4.5 %multiply_bitcast_fusion = f32[1,1,3,512,512]{4,3,2,1,0:T(8,128)} fusion(f32[3,512]{1,0:T(4,128)S(1)} %fusion.133, f32[3,512,512]{2,1,0:T(8,128)} %collective-permute-done.7, f32[1,512,512]{2,1,0:T(8,128)S(1)} %convolution_bitcast_fusion, f32[1,512,512]{2,1,0:T(8,128)S(1)} %convolution_bitcast_fusion.1, f32[1,512,512]{2,1,0:T(8,128)S(1)} %convolution_bitcast_fusion.2), kind=kLoop, calls=%fused_computation.6 | loop fusion | flops 3145728 | bytes 9443328 | tf_op jit(solution)/shard_map/broadcast_in_dim | solution.py:91
  412.4 31.0 %reduce-scatter.8.cloned.1.call-done = bf16[256,512]{1,0:T(8,128)(2,1)} async-done(((bf16[256,2048]{1,0:T(8,128)(2,1)}), bf16[256,512]{1,0:T(8,128)(2,1)}) %reduce-scatter.8.cloned.1.call-update) | async-done | bytes 262160 | tf_op jit(solution)/shard_map/reduce_scatter | solution.py:87
  443.5 2.1 pad_maximum_fusion
  (82 shorter events, 24.9 us)
Async XLA Ops:
  7.2 145.6 %copy-start = (bf16[512,2048]{1,0:T(8,128)(2,1)S(1)}, bf16[512,2048]{1,0:T(8,128)(2,1)}, u32[]{:S(2)}) copy-start(bf16[512,2048]{1,0:T(8,128)(2,1)} %param.12) | copy-start | bytes 6291460
  7.2 2.3 copy-start.2
  7.2 2.9 copy-start.11
  7.2 405.2 %reduce-scatter.4.cloned.1.call-start = ((), (), s32[]{:S(2)}) async-start(), calls=%async_computation.3 | async-start | bytes 1310720 | tf_op jit(solution)/shard_map/reduce_scatter | solution.py:87
  7.2 2.9 copy-start.6
  9.5 12.8 %copy-start.4 = (bf16[3,512,512]{2,1,0:T(8,128)(2,1)}, bf16[3,512,512]{2,1,0:T(8,128)(2,1)S(1)}, u32[]{:S(2)}) copy-start(bf16[3,512,512]{2,1,0:T(8,128)(2,1)S(1)} %bitcast_convert_fusion) | copy-start | bytes 4718596
  10.9 1.9 copy-start.1
  16.2 124.7 %collective-permute-start.4 = (f32[3,512,512]{2,1,0:T(8,128)}, f32[3,512,512]{2,1,0:T(8,128)}, u32[]{:S(2)}, u32[]{:S(2)}) collective-permute-start(f32[3,512,512]{2,1,0:T(8,128)} %broadcast_multiply_fusion.1), channel_id=1, source_target_pairs={{0,4},{4,8},{8,12},{12,16},{16,20},{20,24},{24,28},{28,32},{32,36}... | collective-permute-start | bytes 9437192 | tf_op jit(solution)/shard_map/ppermute | solution.py:9
  19.2 133.5 %collective-permute-start.1 = (bf16[256,512]{1,0:T(8,128)(2,1)}, bf16[256,512]{1,0:T(8,128)(2,1)}, u32[]{:S(2)}, u32[]{:S(2)}) collective-permute-start(bf16[256,512]{1,0:T(8,128)(2,1)} %get-tuple-element.12), channel_id=1, source_target_pairs={{0,4},{4,8},{8,12},{12,16},{16,20},{20,24},{24,28},{28,32},{32,36}... | collective-permute-start | bytes 786440 | tf_op jit(solution)/shard_map/ppermute | solution.py:9
  21.4 117.3 %collective-permute-start = (bf16[256,512]{1,0:T(8,128)(2,1)}, bf16[256,512]{1,0:T(8,128)(2,1)}, u32[]{:S(2)}, u32[]{:S(2)}) collective-permute-start(bf16[256,512]{1,0:T(8,128)(2,1)} %get-tuple-element.8), channel_id=1, source_target_pairs={{0,4},{4,8},{8,12},{12,16},{16,20},{20,24},{24,28},{28,32},{32,36}... | collective-permute-start | bytes 786440 | tf_op jit(solution)/shard_map/ppermute | solution.py:9
  140.9 2.8 copy-start.7
  143.1 1.4 copy-start.3
  148.2 4.5 %copy-start.12 = (f32[512]{0:T(512)S(1)}, f32[512]{0:T(512)}, u32[]{:S(2)}) copy-start(f32[512]{0:T(512)} %param.11) | copy-start | bytes 6148
  152.7 232.7 %collective-permute-start.7 = (f32[3,512,512]{2,1,0:T(8,128)}, f32[3,512,512]{2,1,0:T(8,128)}, u32[]{:S(2)}, u32[]{:S(2)}) collective-permute-start(f32[3,512,512]{2,1,0:T(8,128)} %broadcast_multiply_fusion), channel_id=1, source_target_pairs={{0,4},{4,8},{8,12},{12,16},{16,20},{20,24},{24,28},{28,32},{32,36}... | collective-permute-start | bytes 9437192 | tf_op jit(solution)/shard_map/ppermute | solution.py:9
  156.1 256.3 %reduce-scatter.6.cloned.1.call-start = ((), (), s32[]{:S(2)}) async-start(), calls=%async_computation.4 | async-start | bytes 1310720 | tf_op jit(solution)/shard_map/reduce_scatter | solution.py:87
  156.2 202.4 %collective-permute-start.2 = (bf16[256,512]{1,0:T(8,128)(2,1)}, bf16[256,512]{1,0:T(8,128)(2,1)S(1)}, u32[]{:S(2)}, u32[]{:S(2)}) collective-permute-start(bf16[256,512]{1,0:T(8,128)(2,1)} %get-tuple-element.9), channel_id=1, source_target_pairs={{0,4},{4,8},{8,12},{12,16},{16,20},{20,24},{24,28},{28,32},{32,36}... | collective-permute-start | bytes 786440 | tf_op jit(solution)/shard_map/ppermute | solution.py:9
  156.3 209.7 %collective-permute-start.3 = (bf16[256,512]{1,0:T(8,128)(2,1)}, bf16[256,512]{1,0:T(8,128)(2,1)}, u32[]{:S(2)}, u32[]{:S(2)}) collective-permute-start(bf16[256,512]{1,0:T(8,128)(2,1)} %get-tuple-element.13), channel_id=1, source_target_pairs={{0,4},{4,8},{8,12},{12,16},{16,20},{20,24},{24,28},{28,32},{32,36}... | collective-permute-start | bytes 786440 | tf_op jit(solution)/shard_map/ppermute | solution.py:9
  360.0 0.8 copy-start.10
  369.3 74.2 %reduce-scatter.8.cloned.1.call-start = ((), (), s32[]{:S(2)}) async-start(), calls=%async_computation.5 | async-start | bytes 1310720 | tf_op jit(solution)/shard_map/reduce_scatter | solution.py:87
  369.3 13.9 %collective-permute-start.5 = (bf16[256,512]{1,0:T(8,128)(2,1)}, bf16[256,512]{1,0:T(8,128)(2,1)S(1)}, u32[]{:S(2)}, u32[]{:S(2)}) collective-permute-start(bf16[256,512]{1,0:T(8,128)(2,1)} %get-tuple-element.11), channel_id=1, source_target_pairs={{0,4},{4,8},{8,12},{12,16},{16,20},{20,24},{24,28},{28,32},{32,36}... | collective-permute-start | bytes 786440 | tf_op jit(solution)/shard_map/ppermute | solution.py:9
  369.4 26.3 %collective-permute-start.6 = (bf16[256,512]{1,0:T(8,128)(2,1)}, bf16[256,512]{1,0:T(8,128)(2,1)}, u32[]{:S(2)}, u32[]{:S(2)}) collective-permute-start(bf16[256,512]{1,0:T(8,128)(2,1)} %get-tuple-element.15), channel_id=1, source_target_pairs={{0,4},{4,8},{8,12},{12,16},{16,20},{20,24},{24,28},{28,32},{32,36}... | collective-permute-start | bytes 786440 | tf_op jit(solution)/shard_map/ppermute | solution.py:9
  384.6 0.8 copy-start.9
  387.5 1.1 copy-start.5
  400.3 4.3 copy-start.13
  (1 other events, 0.8 us)
Sparse Core Ops, SparseCore 0:
  156.2 70.8 reduce-scatter.3
  369.4 41.2 reduce-scatter.5
  413.2 30.2 reduce-scatter.7
where the time goes:
time: 453 us; the launch traced here: 452 us
  waiting for transfers between devices  359 us (79%)
  matrix products  41.6 us (9%)
  other arithmetic  26.9 us (6%)
  between operations  14.1 us (3%)
  local copies, waits for them, and re-layouts  6.24 us (1%)
  starting transfers between devices  4.63 us (1%)
    ppermute x8, waiting for transfers between devices, shifted(): return lax.ppermute(x, axis, [(i, (i + by) % count) for i in range(count)])  328 us
    reduce_scatter x3, waiting for transfers between devices, on_device(): lax.psum_scatter(partial_value.astype(jnp.bfloat16), 'head', scatter_dime...  31 us
    dot_general x3, matrix products, on_device(): jnp.dot(combined, out_weight, preferred_element_type=jnp.float32)  9.95 us
  transfers between devices with their start and end apart: 11, of which 4 were waited for; matrix products, arithmetic and copies ran while one was open for 13% of the time, Pallas kernels for 0%

commit v1 on v0

v1 whole, which is shorter than its diff:
```python
import functools

import jax
import jax.numpy as jnp
from jax import lax
from jax.experimental import pallas as pl
from jax.experimental.pallas import tpu as pltpu
from jax.sharding import PartitionSpec as P

BF = jnp.bfloat16
F32 = jnp.float32
ROWS, HD = 256, 512
EPS = 1e-06
NX, NY, NZH = 4, 4, 4
AXES = ("seq", "head")


def flat(spot):
    zh, y, x, head = spot
    return ((zh % NZH) * NY * NX + (y % NY) * NX + x % NX) * 4 + head


def places():
    return [(zh, y, x, h) for zh in range(NZH) for y in range(NY) for x in range(NX) for h in range(4)]


def target(spot, by):
    zh, y, x, head = spot
    block = (zh * 16 + y * 4 + x + by) % 64
    return (block // 16, block // 4 % 4, block % 4, head)


def crosses(spot, by):
    return target(spot, by)[0] != spot[0]


def moved(spot, dx, dy):
    zh, y, x, head = spot
    return (zh, (y + dy) % NY, (x + dx) % NX, head)


def permute(x, pairs):
    return lax.ppermute(x, AXES, [(flat(a), flat(b)) for a, b in pairs])


def send_direct(x, by):
    return permute(x, [(s, target(s, by)) for s in places()])


def send_relayed(x, by, dx, dy):
    near = permute(x, [(s, target(s, by)) for s in places() if not crosses(s, by)])
    first = permute(x, [(s, moved(s, dx, dy)) for s in places() if crosses(s, by)])
    far = permute(first, [(moved(s, dx, dy), target(s, by)) for s in places() if crosses(s, by)])
    return near, far


def send_late(x, by):
    def inside(s):
        return (s[0],) + target(s, by)[1:]

    near = permute(x, [(s, inside(s)) for s in places()])
    far = permute(near, [(inside(s), target(s, by)) for s in places() if crosses(s, by)])
    return near, far


def from_far(by):
    inner = lax.axis_index("seq") % 16 - by
    return (inner < 0) | (inner >= 16)


def dot(a, b):
    return jnp.dot(a, b, preferred_element_type=F32)


def dot_nt(a, b):
    return lax.dot_general(a, b, (((1,), (1,)), ((), ())), preferred_element_type=F32)


def dot_tn(a, b):
    return lax.dot_general(a, b, (((0,), (0,)), ((), ())), preferred_element_type=F32)


def pick(far, pair):
    if len(pair) == 1:
        return pair[0][...]
    return jnp.where(far, pair[1][...], pair[0][...])


def update(w, r, k, v, rates, store):
    ka = dot(k, r[0])
    kb = dot(k, r[1])
    s = jax.nn.sigmoid(ka)
    kas = ka * s
    kh = (kas * kb).astype(BF)
    sv = (rates * v.astype(F32)).astype(BF)
    bk = dot_nt(sv, r[2])
    d1 = (bk * kb * (s * (1.0 + ka * (1.0 - s)))).astype(BF)
    d3 = (bk * kas).astype(BF)
    for i, (a, b) in enumerate(((k, d1), (k, d3), (kh, sv))):
        for j in range(0, HD, 256):
            cols = slice(j, j + 256)
            old = w(i, cols)
            new = old + dot_tn(a, b[:, cols])
            before = jnp.mean(old * old, axis=0, keepdims=True) + EPS
            after = jnp.mean(new * new, axis=0, keepdims=True) + EPS
            store(i, cols, new * jnp.sqrt(before / after))


def fast_out(r, q, gain):
    qa = dot(q, r[0])
    qb = dot(q, r[1])
    qh = (qa * jax.nn.sigmoid(qa) * qb).astype(BF)
    fo = dot(qh, r[2])
    return fo * lax.rsqrt(jnp.mean(fo * fo, axis=1, keepdims=True) + EPS) * gain


def window(q, kp, k, vp, v):
    scale = HD**-0.5
    row = lax.broadcasted_iota(jnp.int32, (ROWS, ROWS), 0)
    col = lax.broadcasted_iota(jnp.int32, (ROWS, ROWS), 1)
    old = jnp.where(col > row, dot_nt(q, kp) * scale, -1e30)
    own = jnp.where(col <= row, dot_nt(q, k) * scale, -1e30)
    peak = jnp.maximum(jnp.max(old, axis=1, keepdims=True), jnp.max(own, axis=1, keepdims=True))
    old = jnp.exp(old - peak)
    own = jnp.exp(own - peak)
    total = jnp.sum(old, axis=1, keepdims=True) + jnp.sum(own, axis=1, keepdims=True)
    return dot((old / total).astype(BF), vp) + dot((own / total).astype(BF), v)


def project(cm, weight, give, keep):
    head = lax.axis_index("head")
    z_lo, core = head // 2, head % 2
    for out, c in ((give, 1 - core), (keep, core)):
        for i, z in enumerate((z_lo, 1 - z_lo)):
            at = pl.multiple_of((z * 2 + c) * HD, HD)
            out[i] = dot(cm, weight[:, pl.ds(at, HD)]).astype(BF)


def first_tick(u, k, v, rates, q, gain, state, normed):
    r = [u[i].astype(BF) for i in range(3)]

    def store(i, cols, new):
        state[i, :, cols] = new

    update(lambda i, cols: u[i, :, cols], r, k[...], v[...], rates[...], store)
    normed[...] = fast_out(r, q[...], gain[...])


def second_update(u, k, vn, vf, rates, w1, w3, w2):
    far = from_far(-1)
    r = [u[i].astype(BF) for i in range(3)]
    outs = (w1, w3, w2)

    def store(i, cols, new):
        outs[i][:, cols] = new.astype(BF)

    update(lambda i, cols: u[i, :, cols], r, k[...], pick(far, (vn, vf)), rates[...], store)


def second_mix(u, q, kp, vp, k, vn, vf, gain, cm):
    far = from_far(-1)
    r = [u[i].astype(BF) for i in range(3)]
    att = window(q[...], kp[...], k[...], vp[...], pick(far, (vn, vf)))
    cm[...] = (att + fast_out(r, q[...], gain[...])).astype(BF)


def first_mix(q, kvn, kvf, k, v, normed, weight, give, keep):
    far = from_far(1)
    kv = pick(far, (kvn, kvf))
    cm = (window(q[...], kv[0], k[...], kv[1], v[...]) + normed[...]).astype(BF)
    project(cm, weight, give, keep)


def project_only(cm, weight, give, keep):
    project(cm[...], weight, give, keep)


def attend(q, kvn, kvf, k, v, att):
    far = from_far(1)
    kv = pick(far, (kvn, kvf))
    att[...] = window(q[...], kv[0], k[...], kv[1], v[...])


def third_mix(w1n, w1f, w3, w2n, w2f, q, att, gain, weight, give, keep, m1, m3, m2):
    far = from_far(2)
    r = [pick(far, (w1n, w1f)), w3[...], pick(far, (w2n, w2f))]
    for m, x in zip((m1, m3, m2), r):
        m[...] = x
    cm = (att[...] + fast_out(r, q[...], gain[...])).astype(BF)
    project(cm, weight, give, keep)


def third_update(m1, m3, m2, k, v, rates, out):
    ms = (m1, m3, m2)

    def store(i, cols, new):
        out[i, :, cols] = new

    update(lambda i, cols: ms[i][:, cols].astype(F32), [m[...] for m in ms], k[...], v[...], rates[...], store)


def call(body, outs, args, matmuls):
    whole = pl.BlockSpec(memory_space=pltpu.VMEM)
    size = sum(a.size * a.dtype.itemsize for a in args)
    return pl.pallas_call(
        body,
        out_shape=[jax.ShapeDtypeStruct(s, d) for s, d in outs],
        in_specs=[whole] * len(args),
        out_specs=[whole] * len(outs),
        compiler_params=pltpu.CompilerParams(vmem_limit_bytes=40 * 1024 * 1024),
        cost_estimate=pl.CostEstimate(flops=matmuls * 2 * ROWS * HD * HD * 2, bytes_accessed=size, transcendentals=ROWS * HD),
    )(*args)


PAIR = ((2, ROWS, HD), BF)
FLAT = ((ROWS, HD), BF)
SQUARE = ((HD, HD), BF)
STATE = ((3, HD, HD), F32)


def head_sum(give, keep):
    spots = places()
    got = permute(give, [(s, s[:3] + (s[3] ^ 1,)) for s in spots])
    pair = got.astype(F32) + keep.astype(F32)
    other = permute(pair[1].astype(BF), [(s, s[:3] + (s[3] ^ 2,)) for s in spots])
    return (pair[0] + other.astype(F32)).astype(BF)


def after(x, y):
    return lax.optimization_barrier((x, y))[0]


def on_device(queries, keys, values, rates, gain, weight, incoming):
    gain = gain.reshape(1, HD)
    u0 = incoming[0, 0]
    q = [queries[t] for t in range(3)]
    k = [keys[t] for t in range(4)]
    v = [values[t] for t in range(4)]

    k2b = send_direct(k[2], -1)
    v2n, v2f = send_late(v[2], -1)
    r1b = send_direct(rates[1].reshape(2, 128), -1).reshape(ROWS, 1)
    kv0 = send_relayed(jnp.stack([k[0], v[0]]), 1, 1, 0)
    kv2 = send_late(jnp.stack([k[2], v[2]]), 1)
    q1b = send_direct(after(q[1], k2b), -1)

    state, normed0 = call(first_tick, [STATE, ((ROWS, HD), F32)], (u0, k[1], v[1], rates[0], q[0], gain), 9)
    w1, w3, w2 = call(second_update, [SQUARE] * 3, (state, k2b, v2n, v2f, r1b), 6)
    w3 = send_direct(w3, 2)
    w1 = send_relayed(w1, 2, 0, 1)
    w2 = send_relayed(w2, 2, 0, -1)
    (cm1,) = call(second_mix, [FLAT], (state, q1b, k[1], v[1], k2b, v2n, v2f, gain), 5)
    cm1 = send_direct(cm1, 1)
    give0, keep0 = call(first_mix, [PAIR] * 2, (q[0], *kv0, k[1], v[1], normed0, weight), 6)
    (att2,) = call(attend, [((ROWS, HD), F32)], (q[2], *kv2, k[3], v[3]), 2)
    out0 = head_sum(give0, keep0)
    give1, keep1 = call(project_only, [PAIR] * 2, (cm1, weight), 4)
    out1 = head_sum(give1, keep1)
    give2, keep2, m1, m3, m2 = call(third_mix, [PAIR] * 2 + [SQUARE] * 3, (*w1, w3, *w2, q[2], att2, gain, weight), 7)
    out2 = head_sum(give2, keep2)
    (outgoing,) = call(third_update, [STATE], (m1, m3, m2, k[3], v[3], rates[2]), 6)
    return jnp.stack([out0, out1, out2]), outgoing[None, None]


def solution(mesh):
    placed = (
        P(None, "seq", "head"),
        P(None, "seq", "head"),
        P(None, "seq", "head"),
        P(None, "seq", "head"),
        P("head"),
        P("head", None),
        P("seq", "head", None, None, None),
    )
    return jax.shard_map(
        on_device,
        mesh=mesh,
        in_specs=placed,
        out_specs=(P(None, "seq", "head"), P("seq", "head", None, None, None)),
        check_vma=False,
    )
```

time: 453 us -> 153 us (0.34)
  waiting for transfers between devices: 359 us -> 15.3 us
  starting transfers between devices: 4.63 us -> 94.1 us
  matrix products: 41.6 us -> 0 us
  other arithmetic: 26.9 us -> 4.34 us
  Pallas kernels: 0 us -> 22 us
  between operations: 14.1 us -> 1.01 us
  local copies, waits for them, and re-layouts: 6.24 us -> 15.5 us
    ppermute x8 -> x24, waiting for transfers between devices: 328 us -> 15.3 us  [permute(): return lax.ppermute(x, AXES, [(flat(a), flat(b)) for a, b in pairs])]
    ppermute x8 -> x24, starting transfers between devices: 4.51 us -> 94.1 us  [permute(): return lax.ppermute(x, AXES, [(flat(a), flat(b)) for a, b in pairs])]
    dot_general x30 -> x0, matrix products: 41.6 us -> none  [the longest x3 9.95 us: on_device(): jnp.dot(combined, out_weight, preferred_element_type=jnp.float32)]
    reduce_scatter x3 -> x0, waiting for transfers between devices: 31 us -> none  [on_device(): lax.psum_scatter(partial_value.astype(jnp.bfloat16), 'head', scatter_dime...]
    pallas_call x0 -> x8, Pallas kernels: none -> 22 us  [call(): pl.pallas_call(body, out_shape=[jax.ShapeDtypeStruct(s, d) for s, d in ou...]
    mul x2 -> x0, other arithmetic: 7.08 us -> none  [fast_update(): return stepped * jnp.sqrt((before_sq + 1e-06) / (after_sq + 1e-06))]
    reduce_sum x6 -> x0, other arithmetic: 6.65 us -> none  [the longest x3 6.27 us: fast_update(): before_sq = jnp.mean(fast_state * fast_state, axis=1, keepdims=True)]
    convert_element_type x3 -> x0, other arithmetic: 6.51 us -> none  [on_device(): rounded = fast_state.astype(jnp.bfloat16)]
  transfers between devices with their start and end apart: 11 -> 24, of which waited for: 4 -> 5; matrix products, arithmetic and copies ran while one was open for 13% -> 3% of each run, Pallas kernels for 0% -> 14%
where the time goes in v1:
time: 153 us; the launch traced here: 152 us
  starting transfers between devices  94.1 us (62%)
  Pallas kernels  22 us (14%)
  local copies, waits for them, and re-layouts  15.5 us (10%)
  waiting for transfers between devices  15.3 us (10%)
  other arithmetic  4.34 us (3%)
    ppermute x24, starting transfers between devices, permute(): return lax.ppermute(x, AXES, [(flat(a), flat(b)) for a, b in pairs])  94.1 us
    pallas_call x8, Pallas kernels, call(): pl.pallas_call(body, out_shape=[jax.ShapeDtypeStruct(s, d) for s, d in ou...  22 us
    ppermute x24, waiting for transfers between devices, permute(): return lax.ppermute(x, AXES, [(flat(a), flat(b)) for a, b in pairs])  15.3 us
    unnamed x40, local copies, waits for them, and re-layouts  9.84 us
  transfers between devices with their start and end apart: 24, of which 5 were waited for; matrix products, arithmetic and copies ran while one was open for 3% of the time, Pallas kernels for 14%

profile of v1, /device:TPU:1, one launch (start us, length us, event | category | flops | bytes accessed | tf_op | source)
XLA Modules:
  0.0 152.3 jit_solution(15693884129687275449)
XLA Ops:
  0.6 2.1 %fusion.12 = (bf16[1,256,512]{2,1,0:T(8,128)(2,1)S(1)}, bf16[256,512]{1,0:T(8,128)(2,1)S(1)}, bf16[256,512]{1,0:T(8,128)(2,1)}, bf16[256,512]{1,0:T(8,128)(2,1)S(1)}, bf16[1,256,512]{2,1,0:T(8,128)(2,1)S(1)}) fusion(bf16[4,256,512]{2,1,0:T(8,128)(2,1)} %param.8), kind=kLoop, calls=%fused_computation.35 | loop fusion | bytes 2359296 | tf_op jit(solution)/shard_map/slice | solution.py:237
  2.7 2.2 %fusion.13 = (bf16[1,256,512]{2,1,0:T(8,128)(2,1)S(1)}, bf16[256,512]{1,0:T(8,128)(2,1)S(1)}, bf16[256,512]{1,0:T(8,128)(2,1)}, bf16[256,512]{1,0:T(8,128)(2,1)}, bf16[1,256,512]{2,1,0:T(8,128)(2,1)S(1)}) fusion(bf16[4,256,512]{2,1,0:T(8,128)(2,1)} %param.9), kind=kLoop, calls=%fused_computation.36 | loop fusion | bytes 2359296 | tf_op jit(solution)/shard_map/slice | solution.py:238
  7.2 4.8 %collective-permute-start = (bf16[2,256,512]{2,1,0:T(8,128)(2,1)}, bf16[2,256,512]{2,1,0:T(8,128)(2,1)}, u32[]{:S(2)}, u32[]{:S(2)}) collective-permute-start(bf16[2,256,512]{2,1,0:T(8,128)(2,1)} %pad_maximum_fusion.1), channel_id=1, source_target_pairs={{0,4},{1,5},{2,6},{3,7},{4,8},{5,9},{6,10},{7,11},{8,12},{9,13},{1... | collective-permute-start | bytes 1572872 | tf_op jit(solution)/shard_map/ppermute | solution.py:43
  12.0 9.5 %collective-permute-start.5 = (bf16[256,512]{1,0:T(8,128)(2,1)S(1)}, bf16[256,512]{1,0:T(8,128)(2,1)S(1)}, u32[]{:S(2)}, u32[]{:S(2)}) collective-permute-start(bf16[256,512]{1,0:T(8,128)(2,1)S(1)} %get-tuple-element.33), channel_id=1, source_target_pairs={{0,252},{1,253},{2,254},{3,255},{4,0},{5,1},{6,2},{7,3},{8,4},{9,5... | collective-permute-start | bytes 786440 | tf_op jit(solution)/shard_map/ppermute | solution.py:43
  24.7 4.3 %collective-permute-done.5.k = bf16[256,512]{1,0:T(8,128)(2,1)S(1)} collective-permute-done((bf16[256,512]{1,0:T(8,128)(2,1)S(1)}, bf16[256,512]{1,0:T(8,128)(2,1)S(1)}, u32[]{:S(2)}, u32[]{:S(2)}) %collective-permute-start.5) | collective-permute-done | bytes 262176 | tf_op jit(solution)/shard_map/ppermute | solution.py:43
  29.8 8.7 %collective-permute-start.6 = (bf16[256,512]{1,0:T(8,128)(2,1)}, bf16[256,512]{1,0:T(8,128)(2,1)}, u32[]{:S(2)}, u32[]{:S(2)}) collective-permute-start(bf16[256,512]{1,0:T(8,128)(2,1)} %get-tuple-element.21), channel_id=1, source_target_pairs={{0,252},{1,253},{2,254},{3,255},{4,0},{5,1},{6,2},{7,3},{8,4},{9,5... | collective-permute-start | bytes 786440 | tf_op jit(solution)/shard_map/ppermute | solution.py:43
  44.1 1.9 %copy-done.12 = f32[1,1,3,512,512]{4,3,2,1,0:T(8,128)S(1)} copy-done((f32[1,1,3,512,512]{4,3,2,1,0:T(8,128)S(1)}, f32[1,1,3,512,512]{4,3,2,1,0:T(8,128)}, u32[]{:S(2)}) %copy-start.12) | copy-done | bytes 3145752
  46.0 2.5 %shard_map.86 = (f32[3,512,512]{2,1,0:T(8,128)S(1)}, f32[256,512]{1,0:T(8,128)S(1)}) custom-call(f32[3,512,512]{2,1,0:T(8,128)S(1)} %bitcast.66, bf16[256,512]{1,0:T(8,128)(2,1)S(1)} %copy-done.1, bf16[256,512]{1,0:T(8,128)(2,1)S(1)} %copy-done.3, f32[256,1]{1,0:T(8,128)S(1)} %copy.9.rates, bf16[256,512]{1,0:T(8,128)(2,1)S(1)} %copy-done.9, ...), custom_call_target="tpu_custom_call" | custom-call | flops 2415919104 | bytes 3935232 | tf_op jit(solution)/shard_map/pallas_call | solution.py:205
  49.3 3.1 %shard_map.88 = bf16[256,512]{1,0:T(8,128)(2,1)} custom-call(f32[3,512,512]{2,1,0:T(8,128)S(1)} %get-tuple-element.20.u, bf16[256,512]{1,0:T(8,128)(2,1)} %collective-permute-done.6.q, bf16[256,512]{1,0:T(8,128)(2,1)S(1)} %copy-done.1, bf16[256,512]{1,0:T(8,128)(2,1)S(1)} %copy-done.3, bf16[256,512]{1,0:T(8,128)(2,1)S(1)} %copy-done.7, ...), custom_call_target="tpu_custom_call" | custom-call | flops 1342177280 | bytes 4720640 | tf_op jit(solution)/shard_map/pallas_call | solution.py:205
  52.5 7.8 %collective-permute-start.12 = (f32[2,128]{1,0:T(2,128)S(1)}, f32[2,128]{1,0:T(2,128)S(1)}, u32[]{:S(2)}, u32[]{:S(2)}) collective-permute-start(f32[2,128]{1,0:T(2,128)S(1)} %bitcast.68), channel_id=1, source_target_pairs={{0,252},{1,253},{2,254},{3,255},{4,0},{5,1},{6,2},{7,3},{8,4},{9,5... | collective-permute-start | bytes 3080 | tf_op jit(solution)/shard_map/ppermute | solution.py:43
  62.1 4.0 %shard_map.90 = (bf16[512,512]{1,0:T(8,128)(2,1)}, bf16[512,512]{1,0:T(8,128)(2,1)}, bf16[512,512]{1,0:T(8,128)(2,1)}) custom-call(f32[3,512,512]{2,1,0:T(8,128)S(1)} %get-tuple-element.20.u, bf16[256,512]{1,0:T(8,128)(2,1)S(1)} %copy-done.8, bf16[256,512]{1,0:T(8,128)(2,1)} %collective-permute-done.7.vn, bf16[256,512]{1,0:T(8,128)(2,1)} %collective-permute-done.8.vf, ...), custom_call_target="tpu_custom_call" | custom-call | flops 1610612736 | bytes 3933184 | tf_op jit(solution)/shard_map/pallas_call | solution.py:205
  69.3 1.9 %collective-permute-start.21 = (bf16[2,256,512]{2,1,0:T(8,128)(2,1)}, bf16[2,256,512]{2,1,0:T(8,128)(2,1)S(1)}, u32[]{:S(2)}, u32[]{:S(2)}) collective-permute-start(bf16[2,256,512]{2,1,0:T(8,128)(2,1)} %collective-permute-done.20.kvn), channel_id=1, source_target_pairs={{0,64},{1,65},{2,66},{3,67},{64,128},{65,129},{66,130},{67,131},{1... | collective-permute-start | bytes 1572872 | tf_op jit(solution)/shard_map/ppermute | solution.py:43
  71.2 2.2 %shard_map.89 = (bf16[2,256,512]{2,1,0:T(8,128)(2,1)}, bf16[2,256,512]{2,1,0:T(8,128)(2,1)S(1)}) custom-call(bf16[256,512]{1,0:T(8,128)(2,1)} %collective-permute-done.9.cm, bf16[512,2048]{1,0:T(8,128)(2,1)S(1)} %copy-done.13), custom_call_target="tpu_custom_call" | custom-call | flops 1073741824 | bytes 2359296 | tf_op jit(solution)/shard_map/pallas_call | solution.py:205
  73.4 6.1 %collective-permute-start.10 = (bf16[2,256,512]{2,1,0:T(8,128)(2,1)}, bf16[2,256,512]{2,1,0:T(8,128)(2,1)}, u32[]{:S(2)}, u32[]{:S(2)}) collective-permute-start(bf16[2,256,512]{2,1,0:T(8,128)(2,1)} %get-tuple-element.22), channel_id=1, source_target_pairs={{0,1},{1,0},{2,3},{3,2},{4,5},{5,4},{6,7},{7,6},{8,9},{9,8},{10,11... | collective-permute-start | bytes 1572872 | tf_op jit(solution)/shard_map/ppermute | solution.py:43
  82.3 2.5 %shard_map.87 = (bf16[2,256,512]{2,1,0:T(8,128)(2,1)S(1)}, bf16[2,256,512]{2,1,0:T(8,128)(2,1)S(1)}) custom-call(bf16[256,512]{1,0:T(8,128)(2,1)S(1)} %copy-done.10, bf16[2,256,512]{2,1,0:T(8,128)(2,1)} %collective-permute-done.kvn, bf16[2,256,512]{2,1,0:T(8,128)(2,1)} %collective-permute-done.2.kvf, bf16[256,512]{1,0:T(8,128)(2,1)S(1)} %copy-done.2, ...), custom_call_target="tpu_custom_call" | custom-call | flops 1610612736 | bytes 4456448 | tf_op jit(solution)/shard_map/pallas_call | solution.py:205
  84.9 2.0 %collective-permute-done.21.kvf = bf16[2,256,512]{2,1,0:T(8,128)(2,1)S(1)} collective-permute-done((bf16[2,256,512]{2,1,0:T(8,128)(2,1)}, bf16[2,256,512]{2,1,0:T(8,128)(2,1)S(1)}, u32[]{:S(2)}, u32[]{:S(2)}) %collective-permute-start.21) | collective-permute-done | bytes 524320 | tf_op jit(solution)/shard_map/ppermute | solution.py:43
  92.2 1.8 %shard_map.91.att = f32[256,512]{1,0:T(8,128)S(1)} custom-call(bf16[256,512]{1,0:T(8,128)(2,1)S(1)} %copy-done.5, bf16[2,256,512]{2,1,0:T(8,128)(2,1)} %collective-permute-done.20.kvn, bf16[2,256,512]{2,1,0:T(8,128)(2,1)S(1)} %collective-permute-done.21.kvf, bf16[256,512]{1,0:T(8,128)(2,1)S(1)} %get-tuple-element.35.k, bf16[256,512]{1,0:T(8,128)(2,1)S(1)} %copy-done), custom_call_target="tpu_custom_call" | custom-call | flops 536870912 | bytes 1835008 | tf_op jit(solution)/shard_map/pallas_call | solution.py:205
  94.0 12.3 %collective-permute-start.3 = (bf16[2,256,512]{2,1,0:T(8,128)(2,1)S(1)}, bf16[2,256,512]{2,1,0:T(8,128)(2,1)S(1)}, u32[]{:S(2)}, u32[]{:S(2)}) collective-permute-start(bf16[2,256,512]{2,1,0:T(8,128)(2,1)S(1)} %get-tuple-element.18), channel_id=1, source_target_pairs={{0,1},{1,0},{2,3},{3,2},{4,5},{5,4},{6,7},{7,6},{8,9},{9,8},{10,11... | collective-permute-start | bytes 1572872 | tf_op jit(solution)/shard_map/ppermute | solution.py:43
  107.5 7.5 %collective-permute-start.11 = (bf16[256,512]{1,0:T(8,128)(2,1)S(1)}, bf16[256,512]{1,0:T(8,128)(2,1)S(1)}, u32[]{:S(2)}, u32[]{:S(2)}) collective-permute-start(bf16[256,512]{1,0:T(8,128)(2,1)S(1)} %fusion.9), channel_id=1, source_target_pairs={{0,2},{1,3},{2,0},{3,1},{4,6},{5,7},{6,4},{7,5},{8,10},{9,11},{10,... | collective-permute-start | bytes 786440 | tf_op jit(solution)/shard_map/ppermute | solution.py:43
  115.0 2.5 %shard_map.92 = (bf16[2,256,512]{2,1,0:T(8,128)(2,1)S(1)}, bf16[2,256,512]{2,1,0:T(8,128)(2,1)S(1)}, bf16[512,512]{1,0:T(8,128)(2,1)S(1)}, bf16[512,512]{1,0:T(8,128)(2,1)S(1)}, bf16[512,512]{1,0:T(8,128)(2,1)S(1)}) custom-call(bf16[512,512]{1,0:T(8,128)(2,1)S(1)} %collective-permute-done.13.w1n, bf16[512,512]{1,0:T(8,128)(2,1)S(1)} %collective-permute-done.15.w1f, ...), custom_call_target="tpu_custom_call" | custom-call | flops 1879048192 | bytes 5507072 | tf_op jit(solution)/shard_map/pallas_call | solution.py:205
  117.5 19.9 %collective-permute-start.22 = (bf16[2,256,512]{2,1,0:T(8,128)(2,1)S(1)}, bf16[2,256,512]{2,1,0:T(8,128)(2,1)S(1)}, u32[]{:S(2)}, u32[]{:S(2)}) collective-permute-start(bf16[2,256,512]{2,1,0:T(8,128)(2,1)S(1)} %get-tuple-element.27), channel_id=1, source_target_pairs={{0,1},{1,0},{2,3},{3,2},{4,5},{5,4},{6,7},{7,6},{8,9},{9,8},{10,11... | collective-permute-start | bytes 1572872 | tf_op jit(solution)/shard_map/ppermute | solution.py:43
  137.7 3.4 %shard_map.93 = f32[3,512,512]{2,1,0:T(8,128)} custom-call(bf16[512,512]{1,0:T(8,128)(2,1)S(1)} %get-tuple-element.29.m1, bf16[512,512]{1,0:T(8,128)(2,1)S(1)} %get-tuple-element.30.m3, bf16[512,512]{1,0:T(8,128)(2,1)S(1)} %get-tuple-element.31.m2, bf16[256,512]{1,0:T(8,128)(2,1)S(1)} %get-tuple-element.35.k, bf16[256,512]{1,0:T(8,128)(2,1)S(1)} %copy-done, ...), custom_call_target="tpu_custom_call" | custom-call | flops 1610612736 | bytes 2098176 | tf_op jit(solution)/shard_map/pallas_call | solution.py:205
  143.0 2.7 %collective-permute-done.4 = bf16[256,512]{1,0:T(8,128)(2,1)S(1)} collective-permute-done((bf16[256,512]{1,0:T(8,128)(2,1)S(1)}, bf16[256,512]{1,0:T(8,128)(2,1)S(1)}, u32[]{:S(2)}, u32[]{:S(2)}) %collective-permute-start.4) | collective-permute-done | bytes 262176 | tf_op jit(solution)/shard_map/ppermute | solution.py:43
  145.7 5.5 %collective-permute-done.23 = bf16[256,512]{1,0:T(8,128)(2,1)S(1)} collective-permute-done((bf16[256,512]{1,0:T(8,128)(2,1)S(1)}, bf16[256,512]{1,0:T(8,128)(2,1)S(1)}, u32[]{:S(2)}, u32[]{:S(2)}) %collective-permute-start.23) | collective-permute-done | bytes 262176 | tf_op jit(solution)/shard_map/ppermute | solution.py:43
  (91 shorter events, 30.0 us)
Async XLA Ops:
  5.7 34.2 %collective-permute-start.1 = (bf16[2,256,512]{2,1,0:T(8,128)(2,1)}, bf16[2,256,512]{2,1,0:T(8,128)(2,1)}, u32[]{:S(2)}, u32[]{:S(2)}) collective-permute-start(bf16[2,256,512]{2,1,0:T(8,128)(2,1)} %pad_maximum_fusion.1), channel_id=1, source_target_pairs={{60,48},{61,49},{62,50},{63,51},{124,112},{125,113},{126,114},{127... | collective-permute-start | bytes 1572872 | tf_op jit(solution)/shard_map/ppermute | solution.py:43
  7.2 60.6 %collective-permute-start = (bf16[2,256,512]{2,1,0:T(8,128)(2,1)}, bf16[2,256,512]{2,1,0:T(8,128)(2,1)}, u32[]{:S(2)}, u32[]{:S(2)}) collective-permute-start(bf16[2,256,512]{2,1,0:T(8,128)(2,1)} %pad_maximum_fusion.1), channel_id=1, source_target_pairs={{0,4},{1,5},{2,6},{3,7},{4,8},{5,9},{6,10},{7,11},{8,12},{9,13},{1... | collective-permute-start | bytes 1572872 | tf_op jit(solution)/shard_map/ppermute | solution.py:43
  12.0 17.1 %collective-permute-start.5 = (bf16[256,512]{1,0:T(8,128)(2,1)S(1)}, bf16[256,512]{1,0:T(8,128)(2,1)S(1)}, u32[]{:S(2)}, u32[]{:S(2)}) collective-permute-start(bf16[256,512]{1,0:T(8,128)(2,1)S(1)} %get-tuple-element.33), channel_id=1, source_target_pairs={{0,252},{1,253},{2,254},{3,255},{4,0},{5,1},{6,2},{7,3},{8,4},{9,5... | collective-permute-start | bytes 786440 | tf_op jit(solution)/shard_map/ppermute | solution.py:43
  21.5 16.9 %collective-permute-start.7 = (bf16[256,512]{1,0:T(8,128)(2,1)S(1)}, bf16[256,512]{1,0:T(8,128)(2,1)}, u32[]{:S(2)}, u32[]{:S(2)}) collective-permute-start(bf16[256,512]{1,0:T(8,128)(2,1)S(1)} %get-tuple-element.38), channel_id=1, source_target_pairs={{0,60},{1,61},{2,62},{3,63},{4,0},{5,1},{6,2},{7,3},{8,4},{9,5},{1... | collective-permute-start | bytes 786440 | tf_op jit(solution)/shard_map/ppermute | solution.py:43
  22.4 43.8 %collective-permute-start.20 = (bf16[2,256,512]{2,1,0:T(8,128)(2,1)}, bf16[2,256,512]{2,1,0:T(8,128)(2,1)}, u32[]{:S(2)}, u32[]{:S(2)}) collective-permute-start(bf16[2,256,512]{2,1,0:T(8,128)(2,1)} %pad_maximum_fusion.2), channel_id=1, source_target_pairs={{0,4},{1,5},{2,6},{3,7},{4,8},{5,9},{6,10},{7,11},{8,12},{9,13},{1... | collective-permute-start | bytes 1572872 | tf_op jit(solution)/shard_map/ppermute | solution.py:43
  29.8 19.6 %collective-permute-start.6 = (bf16[256,512]{1,0:T(8,128)(2,1)}, bf16[256,512]{1,0:T(8,128)(2,1)}, u32[]{:S(2)}, u32[]{:S(2)}) collective-permute-start(bf16[256,512]{1,0:T(8,128)(2,1)} %get-tuple-element.21), channel_id=1, source_target_pairs={{0,252},{1,253},{2,254},{3,255},{4,0},{5,1},{6,2},{7,3},{8,4},{9,5... | collective-permute-start | bytes 786440 | tf_op jit(solution)/shard_map/ppermute | solution.py:43
  38.4 10.9 %collective-permute-start.8 = (bf16[256,512]{1,0:T(8,128)(2,1)}, bf16[256,512]{1,0:T(8,128)(2,1)}, u32[]{:S(2)}, u32[]{:S(2)}) collective-permute-start(bf16[256,512]{1,0:T(8,128)(2,1)} %collective-permute-done.7.vn), channel_id=1, source_target_pairs={{60,252},{61,253},{62,254},{63,255},{124,60},{125,61},{126,62},{12... | collective-permute-start | bytes 786440 | tf_op jit(solution)/shard_map/ppermute | solution.py:43
  40.0 33.5 %collective-permute-start.2 = (bf16[2,256,512]{2,1,0:T(8,128)(2,1)}, bf16[2,256,512]{2,1,0:T(8,128)(2,1)}, u32[]{:S(2)}, u32[]{:S(2)}) collective-permute-start(bf16[2,256,512]{2,1,0:T(8,128)(2,1)} %collective-permute-done.1), channel_id=1, source_target_pairs={{48,64},{49,65},{50,66},{51,67},{112,128},{113,129},{114,130},{115... | collective-permute-start | bytes 1572872 | tf_op jit(solution)/shard_map/ppermute | solution.py:43
  52.5 16.8 %collective-permute-start.9 = (bf16[256,512]{1,0:T(8,128)(2,1)}, bf16[256,512]{1,0:T(8,128)(2,1)}, u32[]{:S(2)}, u32[]{:S(2)}) collective-permute-start(bf16[256,512]{1,0:T(8,128)(2,1)} %shard_map.88), channel_id=1, source_target_pairs={{0,4},{1,5},{2,6},{3,7},{4,8},{5,9},{6,10},{7,11},{8,12},{9,13},{1... | collective-permute-start | bytes 786440 | tf_op jit(solution)/shard_map/ppermute | solution.py:43
  52.5 8.5 %collective-permute-start.12 = (f32[2,128]{1,0:T(2,128)S(1)}, f32[2,128]{1,0:T(2,128)S(1)}, u32[]{:S(2)}, u32[]{:S(2)}) collective-permute-start(f32[2,128]{1,0:T(2,128)S(1)} %bitcast.68), channel_id=1, source_target_pairs={{0,252},{1,253},{2,254},{3,255},{4,0},{5,1},{6,2},{7,3},{8,4},{9,5... | collective-permute-start | bytes 3080 | tf_op jit(solution)/shard_map/ppermute | solution.py:43
  66.1 22.1 %collective-permute-start.16 = (bf16[512,512]{1,0:T(8,128)(2,1)}, bf16[512,512]{1,0:T(8,128)(2,1)}, u32[]{:S(2)}, u32[]{:S(2)}) collective-permute-start(bf16[512,512]{1,0:T(8,128)(2,1)} %get-tuple-element.25), channel_id=1, source_target_pairs={{0,8},{1,9},{2,10},{3,11},{4,12},{5,13},{6,14},{7,15},{8,16},{9,17... | collective-permute-start | bytes 1572872 | tf_op jit(solution)/shard_map/ppermute | solution.py:43
  66.2 23.3 %collective-permute-start.14 = (bf16[512,512]{1,0:T(8,128)(2,1)}, bf16[512,512]{1,0:T(8,128)(2,1)}, u32[]{:S(2)}, u32[]{:S(2)}) collective-permute-start(bf16[512,512]{1,0:T(8,128)(2,1)} %get-tuple-element.24), channel_id=1, source_target_pairs={{56,8},{57,9},{58,10},{59,11},{60,12},{61,13},{62,14},{63,15},{120... | collective-permute-start | bytes 1572872 | tf_op jit(solution)/shard_map/ppermute | solution.py:43
  67.8 23.0 %collective-permute-start.18 = (bf16[512,512]{1,0:T(8,128)(2,1)}, bf16[512,512]{1,0:T(8,128)(2,1)}, u32[]{:S(2)}, u32[]{:S(2)}) collective-permute-start(bf16[512,512]{1,0:T(8,128)(2,1)} %get-tuple-element.26), channel_id=1, source_target_pairs={{56,40},{57,41},{58,42},{59,43},{60,44},{61,45},{62,46},{63,47},{1... | collective-permute-start | bytes 1572872 | tf_op jit(solution)/shard_map/ppermute | solution.py:43
  69.3 17.6 %collective-permute-start.21 = (bf16[2,256,512]{2,1,0:T(8,128)(2,1)}, bf16[2,256,512]{2,1,0:T(8,128)(2,1)S(1)}, u32[]{:S(2)}, u32[]{:S(2)}) collective-permute-start(bf16[2,256,512]{2,1,0:T(8,128)(2,1)} %collective-permute-done.20.kvn), channel_id=1, source_target_pairs={{0,64},{1,65},{2,66},{3,67},{64,128},{65,129},{66,130},{67,131},{1... | collective-permute-start | bytes 1572872 | tf_op jit(solution)/shard_map/ppermute | solution.py:43
  73.4 20.5 %collective-permute-start.10 = (bf16[2,256,512]{2,1,0:T(8,128)(2,1)}, bf16[2,256,512]{2,1,0:T(8,128)(2,1)}, u32[]{:S(2)}, u32[]{:S(2)}) collective-permute-start(bf16[2,256,512]{2,1,0:T(8,128)(2,1)} %get-tuple-element.22), channel_id=1, source_target_pairs={{0,1},{1,0},{2,3},{3,2},{4,5},{5,4},{6,7},{7,6},{8,9},{9,8},{10,11... | collective-permute-start | bytes 1572872 | tf_op jit(solution)/shard_map/ppermute | solution.py:43
  86.9 20.6 %collective-permute-start.13 = (bf16[512,512]{1,0:T(8,128)(2,1)}, bf16[512,512]{1,0:T(8,128)(2,1)S(1)}, u32[]{:S(2)}, u32[]{:S(2)}) collective-permute-start(bf16[512,512]{1,0:T(8,128)(2,1)} %get-tuple-element.24), channel_id=1, source_target_pairs={{0,8},{1,9},{2,10},{3,11},{4,12},{5,13},{6,14},{7,15},{8,16},{9,17... | collective-permute-start | bytes 1572872 | tf_op jit(solution)/shard_map/ppermute | solution.py:43
  88.2 26.8 %collective-permute-start.17 = (bf16[512,512]{1,0:T(8,128)(2,1)}, bf16[512,512]{1,0:T(8,128)(2,1)S(1)}, u32[]{:S(2)}, u32[]{:S(2)}) collective-permute-start(bf16[512,512]{1,0:T(8,128)(2,1)} %get-tuple-element.26), channel_id=1, source_target_pairs={{0,8},{1,9},{2,10},{3,11},{4,12},{5,13},{6,14},{7,15},{8,16},{9,17... | collective-permute-start | bytes 1572872 | tf_op jit(solution)/shard_map/ppermute | solution.py:43
  89.6 25.4 %collective-permute-start.15 = (bf16[512,512]{1,0:T(8,128)(2,1)}, bf16[512,512]{1,0:T(8,128)(2,1)S(1)}, u32[]{:S(2)}, u32[]{:S(2)}) collective-permute-start(bf16[512,512]{1,0:T(8,128)(2,1)} %collective-permute-done.14), channel_id=1, source_target_pairs={{8,64},{9,65},{10,66},{11,67},{12,68},{13,69},{14,70},{15,71},{72,... | collective-permute-start | bytes 1572872 | tf_op jit(solution)/shard_map/ppermute | solution.py:43
  90.9 24.1 %collective-permute-start.19 = (bf16[512,512]{1,0:T(8,128)(2,1)}, bf16[512,512]{1,0:T(8,128)(2,1)S(1)}, u32[]{:S(2)}, u32[]{:S(2)}) collective-permute-start(bf16[512,512]{1,0:T(8,128)(2,1)} %collective-permute-done.18), channel_id=1, source_target_pairs={{40,64},{41,65},{42,66},{43,67},{44,68},{45,69},{46,70},{47,71},{1... | collective-permute-start | bytes 1572872 | tf_op jit(solution)/shard_map/ppermute | solution.py:43
  94.0 43.5 %collective-permute-start.3 = (bf16[2,256,512]{2,1,0:T(8,128)(2,1)S(1)}, bf16[2,256,512]{2,1,0:T(8,128)(2,1)S(1)}, u32[]{:S(2)}, u32[]{:S(2)}) collective-permute-start(bf16[2,256,512]{2,1,0:T(8,128)(2,1)S(1)} %get-tuple-element.18), channel_id=1, source_target_pairs={{0,1},{1,0},{2,3},{3,2},{4,5},{5,4},{6,7},{7,6},{8,9},{9,8},{10,11... | collective-permute-start | bytes 1572872 | tf_op jit(solution)/shard_map/ppermute | solution.py:43
  107.5 35.4 %collective-permute-start.11 = (bf16[256,512]{1,0:T(8,128)(2,1)S(1)}, bf16[256,512]{1,0:T(8,128)(2,1)S(1)}, u32[]{:S(2)}, u32[]{:S(2)}) collective-permute-start(bf16[256,512]{1,0:T(8,128)(2,1)S(1)} %fusion.9), channel_id=1, source_target_pairs={{0,2},{1,3},{2,0},{3,1},{4,6},{5,7},{6,4},{7,5},{8,10},{9,11},{10,... | collective-permute-start | bytes 786440 | tf_op jit(solution)/shard_map/ppermute | solution.py:43
  117.5 23.7 %collective-permute-start.22 = (bf16[2,256,512]{2,1,0:T(8,128)(2,1)S(1)}, bf16[2,256,512]{2,1,0:T(8,128)(2,1)S(1)}, u32[]{:S(2)}, u32[]{:S(2)}) collective-permute-start(bf16[2,256,512]{2,1,0:T(8,128)(2,1)S(1)} %get-tuple-element.27), channel_id=1, source_target_pairs={{0,1},{1,0},{2,3},{3,2},{4,5},{5,4},{6,7},{7,6},{8,9},{9,8},{10,11... | collective-permute-start | bytes 1572872 | tf_op jit(solution)/shard_map/ppermute | solution.py:43
  137.6 8.0 %collective-permute-start.4 = (bf16[256,512]{1,0:T(8,128)(2,1)S(1)}, bf16[256,512]{1,0:T(8,128)(2,1)S(1)}, u32[]{:S(2)}, u32[]{:S(2)}) collective-permute-start(bf16[256,512]{1,0:T(8,128)(2,1)S(1)} %fusion.7), channel_id=1, source_target_pairs={{0,2},{1,3},{2,0},{3,1},{4,6},{5,7},{6,4},{7,5},{8,10},{9,11},{10,... | collective-permute-start | bytes 786440 | tf_op jit(solution)/shard_map/ppermute | solution.py:43
  141.4 9.9 %collective-permute-start.23 = (bf16[256,512]{1,0:T(8,128)(2,1)S(1)}, bf16[256,512]{1,0:T(8,128)(2,1)S(1)}, u32[]{:S(2)}, u32[]{:S(2)}) collective-permute-start(bf16[256,512]{1,0:T(8,128)(2,1)S(1)} %fusion.11), channel_id=1, source_target_pairs={{0,2},{1,3},{2,0},{3,1},{4,6},{5,7},{6,4},{7,5},{8,10},{9,11},{10,... | collective-permute-start | bytes 786440 | tf_op jit(solution)/shard_map/ppermute | solution.py:43
  (20 other events, 229.5 us)

commit v2 on v1

v2 whole, which is shorter than its diff:
```python
import functools

import jax
import jax.numpy as jnp
from jax import lax
from jax.experimental import pallas as pl
from jax.experimental.pallas import tpu as pltpu
from jax.sharding import PartitionSpec as P

BF = jnp.bfloat16
F32 = jnp.float32
ROWS, HD = 256, 512
EPS = 1e-06
NX, NY, NZH = 4, 4, 4
AXES = ("seq", "head")


def flat(spot):
    zh, y, x, head = spot
    return ((zh % NZH) * NY * NX + (y % NY) * NX + x % NX) * 4 + head


def places():
    return [(zh, y, x, h) for zh in range(NZH) for y in range(NY) for x in range(NX) for h in range(4)]


def target(spot, by):
    zh, y, x, head = spot
    block = (zh * 16 + y * 4 + x + by) % 64
    return (block // 16, block // 4 % 4, block % 4, head)


def crosses(spot, by):
    return target(spot, by)[0] != spot[0]


def moved(spot, dx, dy):
    zh, y, x, head = spot
    return (zh, (y + dy) % NY, (x + dx) % NX, head)


def permute(x, pairs):
    return lax.ppermute(x, AXES, [(flat(a), flat(b)) for a, b in pairs])


def send_direct(x, by):
    return permute(x, [(s, target(s, by)) for s in places()])


def send_near(x, by):
    return permute(x, [(s, target(s, by)) for s in places() if not crosses(s, by)])


def send_first(x, by, dx, dy):
    return permute(x, [(s, moved(s, dx, dy)) for s in places() if crosses(s, by)])


def send_far(x, by, dx, dy):
    return permute(x, [(moved(s, dx, dy), target(s, by)) for s in places() if crosses(s, by)])


def send_late(x, by):
    def inside(s):
        return (s[0],) + target(s, by)[1:]

    near = permute(x, [(s, inside(s)) for s in places()])
    return near, [(inside(s), target(s, by)) for s in places() if crosses(s, by)]


def from_far(by):
    inner = lax.axis_index("seq") % 16 - by
    return (inner < 0) | (inner >= 16)


def dot(a, b):
    return jnp.dot(a, b, preferred_element_type=F32)


def dot_nt(a, b):
    return lax.dot_general(a, b, (((1,), (1,)), ((), ())), preferred_element_type=F32)


def dot_tn(a, b):
    return lax.dot_general(a, b, (((0,), (0,)), ((), ())), preferred_element_type=F32)


def column(row):
    eye = lax.broadcasted_iota(jnp.int32, (ROWS, ROWS), 0) == lax.broadcasted_iota(jnp.int32, (ROWS, ROWS), 1)
    return jnp.sum(jnp.where(eye, row, 0.0), axis=1, keepdims=True)


def update(w, r, k, v, rates, store):
    ka = dot(k, r[0])
    kb = dot(k, r[1])
    s = jax.nn.sigmoid(ka)
    kas = ka * s
    kh = (kas * kb).astype(BF)
    sv = (rates * v.astype(F32)).astype(BF)
    bk = dot_nt(sv, r[2])
    d1 = (bk * kb * (s * (1.0 + ka * (1.0 - s)))).astype(BF)
    d3 = (bk * kas).astype(BF)
    for i, (a, b) in enumerate(((k, d1), (k, d3), (kh, sv))):
        for j in range(0, HD, 256):
            cols = slice(j, j + 256)
            old = w(i, cols)
            new = old + dot_tn(a, b[:, cols])
            before = jnp.mean(old * old, axis=0, keepdims=True) + EPS
            after = jnp.mean(new * new, axis=0, keepdims=True) + EPS
            store(i, cols, new * jnp.sqrt(before / after))


def fast_out(r, q, gain):
    qa = dot(q, r[0])
    qb = dot(q, r[1])
    qh = (qa * jax.nn.sigmoid(qa) * qb).astype(BF)
    fo = dot(qh, r[2])
    return fo * lax.rsqrt(jnp.mean(fo * fo, axis=1, keepdims=True) + EPS) * gain


def window(q, kp, k, vp, v):
    scale = HD**-0.5
    row = lax.broadcasted_iota(jnp.int32, (ROWS, ROWS), 0)
    col = lax.broadcasted_iota(jnp.int32, (ROWS, ROWS), 1)
    old = jnp.where(col > row, dot_nt(q, kp) * scale, -1e30)
    own = jnp.where(col <= row, dot_nt(q, k) * scale, -1e30)
    peak = jnp.maximum(jnp.max(old, axis=1, keepdims=True), jnp.max(own, axis=1, keepdims=True))
    old = jnp.exp(old - peak)
    own = jnp.exp(own - peak)
    total = jnp.sum(old, axis=1, keepdims=True) + jnp.sum(own, axis=1, keepdims=True)
    return dot((old / total).astype(BF), vp) + dot((own / total).astype(BF), v)


def project(cm, weight, give, own, far):
    head = lax.axis_index("head")
    z_lo, core = head // 2, head % 2

    def part(z, c):
        at = pl.multiple_of((z * 2 + c) * HD, HD)
        return dot(cm, weight[:, pl.ds(at, HD)]).astype(BF)

    give[1] = part(1 - z_lo, 1 - core)
    give[0] = part(z_lo, 1 - core)
    far[...] = part(1 - z_lo, core)
    own[...] = part(z_lo, core)


def pack_pair(keys, values, out, sems):
    copies = [pltpu.make_async_copy(a.at[2], out.at[i], sems.at[i]) for i, a in enumerate((keys, values))]
    for c in copies:
        c.start()
    for c in copies:
        c.wait()


def pack_rest(keys, values, queries, _, out, q1, sems):
    copies = [pltpu.make_async_copy(a.at[0], out.at[i], sems.at[i]) for i, a in enumerate((keys, values))]
    copies.append(pltpu.make_async_copy(queries.at[1], q1, sems.at[2]))
    for c in copies:
        c.start()
    for c in copies:
        c.wait()


def first_tick(u, k, v, rates, q, gain, state, normed):
    r = [u[0, 0, i].astype(BF) for i in range(3)]

    def store(i, cols, new):
        state[i, :, cols] = new

    update(lambda i, cols: u[0, 0, i, :, cols], r, k[0], v[0], column(rates[0]), store)
    normed[...] = fast_out(r, q[0], gain[...])


def second_update(u, kv, rates, *pieces):
    r = [u[i].astype(BF) for i in range(3)]

    def store(i, cols, new):
        new = new.astype(BF)
        start = 0
        for piece, rows in zip(pieces, PIECES):
            low, high = max(start, i * HD), min(start + rows, (i + 1) * HD)
            if low < high:
                piece[low - start : high - start, cols] = new[low - i * HD : high - i * HD]
            start += rows

    update(lambda i, cols: u[i, :, cols], r, kv[0], kv[1], column(rates[1]), store)


def second_mix(u, qn, qf, kp, vp, kv, gain, cm):
    q = jnp.where(from_far(-1), qf[...], qn[...])
    r = [u[i].astype(BF) for i in range(3)]
    att = window(q, kp[0], kv[0], vp[0], kv[1])
    cm[...] = (att + fast_out(r, q, gain[...])).astype(BF)


def first_mix(q, kvn, kvf, k, v, normed, weight, give, own, far):
    late = from_far(1)
    kp = jnp.where(late, kvf[0], kvn[0])
    vp = jnp.where(late, kvf[1], kvn[1])
    cm = (window(q[0], kp, k[0], vp, v[0]) + normed[...]).astype(BF)
    project(cm, weight, give, own, far)


def project_only(cm, weight, give, own, far):
    project(cm[...], weight, give, own, far)


def attend(q, kv, k, v, att):
    att[...] = window(q[0], kv[0], k[0], kv[1], v[0])


def third_mix(a, bn, bf, cn, cf, q, att, gain, weight, give, own, far, m):
    late = from_far(2)
    one, two = PIECES[0], PIECES[0] + PIECES[1]
    m[:one] = a[...]
    m[one:two] = jnp.where(late, bf[...], bn[...])
    m[two:] = jnp.where(late, cf[...], cn[...])
    r = [m[i * HD : (i + 1) * HD] for i in range(3)]
    cm = (att[...] + fast_out(r, q[0], gain[...])).astype(BF)
    project(cm, weight, give, own, far)


def third_update(m, k, v, rates, out):
    def store(i, cols, new):
        out[0, 0, i, :, cols] = new

    r = [m[i * HD : (i + 1) * HD] for i in range(3)]
    update(lambda i, cols: m[i * HD : (i + 1) * HD, cols].astype(F32), r, k[0], v[0], column(rates[2]), store)


def first_two(other0, got0, own0, other1, got1, own1, out):
    out[0] = (got0[0].astype(F32) + own0[...].astype(F32) + other0[...].astype(F32)).astype(BF)
    out[1] = (got1[0].astype(F32) + own1[...].astype(F32) + other1[...].astype(F32)).astype(BF)


def last_one(_, other, got, own, out):
    out[0] = (got[0].astype(F32) + own[...].astype(F32) + other[...].astype(F32)).astype(BF)


PIECES = (576, 480, 480)
WHOLE = pl.BlockSpec(memory_space=pltpu.VMEM)
HBM = pl.BlockSpec(memory_space=pl.ANY)


def slab(shape, index):
    return pl.BlockSpec(shape, lambda _, index=index: (index,) + (0,) * (len(shape) - 1))


def rows_of(t):
    return slab((1, ROWS, HD), t)


def call(body, outs, args, matmuls=0, scratch=(), **more):
    size = sum(a.size * a.dtype.itemsize for a, _ in args)
    return pl.pallas_call(
        body,
        out_shape=[jax.ShapeDtypeStruct(s, d) for s, d, _ in outs],
        grid=(1,),
        in_specs=[s for _, s in args],
        out_specs=[s for _, _, s in outs],
        scratch_shapes=list(scratch),
        compiler_params=pltpu.CompilerParams(vmem_limit_bytes=32 * 1024 * 1024),
        cost_estimate=pl.CostEstimate(flops=matmuls * 2 * ROWS * HD * HD * 2, bytes_accessed=size, transcendentals=ROWS * HD),
        **more,
    )(*[a for a, _ in args])


FLAT = ((ROWS, HD), BF, WHOLE)
WIDE = ((ROWS, HD), F32, WHOLE)
SUM = [((2, ROWS, HD), BF, WHOLE), FLAT, FLAT]
STATE = ((3, HD, HD), F32, WHOLE)


def head_sum(give, own, far):
    spots = places()
    got = permute(give, [(s, s[:3] + (s[3] ^ 1,)) for s in spots])
    pair = (got[1].astype(F32) + far.astype(F32)).astype(BF)
    other = permute(pair, [(s, s[:3] + (s[3] ^ 2,)) for s in spots])
    return (other, WHOLE), (got, WHOLE), (own, WHOLE)


def after(x, *ys):
    return lax.optimization_barrier((x,) + ys)[0]


def on_device(queries, keys, values, rates, gain, weight, incoming):
    gain = gain.reshape(1, HD)
    rates = rates.reshape(3, 1, ROWS)
    rate = (rates, slab((3, 1, ROWS), 0))
    gain = (gain, slab((1, HD), 0))
    weight = (weight, slab((HD, 4 * HD), 0))

    (kv2,) = call(pack_pair, [((2, ROWS, HD), BF, HBM)], ((keys, HBM), (values, HBM)), scratch=[pltpu.SemaphoreType.DMA((2,))])
    kv0, q1 = call(
        pack_rest,
        [((2, ROWS, HD), BF, HBM), ((ROWS, HD), BF, HBM)],
        ((keys, HBM), (values, HBM), (queries, HBM), (kv2, HBM)),
        scratch=[pltpu.SemaphoreType.DMA((3,))],
    )
    next_rates = send_direct(rates, -1)
    next_kv = send_direct(kv2, -1)
    q1n, q1_pairs = send_late(q1, -1)
    kv2 = send_direct(kv2, 1)
    kv0n, kv0_pairs = send_late(kv0, 1)

    state, normed0 = call(
        first_tick,
        [STATE, WIDE],
        (
            (incoming, slab((1, 1, 3, HD, HD), 0)),
            (keys, rows_of(1)),
            (values, rows_of(1)),
            rate,
            (queries, rows_of(0)),
            gain,
        ),
        9,
    )
    a, b, c = call(
        second_update,
        [((n, HD), BF, WHOLE) for n in PIECES],
        ((state, WHOLE), (next_kv, WHOLE), (next_rates, WHOLE)),
        6,
    )
    b1, c1 = send_first(b, 2, 0, 1), send_first(c, 2, 0, -1)
    a2, bn, cn = send_direct(a, 2), send_near(b, 2), send_near(c, 2)
    q1f = permute(after(q1n, a), q1_pairs)
    (cm1,) = call(
        second_mix,
        [FLAT],
        ((state, WHOLE), (q1n, WHOLE), (q1f, WHOLE), (keys, rows_of(1)), (values, rows_of(1)), (next_kv, WHOLE), gain),
        5,
    )
    kv0f = permute(after(kv0n, cm1), kv0_pairs)
    bf, cf = send_far(after(b1, cm1), 2, 0, 1), send_far(after(c1, cm1), 2, 0, -1)
    cm1 = send_direct(cm1, 1)
    sum0 = call(
        first_mix,
        SUM,
        ((queries, rows_of(0)), (kv0n, WHOLE), (kv0f, WHOLE), (keys, rows_of(1)), (values, rows_of(1)), (normed0, WHOLE), weight),
        6,
    )
    (att2,) = call(attend, [WIDE], ((queries, rows_of(2)), (kv2, WHOLE), (keys, rows_of(3)), (values, rows_of(3))), 2)
    sum0 = head_sum(*sum0)
    sum1 = head_sum(*call(project_only, SUM, ((cm1, WHOLE), weight), 4))
    (mixed,) = call(first_two, [((3, ROWS, HD), BF, slab((3, ROWS, HD), 0))], sum0 + sum1)
    *sum2, m = call(
        third_mix,
        SUM + [((3 * HD, HD), BF, WHOLE)],
        (
            (a2, WHOLE),
            (bn, WHOLE),
            (bf, WHOLE),
            (cn, WHOLE),
            (cf, WHOLE),
            (queries, rows_of(2)),
            (att2, WHOLE),
            gain,
            weight,
        ),
        7,
    )
    sum2 = head_sum(*sum2)
    (outgoing,) = call(
        third_update,
        [((1, 1, 3, HD, HD), F32, slab((1, 1, 3, HD, HD), 0))],
        ((m, WHOLE), (keys, rows_of(3)), (values, rows_of(3)), rate),
        6,
    )
    (mixed,) = call(
        last_one, [((3, ROWS, HD), BF, rows_of(2))], ((mixed, HBM),) + sum2, input_output_aliases={0: 0}
    )
    return mixed, outgoing


def solution(mesh):
    placed = (
        P(None, "seq", "head"),
        P(None, "seq", "head"),
        P(None, "seq", "head"),
        P(None, "seq", "head"),
        P("head"),
        P("head", None),
        P("seq", "head", None, None, None),
    )
    return jax.shard_map(
        on_device,
        mesh=mesh,
        in_specs=placed,
        out_specs=(P(None, "seq", "head"), P("seq", "head", None, None, None)),
        check_vma=False,
    )
```

time: 153 us -> 130 us (0.85)
  waiting for transfers between devices: 15.3 us -> 55.7 us
  starting transfers between devices: 94.1 us -> 55.5 us
  local copies, waits for them, and re-layouts: 15.5 us -> 2.48 us
  Pallas kernels: 22 us -> 15.4 us
  other arithmetic: 4.34 us -> 0.2 us
    ppermute x24 -> x21, waiting for transfers between devices: 15.3 us -> 55.7 us  [permute(): return lax.ppermute(x, AXES, [(flat(a), flat(b)) for a, b in pairs])]
    ppermute x24 -> x21, starting transfers between devices: 94.1 us -> 55.5 us  [permute(): return lax.ppermute(x, AXES, [(flat(a), flat(b)) for a, b in pairs])]
    unnamed x40 -> x18, local copies, waits for them, and re-layouts: 9.84 us -> 2.48 us
    pallas_call x8 -> x12, Pallas kernels: 22 us -> 15.4 us  [call(): pl.pallas_call(body, out_shape=[jax.ShapeDtypeStruct(s, d) for s, d, _ in...]
    slice x2 -> x0, local copies, waits for them, and re-layouts: 4.24 us -> none  [the longest x1 2.16 us: on_device(): v = [values[t] for t in range(4)]]
    another operation x6 -> x0, other arithmetic: 2.88 us -> none  [the longest x4 1.19 us: on_device(): return (jnp.stack([out0, out1, out2]), outgoing[None, None])]
  transfers between devices with their start and end apart: 24 -> 21, of which waited for: 5 -> 8; matrix products, arithmetic and copies ran while one was open for 3% -> 0% of each run, Pallas kernels for 14% -> 11%
where the time goes in v2:
time: 130 us
  waiting for transfers between devices  55.7 us (43%)
  starting transfers between devices  55.5 us (43%)
  Pallas kernels  15.4 us (12%)
  local copies, waits for them, and re-layouts  2.48 us (2%)
    ppermute x21, waiting for transfers between devices, permute(): return lax.ppermute(x, AXES, [(flat(a), flat(b)) for a, b in pairs])  55.7 us
    ppermute x21, starting transfers between devices, permute(): return lax.ppermute(x, AXES, [(flat(a), flat(b)) for a, b in pairs])  55.5 us
    pallas_call x12, Pallas kernels, call(): pl.pallas_call(body, out_shape=[jax.ShapeDtypeStruct(s, d) for s, d, _ in...  15.4 us
  transfers between devices with their start and end apart: 21, of which 8 were waited for; matrix products, arithmetic and copies ran while one was open for 0% of the time, Pallas kernels for 11%

profile of v2, /device:TPU:1, one launch (start us, length us, event | category | flops | bytes accessed | tf_op | source)
XLA Modules:
  0.0 130.1 jit_solution(4514255593912529699)
XLA Ops:
  3.2 11.6 %collective-permute-start.2 = (bf16[2,256,512]{2,1,0:T(8,128)(2,1)S(1)}, bf16[2,256,512]{2,1,0:T(8,128)(2,1)S(1)}, u32[]{:S(2)}, u32[]{:S(2)}) collective-permute-start(bf16[2,256,512]{2,1,0:T(8,128)(2,1)S(1)} %shard_map.86._), channel_id=1, source_target_pairs={{0,252},{1,253},{2,254},{3,255},{4,0},{5,1},{6,2},{7,3},{8,4},{9,5... | collective-permute-start | bytes 1572872 | tf_op jit(solution)/shard_map/ppermute | solution.py:43
  14.7 7.8 %collective-permute-start.3 = (f32[3,1,256]{2,1,0:T(1,128)}, f32[3,1,256]{2,1,0:T(1,128)S(1)}, u32[]{:S(2)}, u32[]{:S(2)}) collective-permute-start(f32[3,1,256]{2,1,0:T(1,128)} %bitcast.17), channel_id=1, source_target_pairs={{0,252},{1,253},{2,254},{3,255},{4,0},{5,1},{6,2},{7,3},{8,4},{9,5... | collective-permute-start | bytes 9224 | tf_op jit(solution)/shard_map/ppermute | solution.py:43
  22.7 1.5 %collective-permute-start = (bf16[2,256,512]{2,1,0:T(8,128)(2,1)S(1)}, bf16[2,256,512]{2,1,0:T(8,128)(2,1)S(1)}, u32[]{:S(2)}, u32[]{:S(2)}) collective-permute-start(bf16[2,256,512]{2,1,0:T(8,128)(2,1)S(1)} %get-tuple-element.23), channel_id=1, source_target_pairs={{0,4},{1,5},{2,6},{3,7},{4,8},{5,9},{6,10},{7,11},{8,12},{9,13},{1... | collective-permute-start | bytes 1572872 | tf_op jit(solution)/shard_map/ppermute | solution.py:43
  24.2 2.6 %shard_map.88 = (f32[3,512,512]{2,1,0:T(8,128)S(1)}, f32[256,512]{1,0:T(8,128)S(1)}) custom-call(f32[1,1,3,512,512]{4,3,2,1,0:T(8,128)S(1)} %copy-done.8, bf16[4,256,512]{2,1,0:T(8,128)(2,1)S(1)} %copy-done, bf16[4,256,512]{2,1,0:T(8,128)(2,1)S(1)} %copy-done.2, f32[3,1,256]{2,1,0:T(1,128)S(1)} %bitcast.18, bf16[3,256,512]{2,1,0:T(8,128)(2,1)S(1)} %copy-done.4, ...), custom_call_target="tpu_custom_call" | custom-call | flops 2415919104 | bytes 6034432 | tf_op jit(solution)/shard_map/pallas_call | solution.py:255
  26.8 7.3 %collective-permute-done.3.rates = f32[3,1,256]{2,1,0:T(1,128)S(1)} collective-permute-done((f32[3,1,256]{2,1,0:T(1,128)}, f32[3,1,256]{2,1,0:T(1,128)S(1)}, u32[]{:S(2)}, u32[]{:S(2)}) %collective-permute-start.3) | collective-permute-done | bytes 3104 | tf_op jit(solution)/shard_map/ppermute | solution.py:43
  34.0 1.8 %shard_map.89 = (bf16[576,512]{1,0:T(8,128)(2,1)S(1)}, bf16[480,512]{1,0:T(8,128)(2,1)S(1)}, bf16[480,512]{1,0:T(8,128)(2,1)S(1)}) custom-call(f32[3,512,512]{2,1,0:T(8,128)S(1)} %get-tuple-element.24.u, bf16[2,256,512]{2,1,0:T(8,128)(2,1)S(1)} %collective-permute-done.2.kv, f32[3,1,256]{2,1,0:T(1,128)S(1)} %collective-permute-done.3.rates), custom_call_target="tpu_custom_call" | custom-call | flops 1610612736 | bytes 3673088 | tf_op jit(solution)/shard_map/pallas_call | solution.py:255
  38.1 1.3 %collective-permute-start.12 = (bf16[480,512]{1,0:T(8,128)(2,1)S(1)}, bf16[480,512]{1,0:T(8,128)(2,1)S(1)}, u32[]{:S(2)}, u32[]{:S(2)}) collective-permute-start(bf16[480,512]{1,0:T(8,128)(2,1)S(1)} %get-tuple-element.36), channel_id=1, source_target_pairs={{0,8},{1,9},{2,10},{3,11},{4,12},{5,13},{6,14},{7,15},{8,16},{9,17... | collective-permute-start | bytes 1474568 | tf_op jit(solution)/shard_map/ppermute | solution.py:43
  39.5 1.4 %shard_map.90 = bf16[256,512]{1,0:T(8,128)(2,1)S(1)} custom-call(f32[3,512,512]{2,1,0:T(8,128)S(1)} %get-tuple-element.24.u, bf16[256,512]{1,0:T(8,128)(2,1)S(1)} %collective-permute-done.1.qn, bf16[256,512]{1,0:T(8,128)(2,1)S(1)} %collective-permute-done.4.qf, bf16[4,256,512]{2,1,0:T(8,128)(2,1)S(1)} %copy-done.1, bf16[4,256,512]{2,1,0:T(8,128)(2,1)S(1)} %copy-done.3, ...), custom_call_target="tpu_custom_call" | custom-call | flops 1342177280 | bytes 6293504 | tf_op jit(solution)/shard_map/pallas_call | solution.py:255
  40.8 5.3 %collective-permute-done.kvn = bf16[2,256,512]{2,1,0:T(8,128)(2,1)S(1)} collective-permute-done((bf16[2,256,512]{2,1,0:T(8,128)(2,1)S(1)}, bf16[2,256,512]{2,1,0:T(8,128)(2,1)S(1)}, u32[]{:S(2)}, u32[]{:S(2)}) %collective-permute-start) | collective-permute-done | bytes 524320 | tf_op jit(solution)/shard_map/ppermute | solution.py:43
  46.2 1.9 %collective-permute-start.5 = (bf16[2,256,512]{2,1,0:T(8,128)(2,1)S(1)}, bf16[2,256,512]{2,1,0:T(8,128)(2,1)S(1)}, u32[]{:S(2)}, u32[]{:S(2)}) collective-permute-start(bf16[2,256,512]{2,1,0:T(8,128)(2,1)S(1)} %collective-permute-done.kvn), channel_id=1, source_target_pairs={{0,64},{1,65},{2,66},{3,67},{64,128},{65,129},{66,130},{67,131},{1... | collective-permute-start | bytes 1572872 | tf_op jit(solution)/shard_map/ppermute | solution.py:43
  48.3 1.3 %collective-permute-start.15 = (bf16[480,512]{1,0:T(8,128)(2,1)S(1)}, bf16[480,512]{1,0:T(8,128)(2,1)S(1)}, u32[]{:S(2)}, u32[]{:S(2)}) collective-permute-start(bf16[480,512]{1,0:T(8,128)(2,1)S(1)} %get-tuple-element.38), channel_id=1, source_target_pairs={{0,8},{1,9},{2,10},{3,11},{4,12},{5,13},{6,14},{7,15},{8,16},{9,17... | collective-permute-start | bytes 1474568 | tf_op jit(solution)/shard_map/ppermute | solution.py:43
  50.9 22.1 %collective-permute-done.8.cm = bf16[256,512]{1,0:T(8,128)(2,1)S(1)} collective-permute-done((bf16[256,512]{1,0:T(8,128)(2,1)S(1)}, bf16[256,512]{1,0:T(8,128)(2,1)S(1)}, u32[]{:S(2)}, u32[]{:S(2)}) %collective-permute-start.8) | collective-permute-done | bytes 262176 | tf_op jit(solution)/shard_map/ppermute | solution.py:43
  75.1 6.9 %collective-permute-start.9 = (bf16[2,256,512]{2,1,0:T(8,128)(2,1)S(1)}, bf16[2,256,512]{2,1,0:T(8,128)(2,1)S(1)}, u32[]{:S(2)}, u32[]{:S(2)}) collective-permute-start(bf16[2,256,512]{2,1,0:T(8,128)(2,1)S(1)} %get-tuple-element.33), channel_id=1, source_target_pairs={{0,1},{1,0},{2,3},{3,2},{4,5},{5,4},{6,7},{7,6},{8,9},{9,8},{10,11... | collective-permute-start | bytes 1572872 | tf_op jit(solution)/shard_map/ppermute | solution.py:43
  82.0 1.4 %shard_map.91 = (bf16[2,256,512]{2,1,0:T(8,128)(2,1)S(1)}, bf16[256,512]{1,0:T(8,128)(2,1)S(1)}, bf16[256,512]{1,0:T(8,128)(2,1)S(1)}) custom-call(bf16[3,256,512]{2,1,0:T(8,128)(2,1)S(1)} %copy-done.4, bf16[2,256,512]{2,1,0:T(8,128)(2,1)S(1)} %collective-permute-done.kvn, bf16[2,256,512]{2,1,0:T(8,128)(2,1)S(1)} %collective-permute-done.5.kvf, ...), custom_call_target="tpu_custom_call" | custom-call | flops 1610612736 | bytes 6553600 | tf_op jit(solution)/shard_map/pallas_call | solution.py:255
  84.3 4.5 %collective-permute-done.11.a = bf16[576,512]{1,0:T(8,128)(2,1)S(1)} collective-permute-done((bf16[576,512]{1,0:T(8,128)(2,1)S(1)}, bf16[576,512]{1,0:T(8,128)(2,1)S(1)}, u32[]{:S(2)}, u32[]{:S(2)}) %collective-permute-start.11) | collective-permute-done | bytes 589856 | tf_op jit(solution)/shard_map/ppermute | solution.py:43
  88.8 4.7 %collective-permute-done.17.cf = bf16[480,512]{1,0:T(8,128)(2,1)S(1)} collective-permute-done((bf16[480,512]{1,0:T(8,128)(2,1)S(1)}, bf16[480,512]{1,0:T(8,128)(2,1)S(1)}, u32[]{:S(2)}, u32[]{:S(2)}) %collective-permute-start.17) | collective-permute-done | bytes 491552 | tf_op jit(solution)/shard_map/ppermute | solution.py:43
  93.5 1.4 %shard_map.95 = (bf16[2,256,512]{2,1,0:T(8,128)(2,1)S(1)}, bf16[256,512]{1,0:T(8,128)(2,1)S(1)}, bf16[256,512]{1,0:T(8,128)(2,1)S(1)}, bf16[1536,512]{1,0:T(8,128)(2,1)S(1)}) custom-call(bf16[576,512]{1,0:T(8,128)(2,1)S(1)} %collective-permute-done.11.a, bf16[480,512]{1,0:T(8,128)(2,1)S(1)} %collective-permute-done.12.bn, ...), custom_call_target="tpu_custom_call" | custom-call | flops 1879048192 | bytes 5965824 | tf_op jit(solution)/shard_map/pallas_call | solution.py:255
  94.9 9.3 %collective-permute-start.19 = (bf16[2,256,512]{2,1,0:T(8,128)(2,1)S(1)}, bf16[2,256,512]{2,1,0:T(8,128)(2,1)S(1)}, u32[]{:S(2)}, u32[]{:S(2)}) collective-permute-start(bf16[2,256,512]{2,1,0:T(8,128)(2,1)S(1)} %get-tuple-element.40), channel_id=1, source_target_pairs={{0,1},{1,0},{2,3},{3,2},{4,5},{5,4},{6,7},{7,6},{8,9},{9,8},{10,11... | collective-permute-start | bytes 1572872 | tf_op jit(solution)/shard_map/ppermute | solution.py:43
  104.3 7.1 %collective-permute-start.10 = (bf16[256,512]{1,0:T(8,128)(2,1)S(1)}, bf16[256,512]{1,0:T(8,128)(2,1)S(1)}, u32[]{:S(2)}, u32[]{:S(2)}) collective-permute-start(bf16[256,512]{1,0:T(8,128)(2,1)S(1)} %fusion.1), channel_id=1, source_target_pairs={{0,2},{1,3},{2,0},{3,1},{4,6},{5,7},{6,4},{7,5},{8,10},{9,11},{10,... | collective-permute-start | bytes 786440 | tf_op jit(solution)/shard_map/ppermute | solution.py:43
  111.7 1.5 %collective-permute-start.20 = (bf16[256,512]{1,0:T(8,128)(2,1)S(1)}, bf16[256,512]{1,0:T(8,128)(2,1)S(1)}, u32[]{:S(2)}, u32[]{:S(2)}) collective-permute-start(bf16[256,512]{1,0:T(8,128)(2,1)S(1)} %fusion), channel_id=1, source_target_pairs={{0,2},{1,3},{2,0},{3,1},{4,6},{5,7},{6,4},{7,5},{8,10},{9,11},{10,... | collective-permute-start | bytes 786440 | tf_op jit(solution)/shard_map/ppermute | solution.py:43
  113.2 3.4 %shard_map.97 = f32[1,1,3,512,512]{4,3,2,1,0:T(8,128)} custom-call(bf16[1536,512]{1,0:T(8,128)(2,1)S(1)} %get-tuple-element.43.m, bf16[4,256,512]{2,1,0:T(8,128)(2,1)S(1)} %copy-done.1, bf16[4,256,512]{2,1,0:T(8,128)(2,1)S(1)} %copy-done.3, f32[3,1,256]{2,1,0:T(1,128)S(1)} %bitcast.19), custom_call_target="tpu_custom_call" | custom-call | flops 1610612736 | bytes 3673088 | tf_op jit(solution)/shard_map/pallas_call | solution.py:255
  116.6 1.5 %collective-permute-done.10.other1 = bf16[256,512]{1,0:T(8,128)(2,1)S(1)} collective-permute-done((bf16[256,512]{1,0:T(8,128)(2,1)S(1)}, bf16[256,512]{1,0:T(8,128)(2,1)S(1)}, u32[]{:S(2)}, u32[]{:S(2)}) %collective-permute-start.10) | collective-permute-done | bytes 262176 | tf_op jit(solution)/shard_map/ppermute | solution.py:43
  118.1 5.6 %collective-permute-done.7.other0 = bf16[256,512]{1,0:T(8,128)(2,1)S(1)} collective-permute-done((bf16[256,512]{1,0:T(8,128)(2,1)S(1)}, bf16[256,512]{1,0:T(8,128)(2,1)S(1)}, u32[]{:S(2)}, u32[]{:S(2)}) %collective-permute-start.7) | collective-permute-done | bytes 262176 | tf_op jit(solution)/shard_map/ppermute | solution.py:43
  124.8 4.5 %collective-permute-done.20.other = bf16[256,512]{1,0:T(8,128)(2,1)S(1)} collective-permute-done((bf16[256,512]{1,0:T(8,128)(2,1)S(1)}, bf16[256,512]{1,0:T(8,128)(2,1)S(1)}, u32[]{:S(2)}, u32[]{:S(2)}) %collective-permute-start.20) | collective-permute-done | bytes 262176 | tf_op jit(solution)/shard_map/ppermute | solution.py:43
  (51 shorter events, 11.4 us)
Async XLA Ops:
  3.1 21.1 %copy-start.7 = (f32[512]{0:T(512)S(1)}, f32[512]{0:T(512)}, u32[]{:S(2)}) copy-start(f32[512]{0:T(512)} %param.11) | copy-start | bytes 6148
  3.1 21.1 %copy-start.8 = (f32[1,1,3,512,512]{4,3,2,1,0:T(8,128)S(1)}, f32[1,1,3,512,512]{4,3,2,1,0:T(8,128)}, u32[]{:S(2)}) copy-start(f32[1,1,3,512,512]{4,3,2,1,0:T(8,128)} %u.1) | copy-start | bytes 9437188
  3.2 30.9 %collective-permute-start.2 = (bf16[2,256,512]{2,1,0:T(8,128)(2,1)S(1)}, bf16[2,256,512]{2,1,0:T(8,128)(2,1)S(1)}, u32[]{:S(2)}, u32[]{:S(2)}) collective-permute-start(bf16[2,256,512]{2,1,0:T(8,128)(2,1)S(1)} %shard_map.86._), channel_id=1, source_target_pairs={{0,252},{1,253},{2,254},{3,255},{4,0},{5,1},{6,2},{7,3},{8,4},{9,5... | collective-permute-start | bytes 1572872 | tf_op jit(solution)/shard_map/ppermute | solution.py:43
  14.7 33.3 %collective-permute-start.18 = (bf16[2,256,512]{2,1,0:T(8,128)(2,1)S(1)}, bf16[2,256,512]{2,1,0:T(8,128)(2,1)S(1)}, u32[]{:S(2)}, u32[]{:S(2)}) collective-permute-start(bf16[2,256,512]{2,1,0:T(8,128)(2,1)S(1)} %shard_map.86._), channel_id=1, source_target_pairs={{0,4},{1,5},{2,6},{3,7},{4,8},{5,9},{6,10},{7,11},{8,12},{9,13},{1... | collective-permute-start | bytes 1572872 | tf_op jit(solution)/shard_map/ppermute | solution.py:43
  14.7 19.3 %collective-permute-start.3 = (f32[3,1,256]{2,1,0:T(1,128)}, f32[3,1,256]{2,1,0:T(1,128)S(1)}, u32[]{:S(2)}, u32[]{:S(2)}) collective-permute-start(f32[3,1,256]{2,1,0:T(1,128)} %bitcast.17), channel_id=1, source_target_pairs={{0,252},{1,253},{2,254},{3,255},{4,0},{5,1},{6,2},{7,3},{8,4},{9,5... | collective-permute-start | bytes 9224 | tf_op jit(solution)/shard_map/ppermute | solution.py:43
  22.6 13.2 %collective-permute-start.1 = (bf16[256,512]{1,0:T(8,128)(2,1)S(1)}, bf16[256,512]{1,0:T(8,128)(2,1)S(1)}, u32[]{:S(2)}, u32[]{:S(2)}) collective-permute-start(bf16[256,512]{1,0:T(8,128)(2,1)S(1)} %get-tuple-element.25), channel_id=1, source_target_pairs={{0,60},{1,61},{2,62},{3,63},{4,0},{5,1},{6,2},{7,3},{8,4},{9,5},{1... | collective-permute-start | bytes 786440 | tf_op jit(solution)/shard_map/ppermute | solution.py:43
  22.7 23.4 %collective-permute-start = (bf16[2,256,512]{2,1,0:T(8,128)(2,1)S(1)}, bf16[2,256,512]{2,1,0:T(8,128)(2,1)S(1)}, u32[]{:S(2)}, u32[]{:S(2)}) collective-permute-start(bf16[2,256,512]{2,1,0:T(8,128)(2,1)S(1)} %get-tuple-element.23), channel_id=1, source_target_pairs={{0,4},{1,5},{2,6},{3,7},{4,8},{5,9},{6,10},{7,11},{8,12},{9,13},{1... | collective-permute-start | bytes 1572872 | tf_op jit(solution)/shard_map/ppermute | solution.py:43
  35.9 2.2 %collective-permute-start.4 = (bf16[256,512]{1,0:T(8,128)(2,1)S(1)}, bf16[256,512]{1,0:T(8,128)(2,1)S(1)}, u32[]{:S(2)}, u32[]{:S(2)}) collective-permute-start(bf16[256,512]{1,0:T(8,128)(2,1)S(1)} %collective-permute-done.1.qn), channel_id=1, source_target_pairs={{60,252},{61,253},{62,254},{63,255},{124,60},{125,61},{126,62},{12... | collective-permute-start | bytes 786440 | tf_op jit(solution)/shard_map/ppermute | solution.py:43
  36.5 11.6 %collective-permute-start.13 = (bf16[480,512]{1,0:T(8,128)(2,1)S(1)}, bf16[480,512]{1,0:T(8,128)(2,1)S(1)}, u32[]{:S(2)}, u32[]{:S(2)}) collective-permute-start(bf16[480,512]{1,0:T(8,128)(2,1)S(1)} %get-tuple-element.36), channel_id=1, source_target_pairs={{56,8},{57,9},{58,10},{59,11},{60,12},{61,13},{62,14},{63,15},{120... | collective-permute-start | bytes 1474568 | tf_op jit(solution)/shard_map/ppermute | solution.py:43
  37.2 37.1 %copy-start.5 = (bf16[512,2048]{1,0:T(8,128)(2,1)S(1)}, bf16[512,2048]{1,0:T(8,128)(2,1)}, u32[]{:S(2)}) copy-start(bf16[512,2048]{1,0:T(8,128)(2,1)} %weight.5) | copy-start | bytes 6291460
  37.3 11.0 %collective-permute-start.16 = (bf16[480,512]{1,0:T(8,128)(2,1)S(1)}, bf16[480,512]{1,0:T(8,128)(2,1)S(1)}, u32[]{:S(2)}, u32[]{:S(2)}) collective-permute-start(bf16[480,512]{1,0:T(8,128)(2,1)S(1)} %get-tuple-element.38), channel_id=1, source_target_pairs={{56,40},{57,41},{58,42},{59,43},{60,44},{61,45},{62,46},{63,47},{1... | collective-permute-start | bytes 1474568 | tf_op jit(solution)/shard_map/ppermute | solution.py:43
  38.1 11.5 %collective-permute-start.12 = (bf16[480,512]{1,0:T(8,128)(2,1)S(1)}, bf16[480,512]{1,0:T(8,128)(2,1)S(1)}, u32[]{:S(2)}, u32[]{:S(2)}) collective-permute-start(bf16[480,512]{1,0:T(8,128)(2,1)S(1)} %get-tuple-element.36), channel_id=1, source_target_pairs={{0,8},{1,9},{2,10},{3,11},{4,12},{5,13},{6,14},{7,15},{8,16},{9,17... | collective-permute-start | bytes 1474568 | tf_op jit(solution)/shard_map/ppermute | solution.py:43
  46.2 29.0 %collective-permute-start.5 = (bf16[2,256,512]{2,1,0:T(8,128)(2,1)S(1)}, bf16[2,256,512]{2,1,0:T(8,128)(2,1)S(1)}, u32[]{:S(2)}, u32[]{:S(2)}) collective-permute-start(bf16[2,256,512]{2,1,0:T(8,128)(2,1)S(1)} %collective-permute-done.kvn), channel_id=1, source_target_pairs={{0,64},{1,65},{2,66},{3,67},{64,128},{65,129},{66,130},{67,131},{1... | collective-permute-start | bytes 1572872 | tf_op jit(solution)/shard_map/ppermute | solution.py:43
  48.1 25.0 %collective-permute-start.8 = (bf16[256,512]{1,0:T(8,128)(2,1)S(1)}, bf16[256,512]{1,0:T(8,128)(2,1)S(1)}, u32[]{:S(2)}, u32[]{:S(2)}) collective-permute-start(bf16[256,512]{1,0:T(8,128)(2,1)S(1)} %shard_map.90), channel_id=1, source_target_pairs={{0,4},{1,5},{2,6},{3,7},{4,8},{5,9},{6,10},{7,11},{8,12},{9,13},{1... | collective-permute-start | bytes 786440 | tf_op jit(solution)/shard_map/ppermute | solution.py:43
  48.2 40.6 %collective-permute-start.11 = (bf16[576,512]{1,0:T(8,128)(2,1)S(1)}, bf16[576,512]{1,0:T(8,128)(2,1)S(1)}, u32[]{:S(2)}, u32[]{:S(2)}) collective-permute-start(bf16[576,512]{1,0:T(8,128)(2,1)S(1)} %get-tuple-element.26), channel_id=1, source_target_pairs={{0,8},{1,9},{2,10},{3,11},{4,12},{5,13},{6,14},{7,15},{8,16},{9,17... | collective-permute-start | bytes 1769480 | tf_op jit(solution)/shard_map/ppermute | solution.py:43
  48.3 35.1 %collective-permute-start.15 = (bf16[480,512]{1,0:T(8,128)(2,1)S(1)}, bf16[480,512]{1,0:T(8,128)(2,1)S(1)}, u32[]{:S(2)}, u32[]{:S(2)}) collective-permute-start(bf16[480,512]{1,0:T(8,128)(2,1)S(1)} %get-tuple-element.38), channel_id=1, source_target_pairs={{0,8},{1,9},{2,10},{3,11},{4,12},{5,13},{6,14},{7,15},{8,16},{9,17... | collective-permute-start | bytes 1474568 | tf_op jit(solution)/shard_map/ppermute | solution.py:43
  49.6 39.2 %collective-permute-start.14 = (bf16[480,512]{1,0:T(8,128)(2,1)S(1)}, bf16[480,512]{1,0:T(8,128)(2,1)S(1)}, u32[]{:S(2)}, u32[]{:S(2)}) collective-permute-start(bf16[480,512]{1,0:T(8,128)(2,1)S(1)} %collective-permute-done.13), channel_id=1, source_target_pairs={{8,64},{9,65},{10,66},{11,67},{12,68},{13,69},{14,70},{15,71},{72,... | collective-permute-start | bytes 1474568 | tf_op jit(solution)/shard_map/ppermute | solution.py:43
  73.0 20.5 %collective-permute-start.17 = (bf16[480,512]{1,0:T(8,128)(2,1)S(1)}, bf16[480,512]{1,0:T(8,128)(2,1)S(1)}, u32[]{:S(2)}, u32[]{:S(2)}) collective-permute-start(bf16[480,512]{1,0:T(8,128)(2,1)S(1)} %collective-permute-done.16), channel_id=1, source_target_pairs={{40,64},{41,65},{42,66},{43,67},{44,68},{45,69},{46,70},{47,71},{1... | collective-permute-start | bytes 1474568 | tf_op jit(solution)/shard_map/ppermute | solution.py:43
  75.1 29.1 %collective-permute-start.9 = (bf16[2,256,512]{2,1,0:T(8,128)(2,1)S(1)}, bf16[2,256,512]{2,1,0:T(8,128)(2,1)S(1)}, u32[]{:S(2)}, u32[]{:S(2)}) collective-permute-start(bf16[2,256,512]{2,1,0:T(8,128)(2,1)S(1)} %get-tuple-element.33), channel_id=1, source_target_pairs={{0,1},{1,0},{2,3},{3,2},{4,5},{5,4},{6,7},{7,6},{8,9},{9,8},{10,11... | collective-permute-start | bytes 1572872 | tf_op jit(solution)/shard_map/ppermute | solution.py:43
  83.4 28.0 %collective-permute-start.6 = (bf16[2,256,512]{2,1,0:T(8,128)(2,1)S(1)}, bf16[2,256,512]{2,1,0:T(8,128)(2,1)S(1)}, u32[]{:S(2)}, u32[]{:S(2)}) collective-permute-start(bf16[2,256,512]{2,1,0:T(8,128)(2,1)S(1)} %get-tuple-element.30), channel_id=1, source_target_pairs={{0,1},{1,0},{2,3},{3,2},{4,5},{5,4},{6,7},{7,6},{8,9},{9,8},{10,11... | collective-permute-start | bytes 1572872 | tf_op jit(solution)/shard_map/ppermute | solution.py:43
  94.9 16.7 %collective-permute-start.19 = (bf16[2,256,512]{2,1,0:T(8,128)(2,1)S(1)}, bf16[2,256,512]{2,1,0:T(8,128)(2,1)S(1)}, u32[]{:S(2)}, u32[]{:S(2)}) collective-permute-start(bf16[2,256,512]{2,1,0:T(8,128)(2,1)S(1)} %get-tuple-element.40), channel_id=1, source_target_pairs={{0,1},{1,0},{2,3},{3,2},{4,5},{5,4},{6,7},{7,6},{8,9},{9,8},{10,11... | collective-permute-start | bytes 1572872 | tf_op jit(solution)/shard_map/ppermute | solution.py:43
  104.3 13.8 %collective-permute-start.10 = (bf16[256,512]{1,0:T(8,128)(2,1)S(1)}, bf16[256,512]{1,0:T(8,128)(2,1)S(1)}, u32[]{:S(2)}, u32[]{:S(2)}) collective-permute-start(bf16[256,512]{1,0:T(8,128)(2,1)S(1)} %fusion.1), channel_id=1, source_target_pairs={{0,2},{1,3},{2,0},{3,1},{4,6},{5,7},{6,4},{7,5},{8,10},{9,11},{10,... | collective-permute-start | bytes 786440 | tf_op jit(solution)/shard_map/ppermute | solution.py:43
  111.5 12.2 %collective-permute-start.7 = (bf16[256,512]{1,0:T(8,128)(2,1)S(1)}, bf16[256,512]{1,0:T(8,128)(2,1)S(1)}, u32[]{:S(2)}, u32[]{:S(2)}) collective-permute-start(bf16[256,512]{1,0:T(8,128)(2,1)S(1)} %fusion.2), channel_id=1, source_target_pairs={{0,2},{1,3},{2,0},{3,1},{4,6},{5,7},{6,4},{7,5},{8,10},{9,11},{10,... | collective-permute-start | bytes 786440 | tf_op jit(solution)/shard_map/ppermute | solution.py:43
  111.7 17.6 %collective-permute-start.20 = (bf16[256,512]{1,0:T(8,128)(2,1)S(1)}, bf16[256,512]{1,0:T(8,128)(2,1)S(1)}, u32[]{:S(2)}, u32[]{:S(2)}) collective-permute-start(bf16[256,512]{1,0:T(8,128)(2,1)S(1)} %fusion), channel_id=1, source_target_pairs={{0,2},{1,3},{2,0},{3,1},{4,6},{5,7},{6,4},{7,5},{8,10},{9,11},{10,... | collective-permute-start | bytes 786440 | tf_op jit(solution)/shard_map/ppermute | solution.py:43
  (6 other events, 68.4 us)

commit v3 on v2

--- a/solution.py
+++ b/solution.py
@@ -171,50 +171,48 @@
     normed[...] = fast_out(r, q[0], gain[...])
 
 
-def second_update(u, kv, rates, *pieces):
+def second_tick(u, kv, rates, qn, qf, kp, vp, held, gain, one, rest, third, relay, cm):
     r = [u[i].astype(BF) for i in range(3)]
 
     def store(i, cols, new):
         new = new.astype(BF)
-        start = 0
-        for piece, rows in zip(pieces, PIECES):
-            low, high = max(start, i * HD), min(start + rows, (i + 1) * HD)
-            if low < high:
-                piece[low - start : high - start, cols] = new[low - i * HD : high - i * HD]
-            start += rows
+        if i == 0:
+            one[:, cols] = new
+        else:
+            rest[(i - 1) * HD : i * HD, cols] = new
+        if i == 2:
+            third[:, cols] = new
 
     update(lambda i, cols: u[i, :, cols], r, kv[0], kv[1], column(rates[1]), store)
-
-
-def second_mix(u, qn, qf, kp, vp, kv, gain, cm):
+    first = lax.axis_index("seq") % 16 == 0
+    for i in range(2):
+        half = slice(i * ROWS, (i + 1) * ROWS)
+        relay[half] = jnp.where(first, held[i], rest[half])
     q = jnp.where(from_far(-1), qf[...], qn[...])
-    r = [u[i].astype(BF) for i in range(3)]
-    att = window(q, kp[0], kv[0], vp[0], kv[1])
-    cm[...] = (att + fast_out(r, q, gain[...])).astype(BF)
-
-
-def first_mix(q, kvn, kvf, k, v, normed, weight, give, own, far):
+    cm[...] = (window(q, kp[0], kv[0], vp[0], kv[1]) + fast_out(r, q, gain[...])).astype(BF)
+
+
+def first_mix(q, kv, k, v, normed, weight, give, own, far):
+    cm = (window(q[0], kv[0], k[0], kv[1], v[0]) + normed[...]).astype(BF)
+    project(cm, weight, give, own, far)
+
+
+def second_project(cm, weight, give, own, far):
+    project(cm[...], weight, give, own, far)
+
+
+def attend(q, kvn, kvf, k, v, att):
     late = from_far(1)
-    kp = jnp.where(late, kvf[0], kvn[0])
-    vp = jnp.where(late, kvf[1], kvn[1])
-    cm = (window(q[0], kp, k[0], vp, v[0]) + normed[...]).astype(BF)
-    project(cm, weight, give, own, far)
-
-
-def project_only(cm, weight, give, own, far):
-    project(cm[...], weight, give, own, far)
-
-
-def attend(q, kv, k, v, att):
-    att[...] = window(q[0], kv[0], k[0], kv[1], v[0])
-
-
-def third_mix(a, bn, bf, cn, cf, q, att, gain, weight, give, own, far, m):
+    kp = jnp.where(late, kvf[:ROWS], kvn[0])
+    vp = jnp.where(late, kvf[ROWS:], kvn[1])
+    att[...] = window(q[0], kp, k[0], vp, v[0])
+
+
+def third_mix(a, near, bf, cf, q, att, gain, weight, give, own, far, m):
     late = from_far(2)
-    one, two = PIECES[0], PIECES[0] + PIECES[1]
-    m[:one] = a[...]
-    m[one:two] = jnp.where(late, bf[...], bn[...])
-    m[two:] = jnp.where(late, cf[...], cn[...])
+    m[:HD] = a[...]
+    m[HD : 2 * HD] = jnp.where(late, bf[...], near[:HD])
+    m[2 * HD :] = jnp.where(late, cf[...], near[HD:])
     r = [m[i * HD : (i + 1) * HD] for i in range(3)]
     cm = (att[...] + fast_out(r, q[0], gain[...])).astype(BF)
     project(cm, weight, give, own, far)
@@ -237,7 +235,7 @@
     out[0] = (got[0].astype(F32) + own[...].astype(F32) + other[...].astype(F32)).astype(BF)
 
 
-PIECES = (576, 480, 480)
+LEAD = 40 * 10**9
 WHOLE = pl.BlockSpec(memory_space=pltpu.VMEM)
 HBM = pl.BlockSpec(memory_space=pl.ANY)
 
@@ -250,8 +248,7 @@
     return slab((1, ROWS, HD), t)
 
 
-def call(body, outs, args, matmuls=0, scratch=(), **more):
-    size = sum(a.size * a.dtype.itemsize for a, _ in args)
+def call(body, outs, args, matmuls=0, scratch=(), lead=0, **more):
     return pl.pallas_call(
         body,
         out_shape=[jax.ShapeDtypeStruct(s, d) for s, d, _ in outs],
@@ -260,7 +257,7 @@
         out_specs=[s for _, _, s in outs],
         scratch_shapes=list(scratch),
         compiler_params=pltpu.CompilerParams(vmem_limit_bytes=32 * 1024 * 1024),
-        cost_estimate=pl.CostEstimate(flops=matmuls * 2 * ROWS * HD * HD * 2, bytes_accessed=size, transcendentals=ROWS * HD),
+        cost_estimate=pl.CostEstimate(flops=1024 * matmuls + lead, bytes_accessed=1024, transcendentals=0),
         **more,
     )(*[a for a, _ in args])
 
@@ -268,13 +265,14 @@
 FLAT = ((ROWS, HD), BF, WHOLE)
 WIDE = ((ROWS, HD), F32, WHOLE)
 SUM = [((2, ROWS, HD), BF, WHOLE), FLAT, FLAT]
+HALF = ((HD, HD), BF, WHOLE)
 STATE = ((3, HD, HD), F32, WHOLE)
 
 
 def head_sum(give, own, far):
     spots = places()
     got = permute(give, [(s, s[:3] + (s[3] ^ 1,)) for s in spots])
-    pair = (got[1].astype(F32) + far.astype(F32)).astype(BF)
+    pair = (got[..., 1, :, :].astype(F32) + far.astype(F32)).astype(BF)
     other = permute(pair, [(s, s[:3] + (s[3] ^ 2,)) for s in spots])
     return (other, WHOLE), (got, WHOLE), (own, WHOLE)
 
@@ -300,14 +298,15 @@
     next_rates = send_direct(rates, -1)
     next_kv = send_direct(kv2, -1)
     q1n, q1_pairs = send_late(q1, -1)
-    kv2 = send_direct(kv2, 1)
-    kv0n, kv0_pairs = send_late(kv0, 1)
+    kv2n, kv2_pairs = send_late(kv2, 1)
+    q1f = permute(q1n, q1_pairs)
+    kv0 = send_direct(kv0, 1)
 
     state, normed0 = call(
         first_tick,
         [STATE, WIDE],
         (
-            (incoming, slab((1, 1, 3, HD, HD), 0)),
+            (after(incoming, next_rates, q1n), slab((1, 1, 3, HD, HD), 0)),
             (keys, rows_of(1)),
             (values, rows_of(1)),
             rate,
@@ -315,43 +314,49 @@
             gain,
         ),
         9,
-    )
-    a, b, c = call(
-        second_update,
-        [((n, HD), BF, WHOLE) for n in PIECES],
-        ((state, WHOLE), (next_kv, WHOLE), (next_rates, WHOLE)),
-        6,
-    )
-    b1, c1 = send_first(b, 2, 0, 1), send_first(c, 2, 0, -1)
-    a2, bn, cn = send_direct(a, 2), send_near(b, 2), send_near(c, 2)
-    q1f = permute(after(q1n, a), q1_pairs)
-    (cm1,) = call(
-        second_mix,
-        [FLAT],
-        ((state, WHOLE), (q1n, WHOLE), (q1f, WHOLE), (keys, rows_of(1)), (values, rows_of(1)), (next_kv, WHOLE), gain),
-        5,
-    )
-    kv0f = permute(after(kv0n, cm1), kv0_pairs)
-    bf, cf = send_far(after(b1, cm1), 2, 0, 1), send_far(after(c1, cm1), 2, 0, -1)
-    cm1 = send_direct(cm1, 1)
-    sum0 = call(
-        first_mix,
-        SUM,
-        ((queries, rows_of(0)), (kv0n, WHOLE), (kv0f, WHOLE), (keys, rows_of(1)), (values, rows_of(1)), (normed0, WHOLE), weight),
-        6,
-    )
-    (att2,) = call(attend, [WIDE], ((queries, rows_of(2)), (kv2, WHOLE), (keys, rows_of(3)), (values, rows_of(3))), 2)
-    sum0 = head_sum(*sum0)
-    sum1 = head_sum(*call(project_only, SUM, ((cm1, WHOLE), weight), 4))
+        lead=LEAD,
+    )
+    a, bc, c, b, cm1 = call(
+        second_tick,
+        [HALF, ((2 * HD, HD), BF, WHOLE), HALF, HALF, FLAT],
+        (
+            (state, WHOLE),
+            (next_kv, WHOLE),
+            (next_rates, WHOLE),
+            (q1n, WHOLE),
+            (q1f, WHOLE),
+            (keys, rows_of(1)),
+            (values, rows_of(1)),
+            (kv2n, WHOLE),
+            gain,
+        ),
+        11,
+    )
+    c1 = send_first(c, 2, 0, -1)
+    b1 = permute(b, [(s, moved(s, 0, 1)) for s in places() if crosses(s, 2)] + kv2_pairs)
+    a2, near = send_direct(a, 2), send_near(bc, 2)
+    bf, cf = send_far(b1, 2, 0, 1), send_far(c1, 2, 0, -1)
+    sum0 = head_sum(
+        *call(
+            first_mix,
+            SUM,
+            ((queries, rows_of(0)), (after(kv0, q1f), WHOLE), (keys, rows_of(1)), (values, rows_of(1)), (normed0, WHOLE), weight),
+            6,
+        )
+    )
+    cm1 = send_direct(after(cm1, b1, c1, sum0[0][0]), 1)
+    (att2,) = call(
+        attend, [WIDE], ((queries, rows_of(2)), (kv2n, WHOLE), (b1, WHOLE), (keys, rows_of(3)), (values, rows_of(3))), 2
+    )
+    sum1 = head_sum(*call(second_project, SUM, ((after(cm1, a2, att2), WHOLE), weight), 4))
     (mixed,) = call(first_two, [((3, ROWS, HD), BF, slab((3, ROWS, HD), 0))], sum0 + sum1)
     *sum2, m = call(
         third_mix,
         SUM + [((3 * HD, HD), BF, WHOLE)],
         (
             (a2, WHOLE),
-            (bn, WHOLE),
+            (near, WHOLE),
             (bf, WHOLE),
-            (cn, WHOLE),
             (cf, WHOLE),
             (queries, rows_of(2)),
             (att2, WHOLE),

time: 130 us -> 132 us (1.015)
  waiting for transfers between devices: 55.7 us -> 68.2 us
  starting transfers between devices: 55.5 us -> 43.3 us
    ppermute x21 -> x19, waiting for transfers between devices: 55.7 us -> 68.2 us  [permute(): return lax.ppermute(x, AXES, [(flat(a), flat(b)) for a, b in pairs])]
    ppermute x21 -> x19, starting transfers between devices: 55.5 us -> 43.3 us  [permute(): return lax.ppermute(x, AXES, [(flat(a), flat(b)) for a, b in pairs])]
    pallas_call x12 -> x11, Pallas kernels: 15.4 us -> 15.2 us  [call(): pl.pallas_call(body, out_shape=[jax.ShapeDtypeStruct(s, d) for s, d, _ in...]
  transfers between devices with their start and end apart: 21 -> 19, of which waited for: 8 -> 8; matrix products, arithmetic and copies ran while one was open for 0% -> 0% of each run, Pallas kernels for 11% -> 11%
where the time goes in v3:
time: 132 us; the launch traced here: 131 us
  waiting for transfers between devices  68.2 us (52%)
  starting transfers between devices  43.3 us (33%)
  Pallas kernels  15.2 us (12%)
  local copies, waits for them, and re-layouts  3.53 us (3%)
    ppermute x19, waiting for transfers between devices, permute(): return lax.ppermute(x, AXES, [(flat(a), flat(b)) for a, b in pairs])  68.2 us
    ppermute x19, starting transfers between devices, permute(): return lax.ppermute(x, AXES, [(flat(a), flat(b)) for a, b in pairs])  43.3 us
    pallas_call x11, Pallas kernels, call(): pl.pallas_call(body, out_shape=[jax.ShapeDtypeStruct(s, d) for s, d, _ in...  15.2 us
    unnamed x18, local copies, waits for them, and re-layouts  3.53 us
  transfers between devices with their start and end apart: 19, of which 8 were waited for; matrix products, arithmetic and copies ran while one was open for 0% of the time, Pallas kernels for 11%

profile of v3, /device:TPU:1, one launch (start us, length us, event | category | flops | bytes accessed | tf_op | source)
XLA Modules:
  0.0 131.4 jit_solution(525561272954743911)
XLA Ops:
  1.9 1.2 copy-done.2
  4.3 5.8 %collective-permute-start.1 = (bf16[256,512]{1,0:T(8,128)(2,1)S(1)}, bf16[256,512]{1,0:T(8,128)(2,1)S(1)}, u32[]{:S(2)}, u32[]{:S(2)}) collective-permute-start(bf16[256,512]{1,0:T(8,128)(2,1)S(1)} %get-tuple-element.26), channel_id=1, source_target_pairs={{0,60},{1,61},{2,62},{3,63},{4,0},{5,1},{6,2},{7,3},{8,4},{9,5},{1... | collective-permute-start | bytes 786440 | tf_op jit(solution)/shard_map/ppermute | solution.py:43
  10.1 6.3 %collective-permute-start.3 = (f32[3,1,256]{2,1,0:T(1,128)S(1)}, f32[3,1,256]{2,1,0:T(1,128)S(1)}, u32[]{:S(2)}, u32[]{:S(2)}) collective-permute-start(f32[3,1,256]{2,1,0:T(1,128)S(1)} %bitcast.20), channel_id=1, source_target_pairs={{0,252},{1,253},{2,254},{3,255},{4,0},{5,1},{6,2},{7,3},{8,4},{9,5... | collective-permute-start | bytes 9224 | tf_op jit(solution)/shard_map/ppermute | solution.py:43
  16.4 5.7 %collective-permute-start.6 = (bf16[2,256,512]{2,1,0:T(8,128)(2,1)S(1)}, bf16[2,256,512]{2,1,0:T(8,128)(2,1)S(1)}, u32[]{:S(2)}, u32[]{:S(2)}) collective-permute-start(bf16[2,256,512]{2,1,0:T(8,128)(2,1)S(1)} %shard_map.86._), channel_id=1, source_target_pairs={{0,252},{1,253},{2,254},{3,255},{4,0},{5,1},{6,2},{7,3},{8,4},{9,5... | collective-permute-start | bytes 1572872 | tf_op jit(solution)/shard_map/ppermute | solution.py:43
  22.8 2.6 %shard_map.88 = (f32[3,512,512]{2,1,0:T(8,128)S(1)}, f32[256,512]{1,0:T(8,128)S(1)}) custom-call(f32[1,1,3,512,512]{4,3,2,1,0:T(8,128)S(1)} %copy-done.8, bf16[4,256,512]{2,1,0:T(8,128)(2,1)S(1)} %copy-done, bf16[4,256,512]{2,1,0:T(8,128)(2,1)S(1)} %copy-done.2, f32[3,1,256]{2,1,0:T(1,128)S(1)} %bitcast.21, bf16[3,256,512]{2,1,0:T(8,128)(2,1)S(1)} %copy-done.5, ...), custom_call_target="tpu_custom_call" | custom-call | flops 40000008192 | bytes 1024 | tf_op jit(solution)/shard_map/pallas_call | solution.py:252
  25.4 17.3 %collective-permute-done.kv = bf16[2,256,512]{2,1,0:T(8,128)(2,1)S(1)} collective-permute-done((bf16[2,256,512]{2,1,0:T(8,128)(2,1)S(1)}, bf16[2,256,512]{2,1,0:T(8,128)(2,1)S(1)}, u32[]{:S(2)}, u32[]{:S(2)}) %collective-permute-start) | collective-permute-done | bytes 524320 | tf_op jit(solution)/shard_map/ppermute | solution.py:43
  42.7 1.3 %shard_map.89 = (bf16[2,256,512]{2,1,0:T(8,128)(2,1)S(1)}, bf16[256,512]{1,0:T(8,128)(2,1)S(1)}, bf16[256,512]{1,0:T(8,128)(2,1)S(1)}) custom-call(bf16[3,256,512]{2,1,0:T(8,128)(2,1)S(1)} %copy-done.5, bf16[2,256,512]{2,1,0:T(8,128)(2,1)S(1)} %collective-permute-done.kv, bf16[4,256,512]{2,1,0:T(8,128)(2,1)S(1)} %copy-done, ...), custom_call_target="tpu_custom_call" | custom-call | flops 6144 | bytes 1024 | tf_op jit(solution)/shard_map/pallas_call | solution.py:252
  44.1 11.3 %collective-permute-start.4 = (bf16[2,256,512]{2,1,0:T(8,128)(2,1)S(1)}, bf16[2,256,512]{2,1,0:T(8,128)(2,1)S(1)}, u32[]{:S(2)}, u32[]{:S(2)}) collective-permute-start(bf16[2,256,512]{2,1,0:T(8,128)(2,1)S(1)} %get-tuple-element.30), channel_id=1, source_target_pairs={{0,1},{1,0},{2,3},{3,2},{4,5},{5,4},{6,7},{7,6},{8,9},{9,8},{10,11... | collective-permute-start | bytes 1572872 | tf_op jit(solution)/shard_map/ppermute | solution.py:43
  55.4 3.0 %shard_map.90 = (bf16[512,512]{1,0:T(8,128)(2,1)S(1)}, bf16[1024,512]{1,0:T(8,128)(2,1)S(1)}, bf16[512,512]{1,0:T(8,128)(2,1)S(1)}, bf16[512,512]{1,0:T(8,128)(2,1)S(1)}, bf16[256,512]{1,0:T(8,128)(2,1)S(1)}) custom-call(f32[3,512,512]{2,1,0:T(8,128)S(1)} %get-tuple-element.33.u, bf16[2,256,512]{2,1,0:T(8,128)(2,1)S(1)} %collective-permute-done.6.kv, ...), custom_call_target="tpu_custom_call" | custom-call | flops 11264 | bytes 1024 | tf_op jit(solution)/shard_map/pallas_call | solution.py:252
  58.5 2.2 %collective-permute-start.8 = (bf16[512,512]{1,0:T(8,128)(2,1)S(1)}, bf16[512,512]{1,0:T(8,128)(2,1)S(1)}, u32[]{:S(2)}, u32[]{:S(2)}) collective-permute-start(bf16[512,512]{1,0:T(8,128)(2,1)S(1)} %get-tuple-element.35), channel_id=1, source_target_pairs={{56,8},{57,9},{58,10},{59,11},{60,12},{61,13},{62,14},{63,15},{120... | collective-permute-start | bytes 1572872 | tf_op jit(solution)/shard_map/ppermute | solution.py:43
  61.4 1.4 %collective-permute-start.14 = (bf16[1024,512]{1,0:T(8,128)(2,1)S(1)}, bf16[1024,512]{1,0:T(8,128)(2,1)S(1)}, u32[]{:S(2)}, u32[]{:S(2)}) collective-permute-start(bf16[1024,512]{1,0:T(8,128)(2,1)S(1)} %get-tuple-element.43), channel_id=1, source_target_pairs={{0,8},{1,9},{2,10},{3,11},{4,12},{5,13},{6,14},{7,15},{8,16},{9,17... | collective-permute-start | bytes 3145736 | tf_op jit(solution)/shard_map/ppermute | solution.py:43
  63.2 23.0 %collective-permute-done.8.kvf = bf16[512,512]{1,0:T(8,128)(2,1)S(1)} collective-permute-done((bf16[512,512]{1,0:T(8,128)(2,1)S(1)}, bf16[512,512]{1,0:T(8,128)(2,1)S(1)}, u32[]{:S(2)}, u32[]{:S(2)}) %collective-permute-start.8) | collective-permute-done | bytes 524320 | tf_op jit(solution)/shard_map/ppermute | solution.py:43
  86.2 1.5 %collective-permute-start.15 = (bf16[512,512]{1,0:T(8,128)(2,1)S(1)}, bf16[512,512]{1,0:T(8,128)(2,1)S(1)}, u32[]{:S(2)}, u32[]{:S(2)}) collective-permute-start(bf16[512,512]{1,0:T(8,128)(2,1)S(1)} %collective-permute-done.8.kvf), channel_id=1, source_target_pairs={{8,64},{9,65},{10,66},{11,67},{12,68},{13,69},{14,70},{15,71},{72,... | collective-permute-start | bytes 1572872 | tf_op jit(solution)/shard_map/ppermute | solution.py:43
  87.7 1.3 collective-permute-start.16
  89.8 6.7 %collective-permute-done.11.a = bf16[512,512]{1,0:T(8,128)(2,1)S(1)} collective-permute-done((bf16[512,512]{1,0:T(8,128)(2,1)S(1)}, bf16[512,512]{1,0:T(8,128)(2,1)S(1)}, u32[]{:S(2)}, u32[]{:S(2)}) %collective-permute-start.11) | collective-permute-done | bytes 524320 | tf_op jit(solution)/shard_map/ppermute | solution.py:43
  96.5 7.5 %collective-permute-done.10.cm = bf16[256,512]{1,0:T(8,128)(2,1)S(1)} collective-permute-done((bf16[256,512]{1,0:T(8,128)(2,1)S(1)}, bf16[256,512]{1,0:T(8,128)(2,1)S(1)}, u32[]{:S(2)}, u32[]{:S(2)}) %collective-permute-start.10) | collective-permute-done | bytes 262176 | tf_op jit(solution)/shard_map/ppermute | solution.py:43
  104.7 4.1 %collective-permute-start.12 = (bf16[2,256,512]{2,1,0:T(8,128)(2,1)S(1)}, bf16[2,256,512]{2,1,0:T(8,128)(2,1)S(1)}, u32[]{:S(2)}, u32[]{:S(2)}) collective-permute-start(bf16[2,256,512]{2,1,0:T(8,128)(2,1)S(1)} %get-tuple-element.40), channel_id=1, source_target_pairs={{0,1},{1,0},{2,3},{3,2},{4,5},{5,4},{6,7},{7,6},{8,9},{9,8},{10,11... | collective-permute-start | bytes 1572872 | tf_op jit(solution)/shard_map/ppermute | solution.py:43
  108.9 4.9 %collective-permute-done.16.cf = bf16[512,512]{1,0:T(8,128)(2,1)S(1)} collective-permute-done((bf16[512,512]{1,0:T(8,128)(2,1)S(1)}, bf16[512,512]{1,0:T(8,128)(2,1)S(1)}, u32[]{:S(2)}, u32[]{:S(2)}) %collective-permute-start.16) | collective-permute-done | bytes 524320 | tf_op jit(solution)/shard_map/ppermute | solution.py:43
  113.8 1.4 %shard_map.94 = (bf16[2,256,512]{2,1,0:T(8,128)(2,1)S(1)}, bf16[256,512]{1,0:T(8,128)(2,1)S(1)}, bf16[256,512]{1,0:T(8,128)(2,1)S(1)}, bf16[1536,512]{1,0:T(8,128)(2,1)S(1)}) custom-call(bf16[512,512]{1,0:T(8,128)(2,1)S(1)} %collective-permute-done.11.a, bf16[1024,512]{1,0:T(8,128)(2,1)S(1)} %collective-permute-done.14.near, ...), custom_call_target="tpu_custom_call" | custom-call | flops 7168 | bytes 1024 | tf_op jit(solution)/shard_map/pallas_call | solution.py:252
  115.2 1.7 %collective-permute-start.17 = (bf16[2,256,512]{2,1,0:T(8,128)(2,1)S(1)}, bf16[2,256,512]{2,1,0:T(8,128)(2,1)S(1)}, u32[]{:S(2)}, u32[]{:S(2)}) collective-permute-start(bf16[2,256,512]{2,1,0:T(8,128)(2,1)S(1)} %get-tuple-element.44), channel_id=1, source_target_pairs={{0,1},{1,0},{2,3},{3,2},{4,5},{5,4},{6,7},{7,6},{8,9},{9,8},{10,11... | collective-permute-start | bytes 1572872 | tf_op jit(solution)/shard_map/ppermute | solution.py:43
  117.1 1.4 %collective-permute-done.17.got = bf16[2,256,512]{2,1,0:T(8,128)(2,1)S(1)} collective-permute-done((bf16[2,256,512]{2,1,0:T(8,128)(2,1)S(1)}, bf16[2,256,512]{2,1,0:T(8,128)(2,1)S(1)}, u32[]{:S(2)}, u32[]{:S(2)}) %collective-permute-start.17) | collective-permute-done | bytes 524320 | tf_op jit(solution)/shard_map/ppermute | solution.py:43
  118.7 3.4 %shard_map.96 = f32[1,1,3,512,512]{4,3,2,1,0:T(8,128)} custom-call(bf16[1536,512]{1,0:T(8,128)(2,1)S(1)} %get-tuple-element.47.m, bf16[4,256,512]{2,1,0:T(8,128)(2,1)S(1)} %copy-done.1, bf16[4,256,512]{2,1,0:T(8,128)(2,1)S(1)} %copy-done.3, f32[3,1,256]{2,1,0:T(1,128)S(1)} %bitcast.22), custom_call_target="tpu_custom_call" | custom-call | flops 6144 | bytes 1024 | tf_op jit(solution)/shard_map/pallas_call | solution.py:252
  122.0 2.9 %collective-permute-done.13.other1 = bf16[256,512]{1,0:T(8,128)(2,1)S(1)} collective-permute-done((bf16[256,512]{1,0:T(8,128)(2,1)S(1)}, bf16[256,512]{1,0:T(8,128)(2,1)S(1)}, u32[]{:S(2)}, u32[]{:S(2)}) %collective-permute-start.13) | collective-permute-done | bytes 262176 | tf_op jit(solution)/shard_map/ppermute | solution.py:43
  126.0 4.5 %collective-permute-done.18.other = bf16[256,512]{1,0:T(8,128)(2,1)S(1)} collective-permute-done((bf16[256,512]{1,0:T(8,128)(2,1)S(1)}, bf16[256,512]{1,0:T(8,128)(2,1)S(1)}, u32[]{:S(2)}, u32[]{:S(2)}) %collective-permute-start.18) | collective-permute-done | bytes 262176 | tf_op jit(solution)/shard_map/ppermute | solution.py:43
  (46 shorter events, 8.1 us)
Async XLA Ops:
  3.1 19.7 %copy-start.6 = (f32[512]{0:T(512)S(1)}, f32[512]{0:T(512)}, u32[]{:S(2)}) copy-start(f32[512]{0:T(512)} %param.11) | copy-start | bytes 6148
  3.1 19.7 %copy-start.8 = (f32[1,1,3,512,512]{4,3,2,1,0:T(8,128)S(1)}, f32[1,1,3,512,512]{4,3,2,1,0:T(8,128)}, u32[]{:S(2)}) copy-start(f32[1,1,3,512,512]{4,3,2,1,0:T(8,128)} %u) | copy-start | bytes 9437188
  4.3 17.8 %collective-permute-start.1 = (bf16[256,512]{1,0:T(8,128)(2,1)S(1)}, bf16[256,512]{1,0:T(8,128)(2,1)S(1)}, u32[]{:S(2)}, u32[]{:S(2)}) collective-permute-start(bf16[256,512]{1,0:T(8,128)(2,1)S(1)} %get-tuple-element.26), channel_id=1, source_target_pairs={{0,60},{1,61},{2,62},{3,63},{4,0},{5,1},{6,2},{7,3},{8,4},{9,5},{1... | collective-permute-start | bytes 786440 | tf_op jit(solution)/shard_map/ppermute | solution.py:43
  10.1 12.0 %collective-permute-start.3 = (f32[3,1,256]{2,1,0:T(1,128)S(1)}, f32[3,1,256]{2,1,0:T(1,128)S(1)}, u32[]{:S(2)}, u32[]{:S(2)}) collective-permute-start(f32[3,1,256]{2,1,0:T(1,128)S(1)} %bitcast.20), channel_id=1, source_target_pairs={{0,252},{1,253},{2,254},{3,255},{4,0},{5,1},{6,2},{7,3},{8,4},{9,5... | collective-permute-start | bytes 9224 | tf_op jit(solution)/shard_map/ppermute | solution.py:43
  16.4 39.0 %collective-permute-start.7 = (bf16[2,256,512]{2,1,0:T(8,128)(2,1)S(1)}, bf16[2,256,512]{2,1,0:T(8,128)(2,1)S(1)}, u32[]{:S(2)}, u32[]{:S(2)}) collective-permute-start(bf16[2,256,512]{2,1,0:T(8,128)(2,1)S(1)} %shard_map.86._), channel_id=1, source_target_pairs={{0,4},{1,5},{2,6},{3,7},{4,8},{5,9},{6,10},{7,11},{8,12},{9,13},{1... | collective-permute-start | bytes 1572872 | tf_op jit(solution)/shard_map/ppermute | solution.py:43
  16.4 39.0 %collective-permute-start.6 = (bf16[2,256,512]{2,1,0:T(8,128)(2,1)S(1)}, bf16[2,256,512]{2,1,0:T(8,128)(2,1)S(1)}, u32[]{:S(2)}, u32[]{:S(2)}) collective-permute-start(bf16[2,256,512]{2,1,0:T(8,128)(2,1)S(1)} %shard_map.86._), channel_id=1, source_target_pairs={{0,252},{1,253},{2,254},{3,255},{4,0},{5,1},{6,2},{7,3},{8,4},{9,5... | collective-permute-start | bytes 1572872 | tf_op jit(solution)/shard_map/ppermute | solution.py:43
  22.1 20.6 %collective-permute-start = (bf16[2,256,512]{2,1,0:T(8,128)(2,1)S(1)}, bf16[2,256,512]{2,1,0:T(8,128)(2,1)S(1)}, u32[]{:S(2)}, u32[]{:S(2)}) collective-permute-start(bf16[2,256,512]{2,1,0:T(8,128)(2,1)S(1)} %get-tuple-element.25), channel_id=1, source_target_pairs={{0,4},{1,5},{2,6},{3,7},{4,8},{5,9},{6,10},{7,11},{8,12},{9,13},{1... | collective-permute-start | bytes 1572872 | tf_op jit(solution)/shard_map/ppermute | solution.py:43
  22.1 3.3 %collective-permute-start.2 = (bf16[256,512]{1,0:T(8,128)(2,1)S(1)}, bf16[256,512]{1,0:T(8,128)(2,1)S(1)}, u32[]{:S(2)}, u32[]{:S(2)}) collective-permute-start(bf16[256,512]{1,0:T(8,128)(2,1)S(1)} %collective-permute-done.1.qn), channel_id=1, source_target_pairs={{60,252},{61,253},{62,254},{63,255},{124,60},{125,61},{126,62},{12... | collective-permute-start | bytes 786440 | tf_op jit(solution)/shard_map/ppermute | solution.py:43
  22.8 19.9 %copy-start.4 = (bf16[512,2048]{1,0:T(8,128)(2,1)S(1)}, bf16[512,2048]{1,0:T(8,128)(2,1)}, u32[]{:S(2)}) copy-start(bf16[512,2048]{1,0:T(8,128)(2,1)} %weight.5) | copy-start | bytes 6291460
  44.1 18.7 %collective-permute-start.4 = (bf16[2,256,512]{2,1,0:T(8,128)(2,1)S(1)}, bf16[2,256,512]{2,1,0:T(8,128)(2,1)S(1)}, u32[]{:S(2)}, u32[]{:S(2)}) collective-permute-start(bf16[2,256,512]{2,1,0:T(8,128)(2,1)S(1)} %get-tuple-element.30), channel_id=1, source_target_pairs={{0,1},{1,0},{2,3},{3,2},{4,5},{5,4},{6,7},{7,6},{8,9},{9,8},{10,11... | collective-permute-start | bytes 1572872 | tf_op jit(solution)/shard_map/ppermute | solution.py:43
  58.5 27.7 %collective-permute-start.8 = (bf16[512,512]{1,0:T(8,128)(2,1)S(1)}, bf16[512,512]{1,0:T(8,128)(2,1)S(1)}, u32[]{:S(2)}, u32[]{:S(2)}) collective-permute-start(bf16[512,512]{1,0:T(8,128)(2,1)S(1)} %get-tuple-element.35), channel_id=1, source_target_pairs={{56,8},{57,9},{58,10},{59,11},{60,12},{61,13},{62,14},{63,15},{120... | collective-permute-start | bytes 1572872 | tf_op jit(solution)/shard_map/ppermute | solution.py:43
  60.7 27.0 %collective-permute-start.9 = (bf16[512,512]{1,0:T(8,128)(2,1)S(1)}, bf16[512,512]{1,0:T(8,128)(2,1)S(1)}, u32[]{:S(2)}, u32[]{:S(2)}) collective-permute-start(bf16[512,512]{1,0:T(8,128)(2,1)S(1)} %get-tuple-element.36), channel_id=1, source_target_pairs={{56,40},{57,41},{58,42},{59,43},{60,44},{61,45},{62,46},{63,47},{1... | collective-permute-start | bytes 1572872 | tf_op jit(solution)/shard_map/ppermute | solution.py:43
  61.4 52.4 %collective-permute-start.14 = (bf16[1024,512]{1,0:T(8,128)(2,1)S(1)}, bf16[1024,512]{1,0:T(8,128)(2,1)S(1)}, u32[]{:S(2)}, u32[]{:S(2)}) collective-permute-start(bf16[1024,512]{1,0:T(8,128)(2,1)S(1)} %get-tuple-element.43), channel_id=1, source_target_pairs={{0,8},{1,9},{2,10},{3,11},{4,12},{5,13},{6,14},{7,15},{8,16},{9,17... | collective-permute-start | bytes 3145736 | tf_op jit(solution)/shard_map/ppermute | solution.py:43
  62.8 26.2 %collective-permute-start.5 = (bf16[256,512]{1,0:T(8,128)(2,1)S(1)}, bf16[256,512]{1,0:T(8,128)(2,1)S(1)}, u32[]{:S(2)}, u32[]{:S(2)}) collective-permute-start(bf16[256,512]{1,0:T(8,128)(2,1)S(1)} %fusion.2), channel_id=1, source_target_pairs={{0,2},{1,3},{2,0},{3,1},{4,6},{5,7},{6,4},{7,5},{8,10},{9,11},{10,... | collective-permute-start | bytes 786440 | tf_op jit(solution)/shard_map/ppermute | solution.py:43
  63.2 33.3 %collective-permute-start.11 = (bf16[512,512]{1,0:T(8,128)(2,1)S(1)}, bf16[512,512]{1,0:T(8,128)(2,1)S(1)}, u32[]{:S(2)}, u32[]{:S(2)}) collective-permute-start(bf16[512,512]{1,0:T(8,128)(2,1)S(1)} %get-tuple-element.38), channel_id=1, source_target_pairs={{0,8},{1,9},{2,10},{3,11},{4,12},{5,13},{6,14},{7,15},{8,16},{9,17... | collective-permute-start | bytes 1572872 | tf_op jit(solution)/shard_map/ppermute | solution.py:43
  86.2 22.7 %collective-permute-start.15 = (bf16[512,512]{1,0:T(8,128)(2,1)S(1)}, bf16[512,512]{1,0:T(8,128)(2,1)S(1)}, u32[]{:S(2)}, u32[]{:S(2)}) collective-permute-start(bf16[512,512]{1,0:T(8,128)(2,1)S(1)} %collective-permute-done.8.kvf), channel_id=1, source_target_pairs={{8,64},{9,65},{10,66},{11,67},{12,68},{13,69},{14,70},{15,71},{72,... | collective-permute-start | bytes 1572872 | tf_op jit(solution)/shard_map/ppermute | solution.py:43
  87.7 26.1 %collective-permute-start.16 = (bf16[512,512]{1,0:T(8,128)(2,1)S(1)}, bf16[512,512]{1,0:T(8,128)(2,1)S(1)}, u32[]{:S(2)}, u32[]{:S(2)}) collective-permute-start(bf16[512,512]{1,0:T(8,128)(2,1)S(1)} %collective-permute-done.9), channel_id=1, source_target_pairs={{40,64},{41,65},{42,66},{43,67},{44,68},{45,69},{46,70},{47,71},{1... | collective-permute-start | bytes 1572872 | tf_op jit(solution)/shard_map/ppermute | solution.py:43
  89.0 15.0 %collective-permute-start.10 = (bf16[256,512]{1,0:T(8,128)(2,1)S(1)}, bf16[256,512]{1,0:T(8,128)(2,1)S(1)}, u32[]{:S(2)}, u32[]{:S(2)}) collective-permute-start(bf16[256,512]{1,0:T(8,128)(2,1)S(1)} %get-tuple-element.37), channel_id=1, source_target_pairs={{0,4},{1,5},{2,6},{3,7},{4,8},{5,9},{6,10},{7,11},{8,12},{9,13},{1... | collective-permute-start | bytes 786440 | tf_op jit(solution)/shard_map/ppermute | solution.py:43
  104.7 14.0 %copy-start.1 = (bf16[4,256,512]{2,1,0:T(8,128)(2,1)S(1)}, bf16[4,256,512]{2,1,0:T(8,128)(2,1)}, u32[]{:S(2)}) copy-start(bf16[4,256,512]{2,1,0:T(8,128)(2,1)} %k.7) | copy-start | bytes 3145732
  104.7 14.0 %copy-start.3 = (bf16[4,256,512]{2,1,0:T(8,128)(2,1)S(1)}, bf16[4,256,512]{2,1,0:T(8,128)(2,1)}, u32[]{:S(2)}) copy-start(bf16[4,256,512]{2,1,0:T(8,128)(2,1)} %v.7) | copy-start | bytes 3145732
  104.7 12.2 %collective-permute-start.12 = (bf16[2,256,512]{2,1,0:T(8,128)(2,1)S(1)}, bf16[2,256,512]{2,1,0:T(8,128)(2,1)S(1)}, u32[]{:S(2)}, u32[]{:S(2)}) collective-permute-start(bf16[2,256,512]{2,1,0:T(8,128)(2,1)S(1)} %get-tuple-element.40), channel_id=1, source_target_pairs={{0,1},{1,0},{2,3},{3,2},{4,5},{5,4},{6,7},{7,6},{8,9},{9,8},{10,11... | collective-permute-start | bytes 1572872 | tf_op jit(solution)/shard_map/ppermute | solution.py:43
  115.2 3.2 %collective-permute-start.17 = (bf16[2,256,512]{2,1,0:T(8,128)(2,1)S(1)}, bf16[2,256,512]{2,1,0:T(8,128)(2,1)S(1)}, u32[]{:S(2)}, u32[]{:S(2)}) collective-permute-start(bf16[2,256,512]{2,1,0:T(8,128)(2,1)S(1)} %get-tuple-element.44), channel_id=1, source_target_pairs={{0,1},{1,0},{2,3},{3,2},{4,5},{5,4},{6,7},{7,6},{8,9},{9,8},{10,11... | collective-permute-start | bytes 1572872 | tf_op jit(solution)/shard_map/ppermute | solution.py:43
  117.0 8.0 %collective-permute-start.13 = (bf16[256,512]{1,0:T(8,128)(2,1)S(1)}, bf16[256,512]{1,0:T(8,128)(2,1)S(1)}, u32[]{:S(2)}, u32[]{:S(2)}) collective-permute-start(bf16[256,512]{1,0:T(8,128)(2,1)S(1)} %fusion.1), channel_id=1, source_target_pairs={{0,2},{1,3},{2,0},{3,1},{4,6},{5,7},{6,4},{7,5},{8,10},{9,11},{10,... | collective-permute-start | bytes 786440 | tf_op jit(solution)/shard_map/ppermute | solution.py:43
  118.5 12.1 %collective-permute-start.18 = (bf16[256,512]{1,0:T(8,128)(2,1)S(1)}, bf16[256,512]{1,0:T(8,128)(2,1)S(1)}, u32[]{:S(2)}, u32[]{:S(2)}) collective-permute-start(bf16[256,512]{1,0:T(8,128)(2,1)S(1)} %fusion), channel_id=1, source_target_pairs={{0,2},{1,3},{2,0},{3,1},{4,6},{5,7},{6,4},{7,5},{8,10},{9,11},{10,... | collective-permute-start | bytes 786440 | tf_op jit(solution)/shard_map/ppermute | solution.py:43
  (4 other events, 10.6 us)

commit v4 on v3

--- a/solution.py
+++ b/solution.py
@@ -171,7 +171,7 @@
     normed[...] = fast_out(r, q[0], gain[...])
 
 
-def second_tick(u, kv, rates, qn, qf, kp, vp, held, gain, one, rest, third, relay, cm):
+def second_tick(u, kv, rates, qn, qf, kp, vp, gain, one, rest, second, third, cm):
     r = [u[i].astype(BF) for i in range(3)]
 
     def store(i, cols, new):
@@ -180,31 +180,26 @@
             one[:, cols] = new
         else:
             rest[(i - 1) * HD : i * HD, cols] = new
-        if i == 2:
-            third[:, cols] = new
+            (second, third)[i - 1][:, cols] = new
 
     update(lambda i, cols: u[i, :, cols], r, kv[0], kv[1], column(rates[1]), store)
-    first = lax.axis_index("seq") % 16 == 0
-    for i in range(2):
-        half = slice(i * ROWS, (i + 1) * ROWS)
-        relay[half] = jnp.where(first, held[i], rest[half])
     q = jnp.where(from_far(-1), qf[...], qn[...])
     cm[...] = (window(q, kp[0], kv[0], vp[0], kv[1]) + fast_out(r, q, gain[...])).astype(BF)
 
 
-def first_mix(q, kv, k, v, normed, weight, give, own, far):
-    cm = (window(q[0], kv[0], k[0], kv[1], v[0]) + normed[...]).astype(BF)
-    project(cm, weight, give, own, far)
-
-
-def second_project(cm, weight, give, own, far):
-    project(cm[...], weight, give, own, far)
+def first_mix(q, kv, k, v, normed, cm):
+    cm[...] = (window(q[0], kv[0], k[0], kv[1], v[0]) + normed[...]).astype(BF)
+
+
+def project_two(cm0, cm1, weight, give, own, far):
+    project(cm0[...], weight, give.at[0], own.at[0], far.at[0])
+    project(cm1[...], weight, give.at[1], own.at[1], far.at[1])
 
 
 def attend(q, kvn, kvf, k, v, att):
     late = from_far(1)
-    kp = jnp.where(late, kvf[:ROWS], kvn[0])
-    vp = jnp.where(late, kvf[ROWS:], kvn[1])
+    kp = jnp.where(late, kvf[0], kvn[0])
+    vp = jnp.where(late, kvf[1], kvn[1])
     att[...] = window(q[0], kp, k[0], vp, v[0])
 
 
@@ -226,9 +221,9 @@
     update(lambda i, cols: m[i * HD : (i + 1) * HD, cols].astype(F32), r, k[0], v[0], column(rates[2]), store)
 
 
-def first_two(other0, got0, own0, other1, got1, own1, out):
-    out[0] = (got0[0].astype(F32) + own0[...].astype(F32) + other0[...].astype(F32)).astype(BF)
-    out[1] = (got1[0].astype(F32) + own1[...].astype(F32) + other1[...].astype(F32)).astype(BF)
+def first_two(other, got, own, out):
+    for t in range(2):
+        out[t] = (got[t, 0].astype(F32) + own[t].astype(F32) + other[t].astype(F32)).astype(BF)
 
 
 def last_one(_, other, got, own, out):
@@ -265,6 +260,7 @@
 FLAT = ((ROWS, HD), BF, WHOLE)
 WIDE = ((ROWS, HD), F32, WHOLE)
 SUM = [((2, ROWS, HD), BF, WHOLE), FLAT, FLAT]
+SUM_TWO = [((2, 2, ROWS, HD), BF, WHOLE), ((2, ROWS, HD), BF, WHOLE), ((2, ROWS, HD), BF, WHOLE)]
 HALF = ((HD, HD), BF, WHOLE)
 STATE = ((3, HD, HD), F32, WHOLE)
 
@@ -300,6 +296,7 @@
     q1n, q1_pairs = send_late(q1, -1)
     kv2n, kv2_pairs = send_late(kv2, 1)
     q1f = permute(q1n, q1_pairs)
+    kv2f = permute(kv2n, kv2_pairs)
     kv0 = send_direct(kv0, 1)
 
     state, normed0 = call(
@@ -316,7 +313,7 @@
         9,
         lead=LEAD,
     )
-    a, bc, c, b, cm1 = call(
+    a, bc, b, c, cm1 = call(
         second_tick,
         [HALF, ((2 * HD, HD), BF, WHOLE), HALF, HALF, FLAT],
         (
@@ -327,29 +324,27 @@
             (q1f, WHOLE),
             (keys, rows_of(1)),
             (values, rows_of(1)),
-            (kv2n, WHOLE),
             gain,
         ),
         11,
+        lead=LEAD,
     )
     c1 = send_first(c, 2, 0, -1)
-    b1 = permute(b, [(s, moved(s, 0, 1)) for s in places() if crosses(s, 2)] + kv2_pairs)
+    b1 = send_first(b, 2, 0, 1)
     a2, near = send_direct(a, 2), send_near(bc, 2)
     bf, cf = send_far(b1, 2, 0, 1), send_far(c1, 2, 0, -1)
-    sum0 = head_sum(
-        *call(
-            first_mix,
-            SUM,
-            ((queries, rows_of(0)), (after(kv0, q1f), WHOLE), (keys, rows_of(1)), (values, rows_of(1)), (normed0, WHOLE), weight),
-            6,
-        )
-    )
-    cm1 = send_direct(after(cm1, b1, c1, sum0[0][0]), 1)
+    (cm0,) = call(
+        first_mix,
+        [FLAT],
+        ((queries, rows_of(0)), (kv0, WHOLE), (keys, rows_of(1)), (values, rows_of(1)), (normed0, WHOLE)),
+        2,
+    )
+    cm1 = send_direct(after(cm1, b1, c1), 1)
     (att2,) = call(
-        attend, [WIDE], ((queries, rows_of(2)), (kv2n, WHOLE), (b1, WHOLE), (keys, rows_of(3)), (values, rows_of(3))), 2
-    )
-    sum1 = head_sum(*call(second_project, SUM, ((after(cm1, a2, att2), WHOLE), weight), 4))
-    (mixed,) = call(first_two, [((3, ROWS, HD), BF, slab((3, ROWS, HD), 0))], sum0 + sum1)
+        attend, [WIDE], ((queries, rows_of(2)), (kv2n, WHOLE), (kv2f, WHOLE), (keys, rows_of(3)), (values, rows_of(3))), 2
+    )
+    two = head_sum(*call(project_two, SUM_TWO, ((after(cm0, att2), WHOLE), (cm1, WHOLE), weight), 8))
+    (mixed,) = call(first_two, [((3, ROWS, HD), BF, slab((3, ROWS, HD), 0))], two)
     *sum2, m = call(
         third_mix,
         SUM + [((3 * HD, HD), BF, WHOLE)],
@@ -364,6 +359,7 @@
             weight,
         ),
         7,
+        lead=LEAD,
     )
     sum2 = head_sum(*sum2)
     (outgoing,) = call(

time: 132 us -> 122 us (0.924)
  waiting for transfers between devices: 68.2 us -> 57.8 us
    ppermute x19 -> x18, waiting for transfers between devices: 68.2 us -> 57.8 us  [permute(): return lax.ppermute(x, AXES, [(flat(a), flat(b)) for a, b in pairs])]
    ppermute x19 -> x18, starting transfers between devices: 43.3 us -> 44.4 us  [permute(): return lax.ppermute(x, AXES, [(flat(a), flat(b)) for a, b in pairs])]
  transfers between devices with their start and end apart: 19 -> 18, of which waited for: 8 -> 7; matrix products, arithmetic and copies ran while one was open for 0% -> 0% of each run, Pallas kernels for 11% -> 12%
where the time goes in v4:
time: 122 us
  waiting for transfers between devices  57.8 us (47%)
  starting transfers between devices  44.4 us (36%)
  Pallas kernels  15.1 us (12%)
  local copies, waits for them, and re-layouts  3.53 us (3%)
    ppermute x18, waiting for transfers between devices, permute(): return lax.ppermute(x, AXES, [(flat(a), flat(b)) for a, b in pairs])  57.8 us
    ppermute x18, starting transfers between devices, permute(): return lax.ppermute(x, AXES, [(flat(a), flat(b)) for a, b in pairs])  44.4 us
    pallas_call x11, Pallas kernels, call(): pl.pallas_call(body, out_shape=[jax.ShapeDtypeStruct(s, d) for s, d, _ in...  15.1 us
    unnamed x18, local copies, waits for them, and re-layouts  3.53 us
  transfers between devices with their start and end apart: 18, of which 7 were waited for; matrix products, arithmetic and copies ran while one was open for 0% of the time, Pallas kernels for 12%

profile of v4, /device:TPU:1, one launch (start us, length us, event | category | flops | bytes accessed | tf_op | source)
XLA Modules:
  0.0 121.9 jit_solution(7854569821706779005)
XLA Ops:
  0.6 1.2 copy-done
  1.9 1.2 %copy-done.2 = bf16[4,256,512]{2,1,0:T(8,128)(2,1)S(1)} copy-done((bf16[4,256,512]{2,1,0:T(8,128)(2,1)S(1)}, bf16[4,256,512]{2,1,0:T(8,128)(2,1)}, u32[]{:S(2)}) %copy-start.2) | copy-done | bytes 1048600
  4.3 5.8 %collective-permute-start.2 = (bf16[256,512]{1,0:T(8,128)(2,1)S(1)}, bf16[256,512]{1,0:T(8,128)(2,1)S(1)}, u32[]{:S(2)}, u32[]{:S(2)}) collective-permute-start(bf16[256,512]{1,0:T(8,128)(2,1)S(1)} %get-tuple-element.22), channel_id=1, source_target_pairs={{0,60},{1,61},{2,62},{3,63},{4,0},{5,1},{6,2},{7,3},{8,4},{9,5},{1... | collective-permute-start | bytes 786440 | tf_op jit(solution)/shard_map/ppermute | solution.py:43
  10.1 6.3 %collective-permute-start.1 = (f32[3,1,256]{2,1,0:T(1,128)S(1)}, f32[3,1,256]{2,1,0:T(1,128)S(1)}, u32[]{:S(2)}, u32[]{:S(2)}) collective-permute-start(f32[3,1,256]{2,1,0:T(1,128)S(1)} %bitcast.12), channel_id=1, source_target_pairs={{0,252},{1,253},{2,254},{3,255},{4,0},{5,1},{6,2},{7,3},{8,4},{9,5... | collective-permute-start | bytes 9224 | tf_op jit(solution)/shard_map/ppermute | solution.py:43
  16.7 1.2 collective-permute-start.3
  18.6 2.5 %shard_map.88 = (f32[3,512,512]{2,1,0:T(8,128)S(1)}, f32[256,512]{1,0:T(8,128)S(1)}) custom-call(f32[1,1,3,512,512]{4,3,2,1,0:T(8,128)S(1)} %copy-done.7, bf16[4,256,512]{2,1,0:T(8,128)(2,1)S(1)} %copy-done, bf16[4,256,512]{2,1,0:T(8,128)(2,1)S(1)} %copy-done.2, f32[3,1,256]{2,1,0:T(1,128)S(1)} %bitcast.13, bf16[3,256,512]{2,1,0:T(8,128)(2,1)S(1)} %copy-done.4, ...), custom_call_target="tpu_custom_call" | custom-call | flops 40000008192 | bytes 1024 | tf_op jit(solution)/shard_map/pallas_call | solution.py:247
  21.2 14.5 %collective-permute-done.5.kv = bf16[2,256,512]{2,1,0:T(8,128)(2,1)S(1)} collective-permute-done((bf16[2,256,512]{2,1,0:T(8,128)(2,1)S(1)}, bf16[2,256,512]{2,1,0:T(8,128)(2,1)S(1)}, u32[]{:S(2)}, u32[]{:S(2)}) %collective-permute-start.5) | collective-permute-done | bytes 524320 | tf_op jit(solution)/shard_map/ppermute | solution.py:43
  35.7 3.0 %shard_map.91 = (bf16[512,512]{1,0:T(8,128)(2,1)S(1)}, bf16[1024,512]{1,0:T(8,128)(2,1)S(1)}, bf16[512,512]{1,0:T(8,128)(2,1)S(1)}, bf16[512,512]{1,0:T(8,128)(2,1)S(1)}, bf16[256,512]{1,0:T(8,128)(2,1)S(1)}) custom-call(f32[3,512,512]{2,1,0:T(8,128)S(1)} %get-tuple-element.26.u, bf16[2,256,512]{2,1,0:T(8,128)(2,1)S(1)} %collective-permute-done.5.kv, ...), custom_call_target="tpu_custom_call" | custom-call | flops 40000012288 | bytes 1024 | tf_op jit(solution)/shard_map/pallas_call | solution.py:247
  40.1 1.4 %collective-permute-start.13 = (bf16[1024,512]{1,0:T(8,128)(2,1)S(1)}, bf16[1024,512]{1,0:T(8,128)(2,1)S(1)}, u32[]{:S(2)}, u32[]{:S(2)}) collective-permute-start(bf16[1024,512]{1,0:T(8,128)(2,1)S(1)} %get-tuple-element.35), channel_id=1, source_target_pairs={{0,8},{1,9},{2,10},{3,11},{4,12},{5,13},{6,14},{7,15},{8,16},{9,17... | collective-permute-start | bytes 3145736 | tf_op jit(solution)/shard_map/ppermute | solution.py:43
  41.5 1.6 %collective-permute-done.3.kvn = bf16[2,256,512]{2,1,0:T(8,128)(2,1)S(1)} collective-permute-done((bf16[2,256,512]{2,1,0:T(8,128)(2,1)S(1)}, bf16[2,256,512]{2,1,0:T(8,128)(2,1)S(1)}, u32[]{:S(2)}, u32[]{:S(2)}) %collective-permute-start.3) | collective-permute-done | bytes 524320 | tf_op jit(solution)/shard_map/ppermute | solution.py:43
  43.0 1.9 %collective-permute-start.4 = (bf16[2,256,512]{2,1,0:T(8,128)(2,1)S(1)}, bf16[2,256,512]{2,1,0:T(8,128)(2,1)S(1)}, u32[]{:S(2)}, u32[]{:S(2)}) collective-permute-start(bf16[2,256,512]{2,1,0:T(8,128)(2,1)S(1)} %collective-permute-done.3.kvn), channel_id=1, source_target_pairs={{0,64},{1,65},{2,66},{3,67},{64,128},{65,129},{66,130},{67,131},{1... | collective-permute-start | bytes 1572872 | tf_op jit(solution)/shard_map/ppermute | solution.py:43
  45.1 1.3 %collective-permute-start.14 = (bf16[512,512]{1,0:T(8,128)(2,1)S(1)}, bf16[512,512]{1,0:T(8,128)(2,1)S(1)}, u32[]{:S(2)}, u32[]{:S(2)}) collective-permute-start(bf16[512,512]{1,0:T(8,128)(2,1)S(1)} %collective-permute-done.7), channel_id=1, source_target_pairs={{8,64},{9,65},{10,66},{11,67},{12,68},{13,69},{14,70},{15,71},{72,... | collective-permute-start | bytes 1572872 | tf_op jit(solution)/shard_map/ppermute | solution.py:43
  46.4 1.3 %collective-permute-start.15 = (bf16[512,512]{1,0:T(8,128)(2,1)S(1)}, bf16[512,512]{1,0:T(8,128)(2,1)S(1)}, u32[]{:S(2)}, u32[]{:S(2)}) collective-permute-start(bf16[512,512]{1,0:T(8,128)(2,1)S(1)} %collective-permute-done.8), channel_id=1, source_target_pairs={{40,64},{41,65},{42,66},{43,67},{44,68},{45,69},{46,70},{47,71},{1... | collective-permute-start | bytes 1572872 | tf_op jit(solution)/shard_map/ppermute | solution.py:43
  47.7 11.5 %collective-permute-done.4.kvf = bf16[2,256,512]{2,1,0:T(8,128)(2,1)S(1)} collective-permute-done((bf16[2,256,512]{2,1,0:T(8,128)(2,1)S(1)}, bf16[2,256,512]{2,1,0:T(8,128)(2,1)S(1)}, u32[]{:S(2)}, u32[]{:S(2)}) %collective-permute-start.4) | collective-permute-done | bytes 524320 | tf_op jit(solution)/shard_map/ppermute | solution.py:43
  60.7 15.8 %collective-permute-done.9.cm1 = bf16[256,512]{1,0:T(8,128)(2,1)S(1)} collective-permute-done((bf16[256,512]{1,0:T(8,128)(2,1)S(1)}, bf16[256,512]{1,0:T(8,128)(2,1)S(1)}, u32[]{:S(2)}, u32[]{:S(2)}) %collective-permute-start.9) | collective-permute-done | bytes 262176 | tf_op jit(solution)/shard_map/ppermute | solution.py:43
  76.5 1.3 %shard_map.92 = (bf16[2,2,256,512]{3,2,1,0:T(8,128)(2,1)S(1)}, bf16[2,256,512]{2,1,0:T(8,128)(2,1)S(1)}, bf16[2,256,512]{2,1,0:T(8,128)(2,1)S(1)}) custom-call(bf16[256,512]{1,0:T(8,128)(2,1)S(1)} %shard_map.89.cm0, bf16[256,512]{1,0:T(8,128)(2,1)S(1)} %collective-permute-done.9.cm1, bf16[512,2048]{1,0:T(8,128)(2,1)S(1)} %copy-done.5), custom_call_target="tpu_custom_call" | custom-call | flops 8192 | bytes 1024 | tf_op jit(solution)/shard_map/pallas_call | solution.py:247
  77.8 5.2 %collective-permute-start.10 = (bf16[2,2,256,512]{3,2,1,0:T(8,128)(2,1)S(1)}, bf16[2,2,256,512]{3,2,1,0:T(8,128)(2,1)S(1)}, u32[]{:S(2)}, u32[]{:S(2)}) collective-permute-start(bf16[2,2,256,512]{3,2,1,0:T(8,128)(2,1)S(1)} %get-tuple-element.31), channel_id=1, source_target_pairs={{0,1},{1,0},{2,3},{3,2},{4,5},{5,4},{6,7},{7,6},{8,9},{9,8},{10,11... | collective-permute-start | bytes 3145736 | tf_op jit(solution)/shard_map/ppermute | solution.py:43
  83.1 1.4 %shard_map.94 = (bf16[2,256,512]{2,1,0:T(8,128)(2,1)S(1)}, bf16[256,512]{1,0:T(8,128)(2,1)S(1)}, bf16[256,512]{1,0:T(8,128)(2,1)S(1)}, bf16[1536,512]{1,0:T(8,128)(2,1)S(1)}) custom-call(bf16[512,512]{1,0:T(8,128)(2,1)S(1)} %collective-permute-done.12.a, bf16[1024,512]{1,0:T(8,128)(2,1)S(1)} %collective-permute-done.13.near, ...), custom_call_target="tpu_custom_call" | custom-call | flops 40000008192 | bytes 1024 | tf_op jit(solution)/shard_map/pallas_call | solution.py:247
  84.5 17.2 %collective-permute-start.16 = (bf16[2,256,512]{2,1,0:T(8,128)(2,1)S(1)}, bf16[2,256,512]{2,1,0:T(8,128)(2,1)S(1)}, u32[]{:S(2)}, u32[]{:S(2)}) collective-permute-start(bf16[2,256,512]{2,1,0:T(8,128)(2,1)S(1)} %get-tuple-element.36), channel_id=1, source_target_pairs={{0,1},{1,0},{2,3},{3,2},{4,5},{5,4},{6,7},{7,6},{8,9},{9,8},{10,11... | collective-permute-start | bytes 1572872 | tf_op jit(solution)/shard_map/ppermute | solution.py:43
  101.9 1.3 %collective-permute-done.16.got = bf16[2,256,512]{2,1,0:T(8,128)(2,1)S(1)} collective-permute-done((bf16[2,256,512]{2,1,0:T(8,128)(2,1)S(1)}, bf16[2,256,512]{2,1,0:T(8,128)(2,1)S(1)}, u32[]{:S(2)}, u32[]{:S(2)}) %collective-permute-start.16) | collective-permute-done | bytes 524320 | tf_op jit(solution)/shard_map/ppermute | solution.py:43
  103.5 3.4 %shard_map.96 = f32[1,1,3,512,512]{4,3,2,1,0:T(8,128)} custom-call(bf16[1536,512]{1,0:T(8,128)(2,1)S(1)} %get-tuple-element.39.m, bf16[4,256,512]{2,1,0:T(8,128)(2,1)S(1)} %copy-done.1, bf16[4,256,512]{2,1,0:T(8,128)(2,1)S(1)} %copy-done.3, f32[3,1,256]{2,1,0:T(1,128)S(1)} %bitcast.14), custom_call_target="tpu_custom_call" | custom-call | flops 6144 | bytes 1024 | tf_op jit(solution)/shard_map/pallas_call | solution.py:247
  106.9 8.5 %collective-permute-done.11.other = bf16[2,256,512]{2,1,0:T(8,128)(2,1)S(1)} collective-permute-done((bf16[2,256,512]{2,1,0:T(8,128)(2,1)S(1)}, bf16[2,256,512]{2,1,0:T(8,128)(2,1)S(1)}, u32[]{:S(2)}, u32[]{:S(2)}) %collective-permute-start.11) | collective-permute-done | bytes 524320 | tf_op jit(solution)/shard_map/ppermute | solution.py:43
  115.5 1.1 shard_map.93._
  116.5 4.5 %collective-permute-done.17.other = bf16[256,512]{1,0:T(8,128)(2,1)S(1)} collective-permute-done((bf16[256,512]{1,0:T(8,128)(2,1)S(1)}, bf16[256,512]{1,0:T(8,128)(2,1)S(1)}, u32[]{:S(2)}, u32[]{:S(2)}) %collective-permute-start.17) | collective-permute-done | bytes 262176 | tf_op jit(solution)/shard_map/ppermute | solution.py:43
  (43 shorter events, 6.5 us)
Async XLA Ops:
  3.1 7.1 %copy-start.6 = (f32[3,256,1]{1,2,0:T(1,128)S(1)}, f32[3,256,1]{1,2,0:T(1,128)}, u32[]{:S(2)}) copy-start(f32[3,256,1]{1,2,0:T(1,128)} %param.10) | copy-start | bytes 9220
  3.1 15.5 %copy-start.7 = (f32[1,1,3,512,512]{4,3,2,1,0:T(8,128)S(1)}, f32[1,1,3,512,512]{4,3,2,1,0:T(8,128)}, u32[]{:S(2)}) copy-start(f32[1,1,3,512,512]{4,3,2,1,0:T(8,128)} %u) | copy-start | bytes 9437188
  3.1 15.5 %copy-start.8 = (f32[512]{0:T(512)S(1)}, f32[512]{0:T(512)}, u32[]{:S(2)}) copy-start(f32[512]{0:T(512)} %param.11) | copy-start | bytes 6148
  4.3 13.6 %collective-permute-start.2 = (bf16[256,512]{1,0:T(8,128)(2,1)S(1)}, bf16[256,512]{1,0:T(8,128)(2,1)S(1)}, u32[]{:S(2)}, u32[]{:S(2)}) collective-permute-start(bf16[256,512]{1,0:T(8,128)(2,1)S(1)} %get-tuple-element.22), channel_id=1, source_target_pairs={{0,60},{1,61},{2,62},{3,63},{4,0},{5,1},{6,2},{7,3},{8,4},{9,5},{1... | collective-permute-start | bytes 786440 | tf_op jit(solution)/shard_map/ppermute | solution.py:43
  10.1 7.8 %collective-permute-start.1 = (f32[3,1,256]{2,1,0:T(1,128)S(1)}, f32[3,1,256]{2,1,0:T(1,128)S(1)}, u32[]{:S(2)}, u32[]{:S(2)}) collective-permute-start(f32[3,1,256]{2,1,0:T(1,128)S(1)} %bitcast.12), channel_id=1, source_target_pairs={{0,252},{1,253},{2,254},{3,255},{4,0},{5,1},{6,2},{7,3},{8,4},{9,5... | collective-permute-start | bytes 9224 | tf_op jit(solution)/shard_map/ppermute | solution.py:43
  16.4 19.2 %collective-permute-start.5 = (bf16[2,256,512]{2,1,0:T(8,128)(2,1)S(1)}, bf16[2,256,512]{2,1,0:T(8,128)(2,1)S(1)}, u32[]{:S(2)}, u32[]{:S(2)}) collective-permute-start(bf16[2,256,512]{2,1,0:T(8,128)(2,1)S(1)} %shard_map.86._), channel_id=1, source_target_pairs={{0,252},{1,253},{2,254},{3,255},{4,0},{5,1},{6,2},{7,3},{8,4},{9,5... | collective-permute-start | bytes 1572872 | tf_op jit(solution)/shard_map/ppermute | solution.py:43
  16.7 26.3 %collective-permute-start.3 = (bf16[2,256,512]{2,1,0:T(8,128)(2,1)S(1)}, bf16[2,256,512]{2,1,0:T(8,128)(2,1)S(1)}, u32[]{:S(2)}, u32[]{:S(2)}) collective-permute-start(bf16[2,256,512]{2,1,0:T(8,128)(2,1)S(1)} %shard_map.86._), channel_id=1, source_target_pairs={{0,4},{1,5},{2,6},{3,7},{4,8},{5,9},{6,10},{7,11},{8,12},{9,13},{1... | collective-permute-start | bytes 1572872 | tf_op jit(solution)/shard_map/ppermute | solution.py:43
  17.9 27.0 %collective-permute-start = (bf16[2,256,512]{2,1,0:T(8,128)(2,1)S(1)}, bf16[2,256,512]{2,1,0:T(8,128)(2,1)S(1)}, u32[]{:S(2)}, u32[]{:S(2)}) collective-permute-start(bf16[2,256,512]{2,1,0:T(8,128)(2,1)S(1)} %get-tuple-element.21), channel_id=1, source_target_pairs={{0,4},{1,5},{2,6},{3,7},{4,8},{5,9},{6,10},{7,11},{8,12},{9,13},{1... | collective-permute-start | bytes 1572872 | tf_op jit(solution)/shard_map/ppermute | solution.py:43
  17.9 17.7 %collective-permute-start.6 = (bf16[256,512]{1,0:T(8,128)(2,1)S(1)}, bf16[256,512]{1,0:T(8,128)(2,1)S(1)}, u32[]{:S(2)}, u32[]{:S(2)}) collective-permute-start(bf16[256,512]{1,0:T(8,128)(2,1)S(1)} %collective-permute-done.2.qn), channel_id=1, source_target_pairs={{60,252},{61,253},{62,254},{63,255},{124,60},{125,61},{126,62},{12... | collective-permute-start | bytes 786440 | tf_op jit(solution)/shard_map/ppermute | solution.py:43
  38.7 6.4 %collective-permute-start.7 = (bf16[512,512]{1,0:T(8,128)(2,1)S(1)}, bf16[512,512]{1,0:T(8,128)(2,1)S(1)}, u32[]{:S(2)}, u32[]{:S(2)}) collective-permute-start(bf16[512,512]{1,0:T(8,128)(2,1)S(1)} %get-tuple-element.28), channel_id=1, source_target_pairs={{56,8},{57,9},{58,10},{59,11},{60,12},{61,13},{62,14},{63,15},{120... | collective-permute-start | bytes 1572872 | tf_op jit(solution)/shard_map/ppermute | solution.py:43
  39.4 7.0 %collective-permute-start.8 = (bf16[512,512]{1,0:T(8,128)(2,1)S(1)}, bf16[512,512]{1,0:T(8,128)(2,1)S(1)}, u32[]{:S(2)}, u32[]{:S(2)}) collective-permute-start(bf16[512,512]{1,0:T(8,128)(2,1)S(1)} %get-tuple-element.29), channel_id=1, source_target_pairs={{56,40},{57,41},{58,42},{59,43},{60,44},{61,45},{62,46},{63,47},{1... | collective-permute-start | bytes 1572872 | tf_op jit(solution)/shard_map/ppermute | solution.py:43
  40.1 43.0 %collective-permute-start.13 = (bf16[1024,512]{1,0:T(8,128)(2,1)S(1)}, bf16[1024,512]{1,0:T(8,128)(2,1)S(1)}, u32[]{:S(2)}, u32[]{:S(2)}) collective-permute-start(bf16[1024,512]{1,0:T(8,128)(2,1)S(1)} %get-tuple-element.35), channel_id=1, source_target_pairs={{0,8},{1,9},{2,10},{3,11},{4,12},{5,13},{6,14},{7,15},{8,16},{9,17... | collective-permute-start | bytes 3145736 | tf_op jit(solution)/shard_map/ppermute | solution.py:43
  43.0 16.2 %collective-permute-start.4 = (bf16[2,256,512]{2,1,0:T(8,128)(2,1)S(1)}, bf16[2,256,512]{2,1,0:T(8,128)(2,1)S(1)}, u32[]{:S(2)}, u32[]{:S(2)}) collective-permute-start(bf16[2,256,512]{2,1,0:T(8,128)(2,1)S(1)} %collective-permute-done.3.kvn), channel_id=1, source_target_pairs={{0,64},{1,65},{2,66},{3,67},{64,128},{65,129},{66,130},{67,131},{1... | collective-permute-start | bytes 1572872 | tf_op jit(solution)/shard_map/ppermute | solution.py:43
  45.0 38.1 %collective-permute-start.12 = (bf16[512,512]{1,0:T(8,128)(2,1)S(1)}, bf16[512,512]{1,0:T(8,128)(2,1)S(1)}, u32[]{:S(2)}, u32[]{:S(2)}) collective-permute-start(bf16[512,512]{1,0:T(8,128)(2,1)S(1)} %get-tuple-element.34), channel_id=1, source_target_pairs={{0,8},{1,9},{2,10},{3,11},{4,12},{5,13},{6,14},{7,15},{8,16},{9,17... | collective-permute-start | bytes 1572872 | tf_op jit(solution)/shard_map/ppermute | solution.py:43
  45.1 38.0 %collective-permute-start.14 = (bf16[512,512]{1,0:T(8,128)(2,1)S(1)}, bf16[512,512]{1,0:T(8,128)(2,1)S(1)}, u32[]{:S(2)}, u32[]{:S(2)}) collective-permute-start(bf16[512,512]{1,0:T(8,128)(2,1)S(1)} %collective-permute-done.7), channel_id=1, source_target_pairs={{8,64},{9,65},{10,66},{11,67},{12,68},{13,69},{14,70},{15,71},{72,... | collective-permute-start | bytes 1572872 | tf_op jit(solution)/shard_map/ppermute | solution.py:43
  46.4 36.7 %collective-permute-start.15 = (bf16[512,512]{1,0:T(8,128)(2,1)S(1)}, bf16[512,512]{1,0:T(8,128)(2,1)S(1)}, u32[]{:S(2)}, u32[]{:S(2)}) collective-permute-start(bf16[512,512]{1,0:T(8,128)(2,1)S(1)} %collective-permute-done.8), channel_id=1, source_target_pairs={{40,64},{41,65},{42,66},{43,67},{44,68},{45,69},{46,70},{47,71},{1... | collective-permute-start | bytes 1572872 | tf_op jit(solution)/shard_map/ppermute | solution.py:43
  59.2 17.3 %collective-permute-start.9 = (bf16[256,512]{1,0:T(8,128)(2,1)S(1)}, bf16[256,512]{1,0:T(8,128)(2,1)S(1)}, u32[]{:S(2)}, u32[]{:S(2)}) collective-permute-start(bf16[256,512]{1,0:T(8,128)(2,1)S(1)} %get-tuple-element.30), channel_id=1, source_target_pairs={{0,4},{1,5},{2,6},{3,7},{4,8},{5,9},{6,10},{7,11},{8,12},{9,13},{1... | collective-permute-start | bytes 786440 | tf_op jit(solution)/shard_map/ppermute | solution.py:43
  59.9 16.6 %copy-start.5 = (bf16[512,2048]{1,0:T(8,128)(2,1)S(1)}, bf16[512,2048]{1,0:T(8,128)(2,1)}, u32[]{:S(2)}) copy-start(bf16[512,2048]{1,0:T(8,128)(2,1)} %weight.3) | copy-start | bytes 6291460
  77.8 25.7 %copy-start.1 = (bf16[4,256,512]{2,1,0:T(8,128)(2,1)S(1)}, bf16[4,256,512]{2,1,0:T(8,128)(2,1)}, u32[]{:S(2)}) copy-start(bf16[4,256,512]{2,1,0:T(8,128)(2,1)} %k.7) | copy-start | bytes 3145732
  77.8 25.7 %copy-start.3 = (bf16[4,256,512]{2,1,0:T(8,128)(2,1)S(1)}, bf16[4,256,512]{2,1,0:T(8,128)(2,1)}, u32[]{:S(2)}) copy-start(bf16[4,256,512]{2,1,0:T(8,128)(2,1)} %v.7) | copy-start | bytes 3145732
  77.8 23.9 %collective-permute-start.10 = (bf16[2,2,256,512]{3,2,1,0:T(8,128)(2,1)S(1)}, bf16[2,2,256,512]{3,2,1,0:T(8,128)(2,1)S(1)}, u32[]{:S(2)}, u32[]{:S(2)}) collective-permute-start(bf16[2,2,256,512]{3,2,1,0:T(8,128)(2,1)S(1)} %get-tuple-element.31), channel_id=1, source_target_pairs={{0,1},{1,0},{2,3},{3,2},{4,5},{5,4},{6,7},{7,6},{8,9},{9,8},{10,11... | collective-permute-start | bytes 3145736 | tf_op jit(solution)/shard_map/ppermute | solution.py:43
  84.5 18.7 %collective-permute-start.16 = (bf16[2,256,512]{2,1,0:T(8,128)(2,1)S(1)}, bf16[2,256,512]{2,1,0:T(8,128)(2,1)S(1)}, u32[]{:S(2)}, u32[]{:S(2)}) collective-permute-start(bf16[2,256,512]{2,1,0:T(8,128)(2,1)S(1)} %get-tuple-element.36), channel_id=1, source_target_pairs={{0,1},{1,0},{2,3},{3,2},{4,5},{5,4},{6,7},{7,6},{8,9},{9,8},{10,11... | collective-permute-start | bytes 1572872 | tf_op jit(solution)/shard_map/ppermute | solution.py:43
  101.8 13.6 %collective-permute-start.11 = (bf16[2,256,512]{2,1,0:T(8,128)(2,1)S(1)}, bf16[2,256,512]{2,1,0:T(8,128)(2,1)S(1)}, u32[]{:S(2)}, u32[]{:S(2)}) collective-permute-start(bf16[2,256,512]{2,1,0:T(8,128)(2,1)S(1)} %fusion), channel_id=1, source_target_pairs={{0,2},{1,3},{2,0},{3,1},{4,6},{5,7},{6,4},{7,5},{8,10},{9,11},{10,... | collective-permute-start | bytes 1572872 | tf_op jit(solution)/shard_map/ppermute | solution.py:43
  103.3 17.8 %collective-permute-start.17 = (bf16[256,512]{1,0:T(8,128)(2,1)S(1)}, bf16[256,512]{1,0:T(8,128)(2,1)S(1)}, u32[]{:S(2)}, u32[]{:S(2)}) collective-permute-start(bf16[256,512]{1,0:T(8,128)(2,1)S(1)} %fusion.1), channel_id=1, source_target_pairs={{0,2},{1,3},{2,0},{3,1},{4,6},{5,7},{6,4},{7,5},{8,10},{9,11},{10,... | collective-permute-start | bytes 786440 | tf_op jit(solution)/shard_map/ppermute | solution.py:43
  (3 other events, 3.6 us)

commit v5 on v4

--- a/solution.py
+++ b/solution.py
@@ -329,10 +329,10 @@
         11,
         lead=LEAD,
     )
-    c1 = send_first(c, 2, 0, -1)
+    c1 = send_first(c, 2, -1, -2)
     b1 = send_first(b, 2, 0, 1)
     a2, near = send_direct(a, 2), send_near(bc, 2)
-    bf, cf = send_far(b1, 2, 0, 1), send_far(c1, 2, 0, -1)
+    bf, cf = send_far(b1, 2, 0, 1), send_far(c1, 2, -1, -2)
     (cm0,) = call(
         first_mix,
         [FLAT],

time: 122 us -> 114 us (0.934); the launches traced: 122 us -> 112 us
  starting transfers between devices: 44.4 us -> 37 us
  waiting for transfers between devices: 57.8 us -> 55.5 us
    ppermute x18, starting transfers between devices: 44.4 us -> 37 us  [permute(): return lax.ppermute(x, AXES, [(flat(a), flat(b)) for a, b in pairs])]
    ppermute x18, waiting for transfers between devices: 57.8 us -> 55.5 us  [permute(): return lax.ppermute(x, AXES, [(flat(a), flat(b)) for a, b in pairs])]
  transfers between devices with their start and end apart: 18 -> 18, of which waited for: 7 -> 6; matrix products, arithmetic and copies ran while one was open for 0% -> 0% of each run, Pallas kernels for 12% -> 13%
where the time goes in v5:
time: 114 us; the launch traced here: 112 us
  waiting for transfers between devices  55.5 us (49%)
  starting transfers between devices  37 us (32%)
  Pallas kernels  15.1 us (13%)
  local copies, waits for them, and re-layouts  3.53 us (3%)
    ppermute x18, waiting for transfers between devices, permute(): return lax.ppermute(x, AXES, [(flat(a), flat(b)) for a, b in pairs])  55.5 us
    ppermute x18, starting transfers between devices, permute(): return lax.ppermute(x, AXES, [(flat(a), flat(b)) for a, b in pairs])  37 us
    pallas_call x11, Pallas kernels, call(): pl.pallas_call(body, out_shape=[jax.ShapeDtypeStruct(s, d) for s, d, _ in...  15.1 us
    unnamed x18, local copies, waits for them, and re-layouts  3.53 us
  transfers between devices with their start and end apart: 18, of which 6 were waited for; matrix products, arithmetic and copies ran while one was open for 0% of the time, Pallas kernels for 13%

profile of v5, /device:TPU:1, one launch (start us, length us, event | category | flops | bytes accessed | tf_op | source)
XLA Modules:
  0.0 112.2 jit_solution(4962460517867265706)
XLA Ops:
  0.6 1.2 %copy-done = bf16[4,256,512]{2,1,0:T(8,128)(2,1)S(1)} copy-done((bf16[4,256,512]{2,1,0:T(8,128)(2,1)S(1)}, bf16[4,256,512]{2,1,0:T(8,128)(2,1)}, u32[]{:S(2)}) %copy-start) | copy-done | bytes 1048600
  1.9 1.2 %copy-done.2 = bf16[4,256,512]{2,1,0:T(8,128)(2,1)S(1)} copy-done((bf16[4,256,512]{2,1,0:T(8,128)(2,1)S(1)}, bf16[4,256,512]{2,1,0:T(8,128)(2,1)}, u32[]{:S(2)}) %copy-start.2) | copy-done | bytes 1048600
  4.3 5.8 %collective-permute-start.2 = (bf16[256,512]{1,0:T(8,128)(2,1)S(1)}, bf16[256,512]{1,0:T(8,128)(2,1)S(1)}, u32[]{:S(2)}, u32[]{:S(2)}) collective-permute-start(bf16[256,512]{1,0:T(8,128)(2,1)S(1)} %get-tuple-element.22), channel_id=1, source_target_pairs={{0,60},{1,61},{2,62},{3,63},{4,0},{5,1},{6,2},{7,3},{8,4},{9,5},{1... | collective-permute-start | bytes 786440 | tf_op jit(solution)/shard_map/ppermute | solution.py:43
  10.1 6.3 %collective-permute-start.1 = (f32[3,1,256]{2,1,0:T(1,128)S(1)}, f32[3,1,256]{2,1,0:T(1,128)S(1)}, u32[]{:S(2)}, u32[]{:S(2)}) collective-permute-start(f32[3,1,256]{2,1,0:T(1,128)S(1)} %bitcast.12), channel_id=1, source_target_pairs={{0,252},{1,253},{2,254},{3,255},{4,0},{5,1},{6,2},{7,3},{8,4},{9,5... | collective-permute-start | bytes 9224 | tf_op jit(solution)/shard_map/ppermute | solution.py:43
  16.7 1.2 %collective-permute-start.3 = (bf16[2,256,512]{2,1,0:T(8,128)(2,1)S(1)}, bf16[2,256,512]{2,1,0:T(8,128)(2,1)S(1)}, u32[]{:S(2)}, u32[]{:S(2)}) collective-permute-start(bf16[2,256,512]{2,1,0:T(8,128)(2,1)S(1)} %shard_map.86._), channel_id=1, source_target_pairs={{0,4},{1,5},{2,6},{3,7},{4,8},{5,9},{6,10},{7,11},{8,12},{9,13},{1... | collective-permute-start | bytes 1572872 | tf_op jit(solution)/shard_map/ppermute | solution.py:43
  18.6 2.5 %shard_map.88 = (f32[3,512,512]{2,1,0:T(8,128)S(1)}, f32[256,512]{1,0:T(8,128)S(1)}) custom-call(f32[1,1,3,512,512]{4,3,2,1,0:T(8,128)S(1)} %copy-done.7, bf16[4,256,512]{2,1,0:T(8,128)(2,1)S(1)} %copy-done, bf16[4,256,512]{2,1,0:T(8,128)(2,1)S(1)} %copy-done.2, f32[3,1,256]{2,1,0:T(1,128)S(1)} %bitcast.13, bf16[3,256,512]{2,1,0:T(8,128)(2,1)S(1)} %copy-done.4, ...), custom_call_target="tpu_custom_call" | custom-call | flops 40000008192 | bytes 1024 | tf_op jit(solution)/shard_map/pallas_call | solution.py:247
  21.2 14.5 %collective-permute-done.5.kv = bf16[2,256,512]{2,1,0:T(8,128)(2,1)S(1)} collective-permute-done((bf16[2,256,512]{2,1,0:T(8,128)(2,1)S(1)}, bf16[2,256,512]{2,1,0:T(8,128)(2,1)S(1)}, u32[]{:S(2)}, u32[]{:S(2)}) %collective-permute-start.5) | collective-permute-done | bytes 524320 | tf_op jit(solution)/shard_map/ppermute | solution.py:43
  35.7 3.0 %shard_map.91 = (bf16[512,512]{1,0:T(8,128)(2,1)S(1)}, bf16[1024,512]{1,0:T(8,128)(2,1)S(1)}, bf16[512,512]{1,0:T(8,128)(2,1)S(1)}, bf16[512,512]{1,0:T(8,128)(2,1)S(1)}, bf16[256,512]{1,0:T(8,128)(2,1)S(1)}) custom-call(f32[3,512,512]{2,1,0:T(8,128)S(1)} %get-tuple-element.26.u, bf16[2,256,512]{2,1,0:T(8,128)(2,1)S(1)} %collective-permute-done.5.kv, ...), custom_call_target="tpu_custom_call" | custom-call | flops 40000012288 | bytes 1024 | tf_op jit(solution)/shard_map/pallas_call | solution.py:247
  40.1 1.4 %collective-permute-start.13 = (bf16[1024,512]{1,0:T(8,128)(2,1)S(1)}, bf16[1024,512]{1,0:T(8,128)(2,1)S(1)}, u32[]{:S(2)}, u32[]{:S(2)}) collective-permute-start(bf16[1024,512]{1,0:T(8,128)(2,1)S(1)} %get-tuple-element.35), channel_id=1, source_target_pairs={{0,8},{1,9},{2,10},{3,11},{4,12},{5,13},{6,14},{7,15},{8,16},{9,17... | collective-permute-start | bytes 3145736 | tf_op jit(solution)/shard_map/ppermute | solution.py:43
  41.5 1.6 %collective-permute-done.3.kvn = bf16[2,256,512]{2,1,0:T(8,128)(2,1)S(1)} collective-permute-done((bf16[2,256,512]{2,1,0:T(8,128)(2,1)S(1)}, bf16[2,256,512]{2,1,0:T(8,128)(2,1)S(1)}, u32[]{:S(2)}, u32[]{:S(2)}) %collective-permute-start.3) | collective-permute-done | bytes 524320 | tf_op jit(solution)/shard_map/ppermute | solution.py:43
  43.0 1.9 %collective-permute-start.4 = (bf16[2,256,512]{2,1,0:T(8,128)(2,1)S(1)}, bf16[2,256,512]{2,1,0:T(8,128)(2,1)S(1)}, u32[]{:S(2)}, u32[]{:S(2)}) collective-permute-start(bf16[2,256,512]{2,1,0:T(8,128)(2,1)S(1)} %collective-permute-done.3.kvn), channel_id=1, source_target_pairs={{0,64},{1,65},{2,66},{3,67},{64,128},{65,129},{66,130},{67,131},{1... | collective-permute-start | bytes 1572872 | tf_op jit(solution)/shard_map/ppermute | solution.py:43
  45.1 1.3 %collective-permute-start.14 = (bf16[512,512]{1,0:T(8,128)(2,1)S(1)}, bf16[512,512]{1,0:T(8,128)(2,1)S(1)}, u32[]{:S(2)}, u32[]{:S(2)}) collective-permute-start(bf16[512,512]{1,0:T(8,128)(2,1)S(1)} %collective-permute-done.7), channel_id=1, source_target_pairs={{8,64},{9,65},{10,66},{11,67},{12,68},{13,69},{14,70},{15,71},{72,... | collective-permute-start | bytes 1572872 | tf_op jit(solution)/shard_map/ppermute | solution.py:43
  46.4 1.3 %collective-permute-start.15 = (bf16[512,512]{1,0:T(8,128)(2,1)S(1)}, bf16[512,512]{1,0:T(8,128)(2,1)S(1)}, u32[]{:S(2)}, u32[]{:S(2)}) collective-permute-start(bf16[512,512]{1,0:T(8,128)(2,1)S(1)} %collective-permute-done.8), channel_id=1, source_target_pairs={{20,64},{21,65},{22,66},{23,67},{24,68},{25,69},{26,70},{27,71},{8... | collective-permute-start | bytes 1572872 | tf_op jit(solution)/shard_map/ppermute | solution.py:43
  47.7 11.5 %collective-permute-done.4.kvf = bf16[2,256,512]{2,1,0:T(8,128)(2,1)S(1)} collective-permute-done((bf16[2,256,512]{2,1,0:T(8,128)(2,1)S(1)}, bf16[2,256,512]{2,1,0:T(8,128)(2,1)S(1)}, u32[]{:S(2)}, u32[]{:S(2)}) %collective-permute-start.4) | collective-permute-done | bytes 524320 | tf_op jit(solution)/shard_map/ppermute | solution.py:43
  60.7 15.8 %collective-permute-done.9.cm1 = bf16[256,512]{1,0:T(8,128)(2,1)S(1)} collective-permute-done((bf16[256,512]{1,0:T(8,128)(2,1)S(1)}, bf16[256,512]{1,0:T(8,128)(2,1)S(1)}, u32[]{:S(2)}, u32[]{:S(2)}) %collective-permute-start.9) | collective-permute-done | bytes 262176 | tf_op jit(solution)/shard_map/ppermute | solution.py:43
  76.5 1.3 %shard_map.92 = (bf16[2,2,256,512]{3,2,1,0:T(8,128)(2,1)S(1)}, bf16[2,256,512]{2,1,0:T(8,128)(2,1)S(1)}, bf16[2,256,512]{2,1,0:T(8,128)(2,1)S(1)}) custom-call(bf16[256,512]{1,0:T(8,128)(2,1)S(1)} %shard_map.89.cm0, bf16[256,512]{1,0:T(8,128)(2,1)S(1)} %collective-permute-done.9.cm1, bf16[512,2048]{1,0:T(8,128)(2,1)S(1)} %copy-done.5), custom_call_target="tpu_custom_call" | custom-call | flops 8192 | bytes 1024 | tf_op jit(solution)/shard_map/pallas_call | solution.py:247
  77.8 5.2 %collective-permute-start.10 = (bf16[2,2,256,512]{3,2,1,0:T(8,128)(2,1)S(1)}, bf16[2,2,256,512]{3,2,1,0:T(8,128)(2,1)S(1)}, u32[]{:S(2)}, u32[]{:S(2)}) collective-permute-start(bf16[2,2,256,512]{3,2,1,0:T(8,128)(2,1)S(1)} %get-tuple-element.31), channel_id=1, source_target_pairs={{0,1},{1,0},{2,3},{3,2},{4,5},{5,4},{6,7},{7,6},{8,9},{9,8},{10,11... | collective-permute-start | bytes 3145736 | tf_op jit(solution)/shard_map/ppermute | solution.py:43
  83.1 1.4 %shard_map.94 = (bf16[2,256,512]{2,1,0:T(8,128)(2,1)S(1)}, bf16[256,512]{1,0:T(8,128)(2,1)S(1)}, bf16[256,512]{1,0:T(8,128)(2,1)S(1)}, bf16[1536,512]{1,0:T(8,128)(2,1)S(1)}) custom-call(bf16[512,512]{1,0:T(8,128)(2,1)S(1)} %collective-permute-done.12.a, bf16[1024,512]{1,0:T(8,128)(2,1)S(1)} %collective-permute-done.13.near, ...), custom_call_target="tpu_custom_call" | custom-call | flops 40000008192 | bytes 1024 | tf_op jit(solution)/shard_map/pallas_call | solution.py:247
  84.5 3.3 %collective-permute-start.16 = (bf16[2,256,512]{2,1,0:T(8,128)(2,1)S(1)}, bf16[2,256,512]{2,1,0:T(8,128)(2,1)S(1)}, u32[]{:S(2)}, u32[]{:S(2)}) collective-permute-start(bf16[2,256,512]{2,1,0:T(8,128)(2,1)S(1)} %get-tuple-element.36), channel_id=1, source_target_pairs={{0,1},{1,0},{2,3},{3,2},{4,5},{5,4},{6,7},{7,6},{8,9},{9,8},{10,11... | collective-permute-start | bytes 1572872 | tf_op jit(solution)/shard_map/ppermute | solution.py:43
  88.0 5.8 %collective-permute-start.11 = (bf16[2,256,512]{2,1,0:T(8,128)(2,1)S(1)}, bf16[2,256,512]{2,1,0:T(8,128)(2,1)S(1)}, u32[]{:S(2)}, u32[]{:S(2)}) collective-permute-start(bf16[2,256,512]{2,1,0:T(8,128)(2,1)S(1)} %fusion), channel_id=1, source_target_pairs={{0,2},{1,3},{2,0},{3,1},{4,6},{5,7},{6,4},{7,5},{8,10},{9,11},{10,... | collective-permute-start | bytes 1572872 | tf_op jit(solution)/shard_map/ppermute | solution.py:43
  94.9 3.4 %shard_map.96 = f32[1,1,3,512,512]{4,3,2,1,0:T(8,128)} custom-call(bf16[1536,512]{1,0:T(8,128)(2,1)S(1)} %get-tuple-element.39.m, bf16[4,256,512]{2,1,0:T(8,128)(2,1)S(1)} %copy-done.1, bf16[4,256,512]{2,1,0:T(8,128)(2,1)S(1)} %copy-done.3, f32[3,1,256]{2,1,0:T(1,128)S(1)} %bitcast.14), custom_call_target="tpu_custom_call" | custom-call | flops 6144 | bytes 1024 | tf_op jit(solution)/shard_map/pallas_call | solution.py:247
  98.2 7.5 %collective-permute-done.11.other = bf16[2,256,512]{2,1,0:T(8,128)(2,1)S(1)} collective-permute-done((bf16[2,256,512]{2,1,0:T(8,128)(2,1)S(1)}, bf16[2,256,512]{2,1,0:T(8,128)(2,1)S(1)}, u32[]{:S(2)}, u32[]{:S(2)}) %collective-permute-start.11) | collective-permute-done | bytes 524320 | tf_op jit(solution)/shard_map/ppermute | solution.py:43
  105.8 1.1 shard_map.93._
  106.8 4.5 %collective-permute-done.17.other = bf16[256,512]{1,0:T(8,128)(2,1)S(1)} collective-permute-done((bf16[256,512]{1,0:T(8,128)(2,1)S(1)}, bf16[256,512]{1,0:T(8,128)(2,1)S(1)}, u32[]{:S(2)}, u32[]{:S(2)}) %collective-permute-start.17) | collective-permute-done | bytes 262176 | tf_op jit(solution)/shard_map/ppermute | solution.py:43
  (43 shorter events, 7.2 us)
Async XLA Ops:
  3.1 7.1 %copy-start.6 = (f32[3,256,1]{1,2,0:T(1,128)S(1)}, f32[3,256,1]{1,2,0:T(1,128)}, u32[]{:S(2)}) copy-start(f32[3,256,1]{1,2,0:T(1,128)} %param.10) | copy-start | bytes 9220
  3.1 15.5 %copy-start.7 = (f32[1,1,3,512,512]{4,3,2,1,0:T(8,128)S(1)}, f32[1,1,3,512,512]{4,3,2,1,0:T(8,128)}, u32[]{:S(2)}) copy-start(f32[1,1,3,512,512]{4,3,2,1,0:T(8,128)} %u) | copy-start | bytes 9437188
  3.1 15.5 %copy-start.8 = (f32[512]{0:T(512)S(1)}, f32[512]{0:T(512)}, u32[]{:S(2)}) copy-start(f32[512]{0:T(512)} %param.11) | copy-start | bytes 6148
  4.3 13.6 %collective-permute-start.2 = (bf16[256,512]{1,0:T(8,128)(2,1)S(1)}, bf16[256,512]{1,0:T(8,128)(2,1)S(1)}, u32[]{:S(2)}, u32[]{:S(2)}) collective-permute-start(bf16[256,512]{1,0:T(8,128)(2,1)S(1)} %get-tuple-element.22), channel_id=1, source_target_pairs={{0,60},{1,61},{2,62},{3,63},{4,0},{5,1},{6,2},{7,3},{8,4},{9,5},{1... | collective-permute-start | bytes 786440 | tf_op jit(solution)/shard_map/ppermute | solution.py:43
  10.1 7.8 %collective-permute-start.1 = (f32[3,1,256]{2,1,0:T(1,128)S(1)}, f32[3,1,256]{2,1,0:T(1,128)S(1)}, u32[]{:S(2)}, u32[]{:S(2)}) collective-permute-start(f32[3,1,256]{2,1,0:T(1,128)S(1)} %bitcast.12), channel_id=1, source_target_pairs={{0,252},{1,253},{2,254},{3,255},{4,0},{5,1},{6,2},{7,3},{8,4},{9,5... | collective-permute-start | bytes 9224 | tf_op jit(solution)/shard_map/ppermute | solution.py:43
  16.4 19.2 %collective-permute-start.5 = (bf16[2,256,512]{2,1,0:T(8,128)(2,1)S(1)}, bf16[2,256,512]{2,1,0:T(8,128)(2,1)S(1)}, u32[]{:S(2)}, u32[]{:S(2)}) collective-permute-start(bf16[2,256,512]{2,1,0:T(8,128)(2,1)S(1)} %shard_map.86._), channel_id=1, source_target_pairs={{0,252},{1,253},{2,254},{3,255},{4,0},{5,1},{6,2},{7,3},{8,4},{9,5... | collective-permute-start | bytes 1572872 | tf_op jit(solution)/shard_map/ppermute | solution.py:43
  16.7 26.3 %collective-permute-start.3 = (bf16[2,256,512]{2,1,0:T(8,128)(2,1)S(1)}, bf16[2,256,512]{2,1,0:T(8,128)(2,1)S(1)}, u32[]{:S(2)}, u32[]{:S(2)}) collective-permute-start(bf16[2,256,512]{2,1,0:T(8,128)(2,1)S(1)} %shard_map.86._), channel_id=1, source_target_pairs={{0,4},{1,5},{2,6},{3,7},{4,8},{5,9},{6,10},{7,11},{8,12},{9,13},{1... | collective-permute-start | bytes 1572872 | tf_op jit(solution)/shard_map/ppermute | solution.py:43
  17.9 27.0 %collective-permute-start = (bf16[2,256,512]{2,1,0:T(8,128)(2,1)S(1)}, bf16[2,256,512]{2,1,0:T(8,128)(2,1)S(1)}, u32[]{:S(2)}, u32[]{:S(2)}) collective-permute-start(bf16[2,256,512]{2,1,0:T(8,128)(2,1)S(1)} %get-tuple-element.21), channel_id=1, source_target_pairs={{0,4},{1,5},{2,6},{3,7},{4,8},{5,9},{6,10},{7,11},{8,12},{9,13},{1... | collective-permute-start | bytes 1572872 | tf_op jit(solution)/shard_map/ppermute | solution.py:43
  17.9 17.7 %collective-permute-start.6 = (bf16[256,512]{1,0:T(8,128)(2,1)S(1)}, bf16[256,512]{1,0:T(8,128)(2,1)S(1)}, u32[]{:S(2)}, u32[]{:S(2)}) collective-permute-start(bf16[256,512]{1,0:T(8,128)(2,1)S(1)} %collective-permute-done.2.qn), channel_id=1, source_target_pairs={{60,252},{61,253},{62,254},{63,255},{124,60},{125,61},{126,62},{12... | collective-permute-start | bytes 786440 | tf_op jit(solution)/shard_map/ppermute | solution.py:43
  38.7 6.4 %collective-permute-start.7 = (bf16[512,512]{1,0:T(8,128)(2,1)S(1)}, bf16[512,512]{1,0:T(8,128)(2,1)S(1)}, u32[]{:S(2)}, u32[]{:S(2)}) collective-permute-start(bf16[512,512]{1,0:T(8,128)(2,1)S(1)} %get-tuple-element.28), channel_id=1, source_target_pairs={{56,8},{57,9},{58,10},{59,11},{60,12},{61,13},{62,14},{63,15},{120... | collective-permute-start | bytes 1572872 | tf_op jit(solution)/shard_map/ppermute | solution.py:43
  39.4 7.0 %collective-permute-start.8 = (bf16[512,512]{1,0:T(8,128)(2,1)S(1)}, bf16[512,512]{1,0:T(8,128)(2,1)S(1)}, u32[]{:S(2)}, u32[]{:S(2)}) collective-permute-start(bf16[512,512]{1,0:T(8,128)(2,1)S(1)} %get-tuple-element.29), channel_id=1, source_target_pairs={{56,20},{57,21},{58,22},{59,23},{60,24},{61,25},{62,26},{63,27},{1... | collective-permute-start | bytes 1572872 | tf_op jit(solution)/shard_map/ppermute | solution.py:43
  40.1 43.0 %collective-permute-start.13 = (bf16[1024,512]{1,0:T(8,128)(2,1)S(1)}, bf16[1024,512]{1,0:T(8,128)(2,1)S(1)}, u32[]{:S(2)}, u32[]{:S(2)}) collective-permute-start(bf16[1024,512]{1,0:T(8,128)(2,1)S(1)} %get-tuple-element.35), channel_id=1, source_target_pairs={{0,8},{1,9},{2,10},{3,11},{4,12},{5,13},{6,14},{7,15},{8,16},{9,17... | collective-permute-start | bytes 3145736 | tf_op jit(solution)/shard_map/ppermute | solution.py:43
  43.0 16.2 %collective-permute-start.4 = (bf16[2,256,512]{2,1,0:T(8,128)(2,1)S(1)}, bf16[2,256,512]{2,1,0:T(8,128)(2,1)S(1)}, u32[]{:S(2)}, u32[]{:S(2)}) collective-permute-start(bf16[2,256,512]{2,1,0:T(8,128)(2,1)S(1)} %collective-permute-done.3.kvn), channel_id=1, source_target_pairs={{0,64},{1,65},{2,66},{3,67},{64,128},{65,129},{66,130},{67,131},{1... | collective-permute-start | bytes 1572872 | tf_op jit(solution)/shard_map/ppermute | solution.py:43
  45.0 38.1 %collective-permute-start.12 = (bf16[512,512]{1,0:T(8,128)(2,1)S(1)}, bf16[512,512]{1,0:T(8,128)(2,1)S(1)}, u32[]{:S(2)}, u32[]{:S(2)}) collective-permute-start(bf16[512,512]{1,0:T(8,128)(2,1)S(1)} %get-tuple-element.34), channel_id=1, source_target_pairs={{0,8},{1,9},{2,10},{3,11},{4,12},{5,13},{6,14},{7,15},{8,16},{9,17... | collective-permute-start | bytes 1572872 | tf_op jit(solution)/shard_map/ppermute | solution.py:43
  45.1 38.0 %collective-permute-start.14 = (bf16[512,512]{1,0:T(8,128)(2,1)S(1)}, bf16[512,512]{1,0:T(8,128)(2,1)S(1)}, u32[]{:S(2)}, u32[]{:S(2)}) collective-permute-start(bf16[512,512]{1,0:T(8,128)(2,1)S(1)} %collective-permute-done.7), channel_id=1, source_target_pairs={{8,64},{9,65},{10,66},{11,67},{12,68},{13,69},{14,70},{15,71},{72,... | collective-permute-start | bytes 1572872 | tf_op jit(solution)/shard_map/ppermute | solution.py:43
  46.4 36.7 %collective-permute-start.15 = (bf16[512,512]{1,0:T(8,128)(2,1)S(1)}, bf16[512,512]{1,0:T(8,128)(2,1)S(1)}, u32[]{:S(2)}, u32[]{:S(2)}) collective-permute-start(bf16[512,512]{1,0:T(8,128)(2,1)S(1)} %collective-permute-done.8), channel_id=1, source_target_pairs={{20,64},{21,65},{22,66},{23,67},{24,68},{25,69},{26,70},{27,71},{8... | collective-permute-start | bytes 1572872 | tf_op jit(solution)/shard_map/ppermute | solution.py:43
  59.2 17.3 %collective-permute-start.9 = (bf16[256,512]{1,0:T(8,128)(2,1)S(1)}, bf16[256,512]{1,0:T(8,128)(2,1)S(1)}, u32[]{:S(2)}, u32[]{:S(2)}) collective-permute-start(bf16[256,512]{1,0:T(8,128)(2,1)S(1)} %get-tuple-element.30), channel_id=1, source_target_pairs={{0,4},{1,5},{2,6},{3,7},{4,8},{5,9},{6,10},{7,11},{8,12},{9,13},{1... | collective-permute-start | bytes 786440 | tf_op jit(solution)/shard_map/ppermute | solution.py:43
  59.9 16.6 %copy-start.5 = (bf16[512,2048]{1,0:T(8,128)(2,1)S(1)}, bf16[512,2048]{1,0:T(8,128)(2,1)}, u32[]{:S(2)}) copy-start(bf16[512,2048]{1,0:T(8,128)(2,1)} %weight.3) | copy-start | bytes 6291460
  77.8 17.1 %copy-start.1 = (bf16[4,256,512]{2,1,0:T(8,128)(2,1)S(1)}, bf16[4,256,512]{2,1,0:T(8,128)(2,1)}, u32[]{:S(2)}) copy-start(bf16[4,256,512]{2,1,0:T(8,128)(2,1)} %k.7) | copy-start | bytes 3145732
  77.8 17.0 %copy-start.3 = (bf16[4,256,512]{2,1,0:T(8,128)(2,1)S(1)}, bf16[4,256,512]{2,1,0:T(8,128)(2,1)}, u32[]{:S(2)}) copy-start(bf16[4,256,512]{2,1,0:T(8,128)(2,1)} %v.7) | copy-start | bytes 3145732
  77.8 10.0 %collective-permute-start.10 = (bf16[2,2,256,512]{3,2,1,0:T(8,128)(2,1)S(1)}, bf16[2,2,256,512]{3,2,1,0:T(8,128)(2,1)S(1)}, u32[]{:S(2)}, u32[]{:S(2)}) collective-permute-start(bf16[2,2,256,512]{3,2,1,0:T(8,128)(2,1)S(1)} %get-tuple-element.31), channel_id=1, source_target_pairs={{0,1},{1,0},{2,3},{3,2},{4,5},{5,4},{6,7},{7,6},{8,9},{9,8},{10,11... | collective-permute-start | bytes 3145736 | tf_op jit(solution)/shard_map/ppermute | solution.py:43
  84.5 9.2 %collective-permute-start.16 = (bf16[2,256,512]{2,1,0:T(8,128)(2,1)S(1)}, bf16[2,256,512]{2,1,0:T(8,128)(2,1)S(1)}, u32[]{:S(2)}, u32[]{:S(2)}) collective-permute-start(bf16[2,256,512]{2,1,0:T(8,128)(2,1)S(1)} %get-tuple-element.36), channel_id=1, source_target_pairs={{0,1},{1,0},{2,3},{3,2},{4,5},{5,4},{6,7},{7,6},{8,9},{9,8},{10,11... | collective-permute-start | bytes 1572872 | tf_op jit(solution)/shard_map/ppermute | solution.py:43
  88.0 17.8 %collective-permute-start.11 = (bf16[2,256,512]{2,1,0:T(8,128)(2,1)S(1)}, bf16[2,256,512]{2,1,0:T(8,128)(2,1)S(1)}, u32[]{:S(2)}, u32[]{:S(2)}) collective-permute-start(bf16[2,256,512]{2,1,0:T(8,128)(2,1)S(1)} %fusion), channel_id=1, source_target_pairs={{0,2},{1,3},{2,0},{3,1},{4,6},{5,7},{6,4},{7,5},{8,10},{9,11},{10,... | collective-permute-start | bytes 1572872 | tf_op jit(solution)/shard_map/ppermute | solution.py:43
  93.8 17.5 %collective-permute-start.17 = (bf16[256,512]{1,0:T(8,128)(2,1)S(1)}, bf16[256,512]{1,0:T(8,128)(2,1)S(1)}, u32[]{:S(2)}, u32[]{:S(2)}) collective-permute-start(bf16[256,512]{1,0:T(8,128)(2,1)S(1)} %fusion.1), channel_id=1, source_target_pairs={{0,2},{1,3},{2,0},{3,1},{4,6},{5,7},{6,4},{7,5},{8,10},{9,11},{10,... | collective-permute-start | bytes 786440 | tf_op jit(solution)/shard_map/ppermute | solution.py:43
  (3 other events, 3.6 us)
